TPU v7x, 32 devices: a whole 2x2x4 slice. The times are simulated.
32 devices in a mesh: dp: 2 (over x), seq: 16 (over z, y, core).
Axes of the slice: x: 2, y: 2, z: 4, core: 2. Of those that a mesh axis runs over, the one named last changes fastest.
Arguments:
- tokens: bfloat16 [4, 8192, 512], P('dp', 'seq'), may hold values from -6 to 6
- cotangent: bfloat16 [4, 8192, 512], P('dp', 'seq'), may hold values from -6 to 6
- gain_attn: float32 [512], replicated, may hold values from 0.5 to 1.5
- shift_attn: float32 [512], replicated, may hold values from -1 to 1
- w_qkv: bfloat16 [512, 1536], replicated, may hold values from -0.25 to 0.25
- b_qkv: float32 [1536], replicated, may hold values from -1 to 1
- w_out: bfloat16 [512, 512], replicated, may hold values from -2 to 2
- b_out: float32 [512], replicated, may hold values from -1 to 1
- gain_ffn: float32 [512], replicated, may hold values from 0.5 to 1.5
- shift_ffn: float32 [512], replicated, may hold values from -1 to 1
- w_up: bfloat16 [512, 2048], replicated, may hold values from -0.25 to 0.25
- b_up: float32 [2048], replicated, may hold values from -1 to 1
- w_down: bfloat16 [2048, 512], replicated, may hold values from -0.125 to 0.125
- b_down: float32 [512], replicated, may hold values from -1 to 1
- tables: bfloat16 [2, 256, 64], replicated, as said below
- pick: int32 [1], replicated, may hold values from 0 to 1023
Outputs:
- block_out: bfloat16 [4, 8192, 512], P('dp', 'seq')
- grad_tokens: bfloat16 [4, 8192, 512], P('dp', 'seq')
- grad_gain_attn: float32 [512], replicated
- grad_shift_attn: float32 [512], replicated
- grad_w_qkv: float32 [512, 1536], replicated
- grad_b_qkv: float32 [1536], replicated
- grad_w_out: float32 [512, 512], replicated
- grad_b_out: float32 [512], replicated
- grad_gain_ffn: float32 [512], replicated
- grad_shift_ffn: float32 [512], replicated
- grad_w_up: float32 [512, 2048], replicated
- grad_b_up: float32 [2048], replicated
- grad_w_down: float32 [2048, 512], replicated
- grad_b_down: float32 [512], replicated
Inputs may be any that keep to these rules, and one draw needn't show every extreme that they name: `tables`: each matrix consists of groups of 64 mutually orthogonal rows, each of length sqrt(64).
All inputs are finite; a program needn't handle non-finite values.
Results may differ from a plain program's by a relative error of at most 0.018.
Values sent between devices are 32-bit elements; how exact they have to be, the bound alone decides.
No kernel may reach another device: no remote copies, remote signals or barrier semaphores. Data moves between devices by JAX's collectives and lax.ppermute only.
A program may use at most 256 MiB of HBM per device.

v0:
```python
import jax
import jax.numpy as jnp
from jax import lax
from jax.sharding import PartitionSpec as P

HEADS = 8
HEAD_DIM = 64
FEATS = 256


highest_precision = lax.Precision.HIGHEST


def prefix(part, axis, combine, identity, reverse):
    count = lax.axis_size(axis)
    place = lax.axis_index(axis)
    ahead = count - 1 - place if reverse else place
    gathered = jax.tree.map(lambda a: lax.all_gather(a, axis), part)
    state = jax.tree.map(lambda a, e: jnp.zeros_like(a) + jnp.asarray(e, a.dtype), part, identity)

    def one(turn, state):
        source = count - 1 - turn if reverse else turn
        return combine(
            state, jax.tree.map(lambda a: lax.dynamic_index_in_dim(a, source, 0, False), gathered)
        )

    return lax.fori_loop(0, ahead, one, state)


def layer_norm(values, gain, shift):
    center = values - jnp.mean(values, axis=-1, keepdims=True)
    spread = jnp.mean(center * center, axis=-1, keepdims=True)
    return center * lax.rsqrt(spread + 1e-05) * gain + shift


def gelu_tanh(values):
    return jax.nn.gelu(values, approximate=True)


def feature_map(heads_in, table):
    head_width = heads_in.shape[-1]
    proj = jnp.einsum(
        "schd,md->schm", heads_in, table, preferred_element_type=jnp.float32
    ) * head_width ** (-0.25)
    widened = heads_in.astype(jnp.float32)
    square = jnp.sum(widened * widened, axis=-1, keepdims=True) * (0.5 * head_width ** (-0.5))
    return jnp.exp(proj - square) * table.shape[0] ** (-0.5)


def feature_back(grad_phi, expo, heads_in, table):
    head_width = heads_in.shape[-1]
    inner = grad_phi * expo
    rounded = inner.astype(jnp.bfloat16)
    back = jnp.einsum(
        "schm,md->schd", rounded, table, preferred_element_type=jnp.float32
    ) * head_width ** (-0.25)
    widened = heads_in.astype(jnp.float32)
    return back - jnp.sum(inner, axis=-1, keepdims=True) * widened * head_width ** (-0.5)


def add_up(earlier, later):
    return jax.tree.map(jnp.add, earlier, later)


def contract_rows(left, right):
    return lax.dot_general(
        left, right, (((0,), (0,)), ((), ())), preferred_element_type=jnp.float32
    )


def contract_cols(left, right):
    return lax.dot_general(
        left, right, (((1,), (1,)), ((), ())), preferred_element_type=jnp.float32
    )


def shards(
    tokens,
    cotangent,
    gain_attn,
    shift_attn,
    w_qkv,
    b_qkv,
    w_out,
    b_out,
    gain_ffn,
    shift_ffn,
    w_up,
    b_up,
    w_down,
    b_down,
    tables,
    pick,
):
    seqs, span, width = tokens.shape
    heads = HEADS
    head_width = HEAD_DIM
    feats = FEATS
    rows = seqs * span
    table = lax.dynamic_index_in_dim(tables, pick[0] % 2, 0, keepdims=False)
    resid_in = tokens.reshape(rows, width).astype(jnp.float32)
    normed_one, norm_one_pull = jax.vjp(layer_norm, resid_in, gain_attn, shift_attn)
    normed_low = normed_one.astype(jnp.bfloat16)
    projected = (jnp.dot(normed_low, w_qkv, preferred_element_type=jnp.float32) + b_qkv).astype(
        jnp.bfloat16
    )
    query = projected[:, :width].reshape(seqs, span, heads, head_width)
    key_in = projected[:, width : 2 * width].reshape(seqs, span, heads, head_width)
    value = projected[:, 2 * width :].reshape(seqs, span, heads, head_width)
    expo_q = feature_map(query, table)
    expo_k = feature_map(key_in, table)
    phi_q = expo_q.astype(jnp.bfloat16)
    phi_k = expo_k.astype(jnp.bfloat16)
    causal = (
        lax.broadcasted_iota(jnp.int32, (span, span), 0)
        >= lax.broadcasted_iota(jnp.int32, (span, span), 1)
    ).astype(jnp.float32)
    score_matrix = (
        jnp.einsum("sihm,sjhm->shij", phi_q, phi_k, preferred_element_type=jnp.float32) * causal
    )
    scores_low = score_matrix.astype(jnp.bfloat16)
    numer_local = jnp.einsum(
        "shij,sjhd->sihd", scores_low, value, preferred_element_type=jnp.float32
    )
    denom_local = jnp.swapaxes(jnp.sum(score_matrix, axis=-1), 1, 2)
    state_local = jnp.einsum(
        "sjhm,sjhd->smhd", phi_k, value, preferred_element_type=jnp.float32
    ).reshape(seqs, feats, heads * head_width)
    norm_local = jnp.sum(phi_k.astype(jnp.float32), axis=1)
    state_prev, norm_prev = prefix(
        (state_local, norm_local),
        "seq",
        add_up,
        (jnp.zeros_like(state_local), jnp.zeros_like(norm_local)),
        False,
    )
    state_low = state_prev.astype(jnp.bfloat16).reshape(seqs, feats, heads, head_width)
    norm_low = norm_prev.astype(jnp.bfloat16)
    numerator = numer_local + jnp.einsum(
        "sihm,smhd->sihd", phi_q, state_low, preferred_element_type=jnp.float32
    )
    denom = denom_local + jnp.einsum(
        "sihm,shm->sih", phi_q, norm_low, preferred_element_type=jnp.float32
    )
    attended = numerator / denom[..., None]
    mixed = attended.reshape(rows, width).astype(jnp.bfloat16)
    middle = resid_in + jnp.dot(mixed, w_out, preferred_element_type=jnp.float32) + b_out
    normed_two, norm_two_pull = jax.vjp(layer_norm, middle, gain_ffn, shift_ffn)
    normed_two_low = normed_two.astype(jnp.bfloat16)
    upper = jnp.dot(normed_two_low, w_up, preferred_element_type=jnp.float32) + b_up
    activated, gelu_pull = jax.vjp(gelu_tanh, upper)
    hidden = activated.astype(jnp.bfloat16)
    result = middle + jnp.dot(hidden, w_down, preferred_element_type=jnp.float32) + b_down
    grad_out = cotangent.reshape(rows, width)
    grad_wide = grad_out.astype(jnp.float32)
    grad_w_down = contract_rows(hidden, grad_out)
    grad_b_down = jnp.sum(grad_wide, axis=0)
    grad_hidden = contract_cols(grad_out, w_down)
    grad_upper = gelu_pull(grad_hidden)[0].astype(jnp.bfloat16)
    grad_w_up = contract_rows(normed_two_low, grad_upper)
    grad_b_up = jnp.sum(grad_upper.astype(jnp.float32), axis=0)
    grad_normed_two = contract_cols(grad_upper, w_up)
    middle_part, grad_gain_ffn, grad_shift_ffn = norm_two_pull(grad_normed_two)
    grad_middle = grad_wide + middle_part
    grad_middle_low = grad_middle.astype(jnp.bfloat16)
    grad_b_out = jnp.sum(grad_middle, axis=0)
    grad_w_out = contract_rows(mixed, grad_middle_low)
    grad_attended = contract_cols(grad_middle_low, w_out).reshape(seqs, span, heads, head_width)
    grad_numer = (grad_attended / denom[..., None]).astype(jnp.bfloat16)
    grad_denom = -jnp.sum(grad_attended * attended, axis=-1) / denom
    grad_phi_q = (
        jnp.einsum("sihd,smhd->sihm", grad_numer, state_low, preferred_element_type=jnp.float32)
        + grad_denom[..., None] * norm_low.astype(jnp.float32)[:, None]
    )
    grad_state = jnp.einsum(
        "sihm,sihd->smhd", phi_q, grad_numer, preferred_element_type=jnp.float32
    ).reshape(seqs, feats, heads * head_width)
    grad_norm = jnp.einsum(
        "sih,sihm->shm", grad_denom, phi_q.astype(jnp.float32), precision=highest_precision
    )
    score_part = jnp.einsum(
        "sihd,sjhd->shij", grad_numer, value, preferred_element_type=jnp.float32
    )
    grad_scores = ((score_part + jnp.swapaxes(grad_denom, 1, 2)[..., None]) * causal).astype(
        jnp.bfloat16
    )
    grad_value = jnp.einsum(
        "shij,sihd->sjhd", scores_low, grad_numer, preferred_element_type=jnp.float32
    )
    grad_phi_q = grad_phi_q + jnp.einsum(
        "shij,sjhm->sihm", grad_scores, phi_k, preferred_element_type=jnp.float32
    )
    grad_phi_k = jnp.einsum(
        "shij,sihm->sjhm", grad_scores, phi_q, preferred_element_type=jnp.float32
    )
    later_state, later_norm = prefix(
        (grad_state, grad_norm),
        "seq",
        add_up,
        (jnp.zeros_like(grad_state), jnp.zeros_like(grad_norm)),
        True,
    )
    later_low = later_state.astype(jnp.bfloat16).reshape(seqs, feats, heads, head_width)
    grad_phi_k = (
        grad_phi_k
        + jnp.einsum("sjhd,smhd->sjhm", value, later_low, preferred_element_type=jnp.float32)
        + later_norm[:, None]
    )
    grad_value = grad_value + jnp.einsum(
        "sjhm,smhd->sjhd", phi_k, later_low, preferred_element_type=jnp.float32
    )
    grad_query = feature_back(grad_phi_q, expo_q, query, table)
    grad_key = feature_back(grad_phi_k, expo_k, key_in, table)
    grad_projected = jnp.concatenate(
        [
            grad_query.reshape(rows, width),
            grad_key.reshape(rows, width),
            grad_value.reshape(rows, width),
        ],
        axis=1,
    ).astype(jnp.bfloat16)
    grad_w_qkv = contract_rows(normed_low, grad_projected)
    grad_b_qkv = jnp.sum(grad_projected.astype(jnp.float32), axis=0)
    grad_normed_one = contract_cols(grad_projected, w_qkv)
    input_part, grad_gain_attn, grad_shift_attn = norm_one_pull(grad_normed_one)
    grad_tokens = (grad_middle + input_part).astype(jnp.bfloat16).reshape(seqs, span, width)
    totals = lax.psum(
        (
            grad_gain_attn,
            grad_shift_attn,
            grad_w_qkv,
            grad_b_qkv,
            grad_w_out,
            grad_b_out,
            grad_gain_ffn,
            grad_shift_ffn,
            grad_w_up,
            grad_b_up,
            grad_w_down,
            grad_b_down,
        ),
        ("dp", "seq"),
    )
    block_out = result.astype(jnp.bfloat16).reshape(seqs, span, width)
    return (
        block_out,
        grad_tokens,
        totals[0],
        totals[1],
        totals[2],
        totals[3],
        totals[4],
        totals[5],
        totals[6],
        totals[7],
        totals[8],
        totals[9],
        totals[10],
        totals[11],
    )


def solution(mesh):
    placed = (
        P("dp", "seq", None),
        P("dp", "seq", None),
        P(),
        P(),
        P(),
        P(),
        P(),
        P(),
        P(),
        P(),
        P(),
        P(),
        P(),
        P(),
        P(),
        P(),
    )
    return jax.shard_map(
        shards,
        mesh=mesh,
        in_specs=placed,
        out_specs=(
            P("dp", "seq", None),
            P("dp", "seq", None),
            P(),
            P(),
            P(),
            P(),
            P(),
            P(),
            P(),
            P(),
            P(),
            P(),
            P(),
            P(),
        ),
        check_vma=False,
    )
```

profile of v0, /device:TPU:13, one launch (start us, length us, event | category | flops | bytes accessed | tf_op | source)
XLA Modules:
  0.0 677.5 jit_solution(6070363679770529416)
XLA Ops:
  24.2 3.9 reshape.202
  30.7 6.5 convert_reduce_fusion.1
  44.4 3.3 copy.96
  47.7 17.8 %all-gather = f32[32,8,256]{2,1,0:T(8,128)S(1)} all-gather(f32[2,8,256]{2,1,0:T(8,128)S(1)} %get-tuple-element.180), channel_id=2, replica_groups=mesh['dp'=2,'seq'=16] {'seq'}, dimensions={0}, use_global_device_ids=true | all-gather | bytes 278528 | tf_op jit(solution)/shard_map/all_gather | solution.py:18
  67.1 5.6 fusion.8
  72.8 11.3 %multiply_reduce_fusion = (f32[2,8,512]{2,1,0:T(8,128)S(1)}, f32[2,8,512,512]{2,3,1,0:T(8,128)}) fusion(f32[512,512]{0,1:T(8,128)S(1)} %fusion.41, bf16[2,512,8,256]{1,3,2,0:T(8,128)(2,1)S(1)} %get-tuple-element.191, bf16[2,512,8,256]{1,3,2,0:T(8,128)(2,1)} %copy-done.6), kind=kOutput, calls=%fused_computation.5 | convolution fusion | flops 2155864064 | bytes 26247168 | tf_op jit(solution)/shard_map/sihm,sjhm->shij/dot_general | solution.py:119
  84.0 9.3 %fusion.15 = f32[2,8,64,512]{3,2,1,0:T(8,128)} fusion(bf16[2,512,8,64]{1,3,2,0:T(8,128)(2,1)} %copy-done.16, f32[2,8,512,512]{2,3,1,0:T(8,128)} %get-tuple-element.195, f32[512,512]{0,1:T(8,128)S(1)} %fusion.41), kind=kOutput, calls=%fused_computation.36 | convolution fusion | flops 545259520 | bytes 20971520 | tf_op jit(solution)/shard_map/shij,sjhd->sihd/dot_general | solution.py:122
  93.4 75.6 %all-gather.5.cloned.1.call-done = f32[16,2,256,512]{3,2,1,0:T(8,128)} async-done(((f32[1,2,256,512]{3,2,1,0:T(8,128)}), f32[16,2,256,512]{3,2,1,0:T(8,128)}) %all-gather.5.cloned.1.call-update) | async-done | bytes 16777232 | tf_op jit(solution)/shard_map/all_gather | solution.py:18
  170.1 19.1 %while.26 = (s32[]{:T(128)}, f32[2,256,512]{2,1,0:T(8,128)}, f32[2,8,256]{2,1,0:T(8,128)S(1)}, s32[]{:T(128)}, f32[16,2,256,512]{3,2,1,0:T(8,128)}, /*index=5*/f...) while((s32[]{:T(128)}, f32[2,256,512]{2,1,0:T(8,128)}, f32[2,8,256]{2,1,0:T(8,128)S(1)}, ...), condition=%wide.region_6.7_spmd, body=%wide.region_5.6_spmd.sunk | while | flops 266245 | bytes 3195015 | solution.py:27
  194.8 3.9 fusion.75
  201.5 6.3 multiply_convert_fusion.2
  207.9 8.6 %convert_reduce_fusion = (f32[2048]{0:T(1024)}, bf16[1024,2048]{1,0:T(8,128)(2,1)S(1)}) fusion(f32[1024,2048]{1,0:T(8,128)S(1)} %get-tuple-element.201, f32[2048]{0:T(1024)S(1)} %copy-done.64, bf16[1024,512]{1,0:T(8,128)(2,1)S(1)} %bitcast.196, bf16[2048,512]{1,0:T(8,128)(2,1)S(1)} %copy-done.60), kind=kOutput, calls=%fused_computation.20 | convolution fusion | flops 2195716096 | bytes 15745024 | tf_op jit(solution)/shard_map/dot_general | solution.py:72
  216.4 3.4 multiply_reduce_fusion.1
  223.8 4.0 reshape.188
  236.5 5.6 fusion.52
  242.2 4.5 fusion.80
  246.7 5.6 multiply_convert_fusion
  252.3 10.4 %fusion.77 = (f32[2,512,8]{1,2,0:T(8,128)S(1)}, bf16[2,512,8,256]{1,3,2,0:T(8,128)(2,1)S(1)}) fusion(f32[2,512,8]{1,2,0:T(8,128)S(1)} %broadcast_multiply_fusion.1, f32[2,512,8,256]{1,3,2,0:T(8,128)} %get-tuple-element.192, bf16[2,512,8,256]{1,3,2,0:T(8,128)(2,1)S(1)} %copy-done.7, bf16[2,8,512,512]{2,3,1,0:T(8,128)(2,1)} %multiply_convert_fusion, ...), kind=kOutput, calls=%fused_computation.133 | convolution fusion | flops 2166349824 | bytes 33669120 | tf_op jit(solution)/shard_map/shij,sjhm->sihm/dot_general | solution.py:190
  265.0 38.7 %all-gather.1 = f32[32,8,256]{2,1,0:T(8,128)S(1)} all-gather(f32[2,8,256]{2,1,0:T(8,128)S(1)} %bitcast.208), channel_id=3, replica_groups=mesh['dp'=2,'seq'=16] {'seq'}, dimensions={0}, use_global_device_ids=true | all-gather | bytes 278528 | tf_op jit(solution)/shard_map/all_gather | solution.py:18
  307.0 4.4 fusion.84
  311.4 4.5 fusion.68
  315.9 10.1 %fusion.14 = f32[2,8,64,512]{3,2,1,0:T(8,128)} fusion(bf16[2,512,8,64]{1,3,2,0:T(8,128)(2,1)S(1)} %copy-done.20, f32[2,8,512,512]{2,3,1,0:T(8,128)} %get-tuple-element.195, f32[512,512]{0,1:T(8,128)S(1)} %fusion.41), kind=kOutput, calls=%fused_computation.35 | convolution fusion | flops 545259520 | bytes 20971520 | tf_op jit(solution)/shard_map/shij,sihd->sjhd/dot_general | solution.py:187
  326.0 9.0 %fusion.81 = f32[2,8,256,512]{3,2,1,0:T(8,128)} fusion(bf16[2,512,8,256]{1,3,2,0:T(8,128)(2,1)S(1)} %copy-done.5, bf16[2,8,512,512]{2,3,1,0:T(8,128)(2,1)} %multiply_convert_fusion), kind=kOutput, calls=%fused_computation.137 | convolution fusion | flops 2147483648 | bytes 20971520 | tf_op jit(solution)/shard_map/shij,sihm->sjhm/dot_general | solution.py:193
  335.0 49.4 %all-gather.7.cloned.1.call-done = f32[16,2,256,512]{3,2,1,0:T(8,128)} async-done(((f32[1,2,256,512]{3,2,1,0:T(8,128)}), f32[16,2,256,512]{3,2,1,0:T(8,128)}) %all-gather.7.cloned.1.call-update) | async-done | bytes 16777232 | tf_op jit(solution)/shard_map/all_gather | solution.py:18
  384.5 12.4 %while.27 = (s32[]{:T(128)}, f32[2,256,512]{2,1,0:T(8,128)S(1)}, f32[2,8,256]{2,1,0:T(8,128)S(1)}, s32[]{:T(128)}, f32[16,2,256,512]{3,2,1,0:T(8,128)}, /*index=...) while((s32[]{:T(128)}, f32[2,256,512]{2,1,0:T(8,128)S(1)}, ...), condition=%wide.region_15.16_spmd, body=%wide.region_14.15_spmd.sunk | while | flops 266246 | bytes 3195035 | solution.py:27
  397.2 3.8 fusion.40
  402.9 5.8 fusion.78
  413.3 3.5 fusion.83
  418.8 6.3 add_convert_fusion.3
  429.4 54.3 %all-reduce = (f32[512]{0:T(512)}, f32[512]{0:T(512)}, f32[1536]{0:T(1024)}, f32[512]{0:T(512)}, f32[512]{0:T(512)}, /*index=5*/f32[512]{0:T(512)}, f32[2048]{0:T(1024)}, f32[512]{0:T(512)}) all-reduce(f32[512]{0:T(512)S(1)} %get-tuple-element.135, f32[512]{0:T(512)S(1)} %get-tuple-element.138, ...), channel_id=1, replica_groups=mesh['dp'=2,'seq'=16] {'dp','seq'}, use_global_device_ids=true, to_apply=%region_20.21 | all-reduce | flops 6656 | bytes 53248 | tf_op jit(solution)/shard_map/psum | solution.py:227
  486.7 173.3 %all-reduce.4.cloned.1.call-done = (f32[512,1536]{1,0:T(8,128)}, f32[512,512]{1,0:T(8,128)}, f32[512,2048]{1,0:T(8,128)}, f32[2048,512]{1,0:T(8,128)}) async-done(((f32[512,1536]{1,0:T(8,128)}, f32[512,512]{1,0:T(8,128)}, f32[512,2048]{1,0:T(8,128)}, f32[2048,512]{1,0:T(8,128)}), (f32[512,1536]{1,0:T(8,128)}, f32[512,512]{1,0:T(8,128)}, f32[512,2048]{1,0:T(8,128)}, ...) | async-done | bytes 12582928 | tf_op jit(solution)/shard_map/psum | solution.py:227
  660.0 3.9 copy.200
  (241 shorter events, 108.6 us)
Async XLA Ops:
  7.2 194.3 %copy-start = (bf16[512,2048]{1,0:T(8,128)(2,1)S(1)}, bf16[512,2048]{1,0:T(8,128)(2,1)}, u32[]{:S(2)}) copy-start(bf16[512,2048]{1,0:T(8,128)(2,1)} %param.30) | copy-start | bytes 6291460
  7.2 8.1 %copy-start.63 = (f32[1536]{0:T(1024)S(1)}, f32[1536]{0:T(1024)}, u32[]{:S(2)}) copy-start(f32[1536]{0:T(1024)} %param.25) | copy-start | bytes 18436
  7.2 161.8 %all-gather.5.cloned.1.call-start = ((), (), s32[]{:S(2)}) async-start(), calls=%async_computation | async-start | bytes 17825792 | tf_op jit(solution)/shard_map/all_gather | solution.py:18
  8.1 7.2 %copy-start.61 = (bf16[512,1536]{1,0:T(8,128)(2,1)S(1)}, bf16[512,1536]{1,0:T(8,128)(2,1)}, u32[]{:S(2)}) copy-start(bf16[512,1536]{1,0:T(8,128)(2,1)} %param.24) | copy-start | bytes 4718596
  24.2 6.5 copy-start.44
  30.6 6.5 copy-start.16
  42.2 342.1 %all-gather.7.cloned.1.call-start = ((), (), s32[]{:S(2)}) async-start(), calls=%async_computation.1 | async-start | bytes 17825792 | tf_op jit(solution)/shard_map/all_gather | solution.py:18
  47.7 19.4 %copy-start.23 = (bf16[2,512,8,64]{1,3,2,0:T(8,128)(2,1)S(1)}, bf16[2,512,8,64]{1,3,2,0:T(8,128)(2,1)}, u32[]{:S(2)}) copy-start(bf16[2,512,8,64]{1,3,2,0:T(8,128)(2,1)} %copy.96) | copy-start | bytes 3145732
  72.8 11.3 %copy-start.2 = (bf16[2,512,8,256]{1,3,2,0:T(8,128)(2,1)}, bf16[2,512,8,256]{1,3,2,0:T(8,128)(2,1)S(1)}, u32[]{:S(2)}) copy-start(bf16[2,512,8,256]{1,3,2,0:T(8,128)(2,1)S(1)} %get-tuple-element.191) | copy-start | bytes 12582916
  201.0 18.8 %copy-start.11 = (f32[1024,512]{1,0:T(8,128)}, f32[1024,512]{1,0:T(8,128)S(1)}, u32[]{:S(2)}) copy-start(f32[1024,512]{1,0:T(8,128)S(1)} %get-tuple-element.199) | copy-start | bytes 6291460
  201.5 6.4 copy-start.34
  201.5 6.3 copy-start.60
  221.7 83.0 %copy-start.9 = (f32[1024,512]{1,0:T(8,128)}, f32[1024,512]{1,0:T(8,128)S(1)}, u32[]{:S(2)}) copy-start(f32[1024,512]{1,0:T(8,128)S(1)} %get-tuple-element.177) | copy-start | bytes 6291460
  236.2 423.8 %all-reduce.4.cloned.1.call-start = ((), (), s32[]{:S(2)}) async-start(), calls=%async_computation.2 | async-start | bytes 25165824 | tf_op jit(solution)/shard_map/psum | solution.py:227
  236.4 5.7 copy-start.20
  236.4 5.7 copy-start.39
  242.2 4.5 copy-start.17
  246.7 5.6 copy-start.7
  252.3 10.5 %copy-start.24 = (bf16[2,512,8,64]{1,3,2,0:T(8,128)(2,1)S(1)}, bf16[2,512,8,64]{1,3,2,0:T(8,128)(2,1)}, u32[]{:S(2)}) copy-start(bf16[2,512,8,64]{1,3,2,0:T(8,128)(2,1)} %copy.96) | copy-start | bytes 3145732
  252.3 10.5 %copy-start.45 = (bf16[2,256,64]{1,2,0:T(8,128)(2,1)S(1)}, bf16[2,256,64]{1,2,0:T(8,128)(2,1)}, u32[]{:S(2)}) copy-start(bf16[2,256,64]{1,2,0:T(8,128)(2,1)} %param.34) | copy-start | bytes 196612
  263.6 41.1 %copy-start.38 = (bf16[64,8,2,512]{3,1,2,0:T(8,128)(2,1)S(1)}, bf16[64,8,2,512]{3,1,2,0:T(8,128)(2,1)}, u32[]{:S(2)}) copy-start(bf16[64,8,2,512]{3,1,2,0:T(8,128)(2,1)} %copy-done.37) | copy-start | bytes 3145732
  315.9 10.1 %copy-start.5 = (bf16[2,512,8,256]{1,3,2,0:T(8,128)(2,1)S(1)}, bf16[2,512,8,256]{1,3,2,0:T(8,128)(2,1)}, u32[]{:S(2)}) copy-start(bf16[2,512,8,256]{1,3,2,0:T(8,128)(2,1)} %copy-done.2) | copy-start | bytes 12582916
  397.2 5.2 copy-start.8
  402.9 5.8 copy-start.22
  418.7 6.3 copy-start.15
  418.7 6.3 copy-start.30
  418.7 6.3 copy-start.49
  418.7 6.3 copy-start.53
  418.7 6.3 copy-start.62
  427.5 56.2 %copy-start.10 = (f32[1024,512]{1,0:T(8,128)S(1)}, f32[1024,512]{1,0:T(8,128)}, u32[]{:S(2)}) copy-start(f32[1024,512]{1,0:T(8,128)} %copy-done.9) | copy-start | bytes 6291460
  660.0 4.9 copy-start.32
  664.9 5.7 copy-start.1
  (39 other events, 83.5 us)
Sparse Core Ops, SparseCore 0:
  42.4 126.5 all-gather.4
  236.3 148.0 all-gather.6
  417.0 242.9 all-reduce.3
where the time goes:
time: 688 us; the launch traced here: 678 us
  waiting for transfers between devices  298 us (43%)
  matrix products  147 us (21%)
  blocking collectives  111 us (16%)
  local copies, waits for them, and re-layouts  56.9 us (8%)
  other arithmetic  48.3 us (7%)
  between operations  15.8 us (2%)
    psum x1, waiting for transfers between devices, shards(): lax.psum((grad_gain_attn, grad_shift_attn, grad_w_qkv, grad_b_qkv, grad_w...  173 us
    all_gather x2, waiting for transfers between devices, prefix(): gathered = jax.tree.map(lambda a: lax.all_gather(a, axis), part)  125 us
    all_gather x2, blocking collectives, prefix(): gathered = jax.tree.map(lambda a: lax.all_gather(a, axis), part)  56.5 us
    psum x1, blocking collectives, shards(): lax.psum((grad_gain_attn, grad_shift_attn, grad_w_qkv, grad_b_qkv, grad_w...  54.3 us
    add x30, other arithmetic, add_up(): return jax.tree.map(jnp.add, earlier, later)  31.2 us
    unnamed x148, local copies, waits for them, and re-layouts  21.7 us
    dot_general x4, matrix products, contract_cols(): lax.dot_general(left, right, (((1,), (1,)), ((), ())), preferred_element_...  16.4 us
    dot_general x4, matrix products, contract_rows(): lax.dot_general(left, right, (((0,), (0,)), ((), ())), preferred_element_...  14.1 us
  transfers between devices with their start and end apart: 3, of which 3 were waited for; matrix products, arithmetic and copies ran while one was open for 16% of the time, Pallas kernels for 0%

commit v1 on v0

v1 whole, which is shorter than its diff:
```python
import functools
import math

import jax
import jax.numpy as jnp
from jax import lax
from jax.experimental import pallas as pl
from jax.experimental.pallas import tpu as pltpu
from jax.sharding import PartitionSpec as P

HEADS = 8
HEAD_DIM = 64
FEATS = 256
PAIRS = HEADS // 2
LANES = 2 * HEAD_DIM
AXES = ("dp", "seq")
BF = jnp.bfloat16
F32 = jnp.float32
Z_SCALE = HEAD_DIM ** (-0.25)
SQ_SCALE = 0.5 * HEAD_DIM ** (-0.5) / Z_SCALE
EXP_SCALE = Z_SCALE * math.log2(math.e)
EXP_SHIFT = 0.5 * math.log2(FEATS)
STATE_ROWS = PAIRS * LANES
SCAN_ROWS = STATE_ROWS + 16
TILE = 256
GELU_A = math.sqrt(2.0 / math.pi)
GELU_B = 0.044715
VMEM = 56 * 1024 * 1024


def dot(a, b):
    return lax.dot_general(a, b, (((1,), (0,)), ((), ())), preferred_element_type=F32)


def dot_nt(a, b):
    return lax.dot_general(a, b, (((1,), (1,)), ((), ())), preferred_element_type=F32)


def dot_tn(a, b):
    return lax.dot_general(a, b, (((0,), (0,)), ((), ())), preferred_element_type=F32)


def lower_half(shape):
    return lax.broadcasted_iota(jnp.int32, shape, 1) < HEAD_DIM


def swap_halves(values):
    return pltpu.roll(values, HEAD_DIM, 1)


def normalise(values):
    center = values - jnp.mean(values, axis=-1, keepdims=True)
    spread = jnp.mean(center * center, axis=-1, keepdims=True)
    scale = lax.rsqrt(spread + 1e-05)
    return center * scale, scale


def normalise_back(grad, unit, scale, gain):
    inner = grad * gain
    first = jnp.mean(inner, axis=-1, keepdims=True)
    second = jnp.mean(inner * unit, axis=-1, keepdims=True)
    return scale * (inner - first - unit * second)


def features(pair, tabs):
    wide = pair.astype(F32)
    square = wide * wide * SQ_SCALE
    high = square.astype(BF).astype(F32)
    low = swap_halves(square - high)
    keep = lower_half(wide.shape)
    even = jnp.where(keep, high, low).astype(BF)
    odd = jnp.where(keep, low, high).astype(BF)
    out = []
    for block, tab in ((even, tabs[0]), (odd, tabs[1])):
        proj = dot_nt(jnp.concatenate([pair, block], axis=1), tab)
        out.append(jnp.exp2(proj * EXP_SCALE - EXP_SHIFT).astype(BF))
    return out


def values_ones(pair):
    keep = lower_half(pair.shape)
    one = jnp.ones_like(pair)
    return jnp.where(keep, pair, one), jnp.where(keep, one, pair)


def causal_rows(first_row, rows, cols):
    return (
        lax.broadcasted_iota(jnp.int32, (rows, cols), 0) + first_row
        >= lax.broadcasted_iota(jnp.int32, (rows, cols), 1)
    )


def state_pair(state, norm, parity):
    wide = jnp.broadcast_to(norm, (HEAD_DIM, norm.shape[1]))
    return jnp.concatenate([state, wide] if parity == 0 else [wide, state], axis=0)


def kv_kernel(x_ref, gain_ref, shift_ref, w_ref, b_ref, tab_ref, h_ref, qkv_ref, phik_ref, state_ref):
    width = x_ref.shape[-1]
    unit, _ = normalise(x_ref[0].astype(F32))
    low = (unit * gain_ref[...] + shift_ref[...]).astype(BF)
    h_ref[0] = low
    qkv_ref[0] = (dot(low, w_ref[...]) + b_ref[...]).astype(BF)
    tabs = (tab_ref[0], tab_ref[1])
    norms = []
    for pair in range(PAIRS):
        key = qkv_ref[0, :, width + pair * LANES : width + (pair + 1) * LANES]
        value = qkv_ref[0, :, 2 * width + pair * LANES : 2 * width + (pair + 1) * LANES]
        phi = features(key, tabs)
        ones = values_ones(value)
        full = []
        for head in range(2):
            at = (2 * pair + head) * FEATS
            phik_ref[0, :, at : at + FEATS] = phi[head]
            full.append(dot_tn(ones[head], phi[head]))
        state_ref[0, pair * LANES : pair * LANES + HEAD_DIM, :] = full[0][:HEAD_DIM]
        state_ref[0, pair * LANES + HEAD_DIM : (pair + 1) * LANES, :] = full[1][HEAD_DIM:]
        norms += [full[0][HEAD_DIM : HEAD_DIM + 1], full[1][0:1]]
    state_ref[0, STATE_ROWS : STATE_ROWS + HEADS, :] = jnp.concatenate(norms, axis=0)
    state_ref[0, STATE_ROWS + HEADS :, :] = jnp.zeros((SCAN_ROWS - STATE_ROWS - HEADS, FEATS), F32)


def local_kernel(q_ref, v_ref, phik_ref, tab_ref, phiq_ref, num_ref):
    phi = features(q_ref[0], (tab_ref[0], tab_ref[1]))
    ones = values_ones(v_ref[0])
    span = q_ref.shape[1]
    for head in range(2):
        phiq_ref[0, :, head * FEATS : (head + 1) * FEATS] = phi[head]
        for row in range(0, span, TILE):
            cols = row + TILE
            keys = phik_ref[0, :cols, head * FEATS : (head + 1) * FEATS]
            scores = dot_nt(phi[head][row : row + TILE], keys)
            scores = jnp.where(causal_rows(row, TILE, cols), scores, 0.0).astype(BF)
            num_ref[0, row : row + TILE, head * LANES : (head + 1) * LANES] = dot(scores, ones[head][:cols])


def middle_kernel(
    per, x_ref, dy_ref, num_ref, phiq_ref, state_ref, w_out_ref, b_out_ref, gain_ref, shift_ref,
    w_up_ref, b_up_ref, w_down_ref, b_down_ref,
    out_ref, hid_ref, dup_ref, h2_ref, att_ref, dy1_ref, dy1_low_ref, dnum_ref, dstate_ref, sums_ref, sum_up_ref,
):
    step = pl.program_id(0)
    width = x_ref.shape[-1]
    att_parts, den_parts = [], []
    for pair in range(PAIRS):
        nums = []
        for head in range(2):
            at = 2 * pair + head
            rows = pair * LANES + head * HEAD_DIM
            state = state_pair(
                state_ref[0, rows : rows + HEAD_DIM, :].astype(BF),
                state_ref[0, STATE_ROWS + at : STATE_ROWS + at + 1, :].astype(BF),
                head,
            )
            nums.append(
                num_ref[:, at * LANES : (at + 1) * LANES]
                + dot_nt(phiq_ref[:, at * FEATS : (at + 1) * FEATS], state)
            )
        keep = lower_half(nums[0].shape)
        den = swap_halves(jnp.where(keep, nums[1], nums[0]))
        recip = 1.0 / den
        att_parts.append(jnp.where(keep, nums[0], nums[1]) * recip)
        den_parts.append(recip)
    mixed = jnp.concatenate([part.astype(BF) for part in att_parts], axis=1)
    att_ref[...] = mixed
    middle = x_ref[...].astype(F32) + dot(mixed, w_out_ref[...]) + b_out_ref[...]
    unit, scale = normalise(middle)
    low = (unit * gain_ref[...] + shift_ref[...]).astype(BF)
    h2_ref[...] = low
    grad_out = dy_ref[...]
    hidden = w_up_ref.shape[1]
    chunk = 512
    result = middle + b_down_ref[...]
    grad_low = jnp.zeros(middle.shape, F32)

    @pl.when(step == 0)
    def _():
        sums_ref[...] = jnp.zeros_like(sums_ref)
        sum_up_ref[...] = jnp.zeros_like(sum_up_ref)

    for at in range(0, hidden, chunk):
        up = dot(low, w_up_ref[:, at : at + chunk]) + b_up_ref[:, at : at + chunk]
        square = up * up
        tanh = jnp.tanh(up * (GELU_A + GELU_A * GELU_B * square))
        half = 0.5 + 0.5 * tanh
        act = (up * half).astype(BF)
        hid_ref[:, at : at + chunk] = act
        slope = half + (0.5 * up) * (1.0 - tanh * tanh) * (GELU_A + 3.0 * GELU_A * GELU_B * square)
        result += dot(act, w_down_ref[at : at + chunk, :])
        dup = (dot_nt(grad_out, w_down_ref[at : at + chunk, :]) * slope).astype(BF)
        dup_ref[:, at : at + chunk] = dup
        grad_low += dot_nt(dup, w_up_ref[:, at : at + chunk])
        sum_up_ref[:, at : at + chunk] += jnp.sum(dup.astype(F32), axis=0, keepdims=True)
    out_ref[...] = result.astype(BF)
    wide = grad_out.astype(F32)
    grad_mid = wide + normalise_back(grad_low, unit, scale, gain_ref[...])
    dy1_ref[...] = grad_mid
    grad_mid_low = grad_mid.astype(BF)
    dy1_low_ref[...] = grad_mid_low
    for row, item in enumerate((wide, grad_mid, grad_low * unit, grad_low)):
        sums_ref[row : row + 1, :] += jnp.sum(item, axis=0, keepdims=True)
    grad_att = dot_nt(grad_mid_low, w_out_ref[...])

    @pl.when(lax.rem(step, per) == 0)
    def _():
        dstate_ref[...] = jnp.zeros_like(dstate_ref)

    for pair in range(PAIRS):
        grad = grad_att[:, pair * LANES : (pair + 1) * LANES] * den_parts[pair]
        keep = lower_half(grad.shape)
        prod = swap_halves(-(grad * att_parts[pair]))
        both = (jnp.where(keep, grad, prod).astype(BF), jnp.where(keep, prod, grad).astype(BF))
        for head in range(2):
            at = 2 * pair + head
            dnum_ref[:, at * LANES : (at + 1) * LANES] = both[head]
            full = dot_tn(both[head], phiq_ref[:, at * FEATS : (at + 1) * FEATS])
            rows = pair * LANES + head * HEAD_DIM
            main = full[:HEAD_DIM] if head == 0 else full[HEAD_DIM:]
            rest = full[HEAD_DIM:] if head == 0 else full[:HEAD_DIM]
            dstate_ref[0, rows : rows + HEAD_DIM, :] += main
            dstate_ref[0, STATE_ROWS + at : STATE_ROWS + at + 1, :] += jnp.sum(rest, axis=0, keepdims=True)


def score_back_kernel(
    q_ref, v_ref, phiq_ref, phik_ref, dnum_ref, state_ref, norm_ref, tab_ref, dq_ref, dphik_ref, dv_ref
):
    span = q_ref.shape[1]
    ones = values_ones(v_ref[0])
    back, dvs = [], []
    for head in range(2):
        phiq = phiq_ref[0, :, head * FEATS : (head + 1) * FEATS]
        phik = phik_ref[0, :, head * FEATS : (head + 1) * FEATS]
        dnum = dnum_ref[0, :, head * LANES : (head + 1) * LANES]
        state = state_pair(
            state_ref[0, head * HEAD_DIM : (head + 1) * HEAD_DIM, :].astype(BF),
            norm_ref[0, pl.ds(2 * pl.program_id(1) + head, 1), :].astype(BF),
            head,
        )
        grads = []
        for row in range(0, span, TILE):
            cols = row + TILE
            mine = dnum[row : row + TILE]
            grad = dot_nt(mine, ones[head][:cols])
            grad = jnp.where(causal_rows(row, TILE, cols), grad, 0.0).astype(BF)
            grad_phi = dot(mine, state) + dot(grad, phik[:cols])
            grads.append((grad_phi * phiq[row : row + TILE].astype(F32)).astype(BF))
        back.append(dot(jnp.concatenate(grads, axis=0), tab_ref[head]))
        dv = []
        for row in range(0, span, TILE):
            count = span - row
            seen = (
                lax.broadcasted_iota(jnp.int32, (TILE, count), 0)
                <= lax.broadcasted_iota(jnp.int32, (TILE, count), 1)
            )
            turned = dot_nt(ones[head][row : row + TILE], dnum[row:])
            turned = jnp.where(seen, turned, 0.0).astype(BF)
            dphik_ref[0, row : row + TILE, head * FEATS : (head + 1) * FEATS] = dot(turned, phiq[row:])
            scores = dot_nt(phik[row : row + TILE], phiq[row:])
            scores = jnp.where(seen, scores, 0.0).astype(BF)
            dv.append(dot(scores, dnum[row:]))
        dvs.append(jnp.concatenate(dv, axis=0))
    keep = lower_half(dvs[0].shape)
    dv_ref[0] = jnp.where(keep, dvs[0], dvs[1])
    dq_ref[0] = finish_back(back, q_ref[0]).astype(BF)


def finish_back(back, pair):
    keep = lower_half(back[0].shape)
    main = jnp.where(keep, back[0], back[1])
    total = swap_halves(jnp.where(keep, back[1], back[0]))
    return main * Z_SCALE - total * pair.astype(F32) * (HEAD_DIM ** (-0.5))


def final_kernel(
    x_ref, dy1_ref, qkv_ref, phik_ref, dq_ref, dphik_ref, dv_ref, later_ref, tab_ref, gain_ref, shift_ref, w_ref,
    dx_ref, dkv_ref, sums_ref, sum_qkv_ref,
):
    width = x_ref.shape[-1]
    grad = dot_nt(dq_ref[0], w_ref[:, :width])

    @pl.when(pl.program_id(0) == 0)
    def _():
        sums_ref[...] = jnp.zeros_like(sums_ref)
        sum_qkv_ref[...] = jnp.zeros_like(sum_qkv_ref)

    for pair in range(PAIRS):
        key = qkv_ref[0, :, width + pair * LANES : width + (pair + 1) * LANES]
        value = qkv_ref[0, :, 2 * width + pair * LANES : 2 * width + (pair + 1) * LANES]
        ones = values_ones(value)
        back, dvs = [], []
        for head in range(2):
            at = 2 * pair + head
            rows = pair * LANES + head * HEAD_DIM
            state = later_ref[0, rows : rows + HEAD_DIM, :].astype(BF)
            norm = later_ref[0, STATE_ROWS + at : STATE_ROWS + at + 1, :]
            high = norm.astype(BF)
            low = (norm - high.astype(F32)).astype(BF)
            rest = jnp.concatenate(
                [high.astype(F32), low.astype(F32), jnp.zeros((HEAD_DIM - 2, FEATS), F32)], axis=0
            ).astype(BF)
            full = jnp.concatenate([state, rest] if head == 0 else [rest, state], axis=0)
            phik = phik_ref[0, :, at * FEATS : (at + 1) * FEATS]
            grad_phi = dphik_ref[0, :, at * FEATS : (at + 1) * FEATS] + dot(ones[head], full)
            inner = (grad_phi * phik.astype(F32)).astype(BF)
            back.append(dot(inner, tab_ref[head]))
            dvs.append(dot_nt(phik, full))
        keep = lower_half(dvs[0].shape)
        dk = finish_back(back, key).astype(BF)
        dv = (dv_ref[0, :, pair * LANES : (pair + 1) * LANES] + jnp.where(keep, dvs[0], dvs[1])).astype(BF)
        dkv_ref[0, :, pair * LANES : (pair + 1) * LANES] = dk
        dkv_ref[0, :, width + pair * LANES : width + (pair + 1) * LANES] = dv
    dkv = dkv_ref[0]
    grad += dot_nt(dkv, w_ref[:, width:])
    unit, scale = normalise(x_ref[0].astype(F32))
    dx_ref[0] = (dy1_ref[0] + normalise_back(grad, unit, scale, gain_ref[...])).astype(BF)
    sums_ref[0:1, :] += jnp.sum(grad * unit, axis=0, keepdims=True)
    sums_ref[1:2, :] += jnp.sum(grad, axis=0, keepdims=True)
    sum_qkv_ref[:, :width] += jnp.sum(dq_ref[0].astype(F32), axis=0, keepdims=True)
    sum_qkv_ref[:, width:] += jnp.sum(dkv.astype(F32), axis=0, keepdims=True)


def whole(shape):
    return pl.BlockSpec(shape, lambda *_: (0,) * len(shape))


def params(count):
    return pltpu.CompilerParams(
        dimension_semantics=("arbitrary",) * count, vmem_limit_bytes=VMEM
    )


def cost(flops, moved, exps=0):
    return pl.CostEstimate(flops=int(flops), bytes_accessed=int(moved), transcendentals=int(exps))


def shape(dims, kind):
    return jax.ShapeDtypeStruct(dims, kind)


def flip(bit, count):
    return [(i, i ^ (1 << bit)) for i in range(count)]


def bit_of(bit):
    place = lax.axis_index("dp") * lax.axis_size("seq") + lax.axis_index("seq")
    return (place >> bit) & 1


def swap_with(values, bit):
    return lax.ppermute(values, AXES, flip(bit, lax.axis_size("dp") * lax.axis_size("seq")))


def scan_blocks(values, bits, split, reverse):
    if not bits:
        return jnp.zeros_like(values)
    bit = bits[0]
    mine = bit_of(bit)
    far = (mine == 0) if reverse else (mine == 1)
    if split:
        half = values.shape[0] // 2
        got = swap_with(lax.dynamic_slice_in_dim(values, (1 - mine) * half, half, 0), bit)
        kept = lax.dynamic_slice_in_dim(values, mine * half, half, 0)
        before = scan_blocks(kept + got, bits[1:], split - 1, reverse)
        ours = before + jnp.where(far, got, 0.0)
        theirs = swap_with(before + jnp.where(far, 0.0, kept), bit)
        return jnp.concatenate(
            [jnp.where(mine == 0, ours, theirs), jnp.where(mine == 0, theirs, ours)], axis=0
        )
    got = swap_with(values, bit)
    part = jnp.where(far, got, 0.0)
    if len(bits) == 1:
        return part
    return part + scan_blocks(values + got, bits[1:], 0, reverse)


def shards(
    tokens, cotangent, gain_attn, shift_attn, w_qkv, b_qkv, w_out, b_out,
    gain_ffn, shift_ffn, w_up, b_up, w_down, b_down, tables, pick,
):
    seqs, span, width = tokens.shape
    hidden = w_up.shape[1]
    rows = seqs * span
    table = lax.dynamic_index_in_dim(tables, pick[0] % 2, 0, keepdims=False)
    none = jnp.zeros_like(table)
    minus = jnp.full((FEATS, LANES), -1.0, BF)
    tab_in = jnp.stack(
        [jnp.concatenate([table, none, minus], axis=1), jnp.concatenate([none, table, minus], axis=1)]
    )
    one = jnp.ones_like(table)
    tab_back = jnp.stack([jnp.concatenate([table, one], axis=1), jnp.concatenate([one, table], axis=1)])
    row = lambda a: a.reshape(1, -1)
    seq_bits = list(range(lax.axis_size("seq").bit_length() - 1))

    three = lambda d: pl.BlockSpec((1,) + d, lambda s: (s, 0, 0))
    h1, qkv, phi_k, state = pl.pallas_call(
        kv_kernel,
        grid=(seqs,),
        in_specs=[
            three((span, width)), whole((1, width)), whole((1, width)), whole((width, 3 * width)),
            whole((1, 3 * width)), whole((2, FEATS, 2 * LANES)),
        ],
        out_specs=[
            three((span, width)), three((span, 3 * width)), three((span, HEADS * FEATS)), three((SCAN_ROWS, FEATS)),
        ],
        out_shape=[
            shape((seqs, span, width), BF), shape((seqs, span, 3 * width), BF),
            shape((seqs, span, HEADS * FEATS), BF), shape((seqs, SCAN_ROWS, FEATS), F32),
        ],
        compiler_params=params(1),
        cost_estimate=cost(5e9, 12e6, 2e6),
        name="keys",
    )(tokens, row(gain_attn), row(shift_attn), w_qkv, row(b_qkv), tab_in)

    before = scan_blocks(state.reshape(seqs * SCAN_ROWS, FEATS), seq_bits, 2, False).reshape(
        seqs, SCAN_ROWS, FEATS
    )

    block = lambda w, at=0: pl.BlockSpec((1, span, w), lambda s, p: (s, 0, at + p))
    phi_q, num = pl.pallas_call(
        local_kernel,
        grid=(seqs, PAIRS),
        in_specs=[block(LANES), block(LANES, 2 * PAIRS), block(2 * FEATS), whole((2, FEATS, 2 * LANES))],
        out_specs=[block(2 * FEATS), block(2 * LANES)],
        out_shape=[shape((seqs, span, HEADS * FEATS), BF), shape((seqs, span, HEADS * LANES), F32)],
        compiler_params=params(2),
        cost_estimate=cost(8e9, 16e6, 2e6),
        name="local",
    )(qkv, qkv, phi_k, tab_in)

    per = span // TILE
    tile = lambda w: pl.BlockSpec((TILE, w), lambda t: (t, 0))
    of_seq = lambda d: pl.BlockSpec((1,) + d, lambda t: (t // per, 0, 0))
    flat = lambda a: a.reshape(rows, a.shape[-1])
    out, hid, dup, h2, att, dy1, dy1_low, dnum, dstate, sums, sum_up = pl.pallas_call(
        functools.partial(middle_kernel, per),
        grid=(seqs * per,),
        in_specs=[
            tile(width), tile(width), tile(HEADS * LANES), tile(HEADS * FEATS), of_seq((SCAN_ROWS, FEATS)),
            whole((width, width)), whole((1, width)), whole((1, width)), whole((1, width)),
            whole((width, hidden)), whole((1, hidden)), whole((hidden, width)), whole((1, width)),
        ],
        out_specs=[
            tile(width), tile(hidden), tile(hidden), tile(width), tile(width), tile(width), tile(width),
            tile(HEADS * LANES), of_seq((SCAN_ROWS, FEATS)), whole((8, width)), whole((1, hidden)),
        ],
        out_shape=[
            shape((rows, width), BF), shape((rows, hidden), BF), shape((rows, hidden), BF), shape((rows, width), BF),
            shape((rows, width), BF), shape((rows, width), F32), shape((rows, width), BF),
            shape((rows, HEADS * LANES), BF), shape((seqs, SCAN_ROWS, FEATS), F32), shape((8, width), F32),
            shape((1, hidden), F32),
        ],
        compiler_params=params(1),
        cost_estimate=cost(20e9, 40e6, 2e6),
        name="middle",
    )(
        flat(tokens), flat(cotangent), flat(num), flat(phi_q), before, w_out, row(b_out), row(gain_ffn),
        row(shift_ffn), w_up, row(b_up), w_down, row(b_down),
    )

    later = scan_blocks(dstate.reshape(seqs * SCAN_ROWS, FEATS), seq_bits, 2, True).reshape(
        seqs, SCAN_ROWS, FEATS
    )
    grad_w_down = dot_tn(hid, flat(cotangent))
    grad_w_up = dot_tn(h2, dup)
    grad_w_out = dot_tn(att, dy1_low)

    dq, dphik, dv = pl.pallas_call(
        score_back_kernel,
        grid=(seqs, PAIRS),
        in_specs=[
            block(LANES), block(LANES, 2 * PAIRS), block(2 * FEATS), block(2 * FEATS), block(2 * LANES),
            pl.BlockSpec((1, LANES, FEATS), lambda s, p: (s, p, 0)),
            pl.BlockSpec((1, HEADS, FEATS), lambda s, p: (s, STATE_ROWS // HEADS, 0)),
            whole((2, FEATS, LANES)),
        ],
        out_specs=[block(LANES), block(2 * FEATS), block(LANES)],
        out_shape=[
            shape((seqs, span, width), BF), shape((seqs, span, HEADS * FEATS), F32), shape((seqs, span, width), F32),
        ],
        compiler_params=params(2),
        cost_estimate=cost(20e9, 30e6),
        name="scores",
    )(qkv, qkv, phi_q, phi_k, dnum.reshape(seqs, span, -1), before, before, tab_back)

    dx, dkv, sums_attn, sum_qkv = pl.pallas_call(
        final_kernel,
        grid=(seqs,),
        in_specs=[
            three((span, width)), three((span, width)), three((span, 3 * width)), three((span, HEADS * FEATS)),
            three((span, width)), three((span, HEADS * FEATS)), three((span, width)), three((SCAN_ROWS, FEATS)),
            whole((2, FEATS, LANES)), whole((1, width)), whole((1, width)), whole((width, 3 * width)),
        ],
        out_specs=[three((span, width)), three((span, 2 * width)), whole((8, width)), whole((1, 3 * width))],
        out_shape=[
            shape((seqs, span, width), BF), shape((seqs, span, 2 * width), BF), shape((8, width), F32),
            shape((1, 3 * width), F32),
        ],
        compiler_params=params(1),
        cost_estimate=cost(8e9, 20e6),
        name="final",
    )(
        tokens, dy1.reshape(seqs, span, width), qkv, phi_k, dq, dphik, dv, later, tab_back, row(gain_attn),
        row(shift_attn), w_qkv,
    )
    grad_w_q = dot_tn(flat(h1), flat(dq))
    grad_w_kv = dot_tn(flat(h1), flat(dkv))
    return finish(
        out.reshape(seqs, span, width), dx, grad_w_down, grad_w_up, grad_w_out, grad_w_q, grad_w_kv,
        sums, sum_up, sums_attn, sum_qkv,
    )


def finish(out, dx, grad_w_down, grad_w_up, grad_w_out, grad_w_q, grad_w_kv, sums, sum_up, sums_attn, sum_qkv):
    total = lax.psum(
        (grad_w_down, grad_w_up, grad_w_out, grad_w_q, grad_w_kv, sums, sum_up, sums_attn, sum_qkv), AXES
    )
    grad_w_down, grad_w_up, grad_w_out, grad_w_q, grad_w_kv, sums, sum_up, sums_attn, sum_qkv = total
    return (
        out, dx, sums_attn[0], sums_attn[1], jnp.concatenate([grad_w_q, grad_w_kv], axis=1), sum_qkv[0],
        grad_w_out, sums[1], sums[2], sums[3], grad_w_up, sum_up[0], grad_w_down, sums[0],
    )


def solution(mesh):
    split = P("dp", "seq", None)
    return jax.shard_map(
        shards,
        mesh=mesh,
        in_specs=(split, split) + (P(),) * 14,
        out_specs=(split, split) + (P(),) * 12,
        check_vma=False,
    )
```

time: 688 us -> 443 us (0.64); the launches traced: 678 us -> 440 us
  matrix products: 147 us -> 18.8 us
  Pallas kernels: 0 us -> 85.3 us
  blocking collectives: 111 us -> 42.4 us
  waiting for transfers between devices: 298 us -> 244 us
  local copies, waits for them, and re-layouts: 56.9 us -> 11.8 us
  other arithmetic: 48.3 us -> 11.4 us
  starting transfers between devices: 0.29 us -> 11.8 us
    dot_general x30 -> x5, matrix products: 147 us -> 18.8 us  [dot_tn(): lax.dot_general(a, b, (((0,), (0,)), ((), ())), preferred_element_type=F32)]
    all_gather x2 -> x0, waiting for transfers between devices: 125 us -> none  [prefix(): gathered = jax.tree.map(lambda a: lax.all_gather(a, axis), part)]
    pallas_call x0 -> x5, Pallas kernels: none -> 85.3 us  [the longest x1 27.5 us: shards(): pl.pallas_call(functools.partial(middle_kernel, per), grid=(seqs * per,),...]
    all_gather x2 -> x0, blocking collectives: 56.5 us -> none  [prefix(): gathered = jax.tree.map(lambda a: lax.all_gather(a, axis), part)]
    ppermute x0 -> x12, waiting for transfers between devices: none -> 50.6 us  [swap_with(): lax.ppermute(values, AXES, flip(bit, lax.axis_size('dp') * lax.axis_size(...]
    add x31 -> x10, other arithmetic: 31.2 us -> 3.4 us  [the longest x4 2.3 us: scan_blocks(): before = scan_blocks(kept + got, bits[1:], split - 1, reverse)]
    psum x1, waiting for transfers between devices: 173 us -> 193 us  [finish(): lax.psum((grad_w_down, grad_w_up, grad_w_out, grad_w_q, grad_w_kv, sums,...]
    reshape x7 -> x1, local copies, waits for them, and re-layouts: 20.3 us -> 1.3 us  [shards(): row = lambda a: a.reshape(1, -1)]
  transfers between devices with their start and end apart: 3 -> 13, of which waited for: 3 -> 10; matrix products, arithmetic and copies ran while one was open for 16% -> 4% of each run, Pallas kernels for 0% -> 8%
where the time goes in v1:
time: 443 us; the launch traced here: 440 us
  waiting for transfers between devices  244 us (55%)
  Pallas kernels  85.3 us (19%)
  blocking collectives  42.4 us (10%)
  matrix products  18.8 us (4%)
  between operations  14.9 us (3%)
  local copies, waits for them, and re-layouts  11.8 us (3%)
  starting transfers between devices  11.8 us (3%)
  other arithmetic  11.4 us (3%)
    psum x1, waiting for transfers between devices, finish(): lax.psum((grad_w_down, grad_w_up, grad_w_out, grad_w_q, grad_w_kv, sums,...  193 us
    ppermute x12, waiting for transfers between devices, swap_with(): lax.ppermute(values, AXES, flip(bit, lax.axis_size('dp') * lax.axis_size(...  50.6 us
    psum x1, blocking collectives, finish(): lax.psum((grad_w_down, grad_w_up, grad_w_out, grad_w_q, grad_w_kv, sums,...  42.4 us
    pallas_call x1, Pallas kernels, shards(): pl.pallas_call(functools.partial(middle_kernel, per), grid=(seqs * per,),...  27.5 us
    pallas_call x1, Pallas kernels, shards(): pl.pallas_call(score_back_kernel, grid=(seqs, PAIRS), in_specs=[block(LAN...  22.4 us
    dot_general x5, matrix products, dot_tn(): lax.dot_general(a, b, (((0,), (0,)), ((), ())), preferred_element_type=F32)  18.8 us
    pallas_call x1, Pallas kernels, shards(): pl.pallas_call(final_kernel, grid=(seqs,), in_specs=[three((span, width))...  15 us
    ppermute x12, starting transfers between devices, swap_with(): lax.ppermute(values, AXES, flip(bit, lax.axis_size('dp') * lax.axis_size(...  11.8 us
  transfers between devices with their start and end apart: 13, of which 10 were waited for; matrix products, arithmetic and copies ran while one was open for 4% of the time, Pallas kernels for 8%

profile of v1, /device:TPU:13, one launch (start us, length us, event | category | flops | bytes accessed | tf_op | source)
XLA Modules:
  0.0 440.2 jit_solution(4456115243510584635)
XLA Ops:
  7.9 1.3 reshape.96.b_ref
  10.3 8.9 %keys.1 = (bf16[2,512,512]{2,1,0:T(8,128)(2,1)}, bf16[2,512,1536]{2,1,0:T(8,128)(2,1)}, bf16[2,512,2048]{2,1,0:T(8,128)(2,1)}, f32[2,528,256]{2,1,0:T(8,128)}) custom-call(bf16[2,512,512]{2,1,0:T(8,128)(2,1)} %x_ref.3, f32[1,512]{1,0:T(1,128)} %bitcast.79, f32[1,512]{1,0:T(1,128)} %bitcast.81, bf16[512,1536]{1,0:T(8,128)(2,1)} %w_ref.3, ...), custom_call_target="tpu_custom_call" | custom-call | flops 5000000000 | bytes 12000000 | tf_op jit(solution)/shard_map/keys/pallas_call | solution.py:395
  21.0 1.6 collective-permute-done
  22.5 1.1 dynamic-slice_add_fusion.1
  24.0 7.5 %collective-permute-done.1 = f32[264,256]{1,0:T(8,128)S(1)} collective-permute-done((f32[264,256]{1,0:T(8,128)S(1)}, f32[264,256]{1,0:T(8,128)S(1)}, u32[]{:S(2)}, u32[]{:S(2)}) %collective-permute-start.1) | collective-permute-done | bytes 270368 | tf_op jit(solution)/shard_map/ppermute | solution.py:350
  31.7 6.6 %collective-permute-done.2 = f32[264,256]{1,0:T(8,128)S(1)} collective-permute-done((f32[264,256]{1,0:T(8,128)S(1)}, f32[264,256]{1,0:T(8,128)S(1)}, u32[]{:S(2)}, u32[]{:S(2)}) %collective-permute-start.2) | collective-permute-done | bytes 270368 | tf_op jit(solution)/shard_map/ppermute | solution.py:350
  38.4 2.4 collective-permute-start.3
  40.7 11.9 %collective-permute-done.3 = f32[264,256]{1,0:T(8,128)S(1)} collective-permute-done((f32[264,256]{1,0:T(8,128)S(1)}, f32[264,256]{1,0:T(8,128)S(1)}, u32[]{:S(2)}, u32[]{:S(2)}) %collective-permute-start.3) | collective-permute-done | bytes 270368 | tf_op jit(solution)/shard_map/ppermute | solution.py:350
  53.6 7.6 %collective-permute-done.4 = f32[264,256]{1,0:T(8,128)S(1)} collective-permute-done((f32[264,256]{1,0:T(8,128)}, f32[264,256]{1,0:T(8,128)S(1)}, u32[]{:S(2)}, u32[]{:S(2)}) %collective-permute-start.4) | collective-permute-done | bytes 270368 | tf_op jit(solution)/shard_map/ppermute | solution.py:350
  61.3 1.4 collective-permute-start.5
  62.7 11.5 %local.1 = (bf16[2,512,2048]{2,1,0:T(8,128)(2,1)}, f32[2,512,1024]{2,1,0:T(8,128)}) custom-call(bf16[2,512,1536]{2,1,0:T(8,128)(2,1)} %get-tuple-element.38.q_ref.v_ref.qkv_ref, bf16[2,512,1536]{2,1,0:T(8,128)(2,1)} %get-tuple-element.38.q_ref.v_ref.qkv_ref, bf16[2,512,2048]{2,1,0:T(8,128)(2,1)} %get-tuple-element.39.phik_ref, ...), custom_call_target="tpu_custom_call" | custom-call | flops 8000000000 | bytes 16000000 | tf_op jit(solution)/shard_map/local/pallas_call | solution.py:419
  75.4 27.5 %middle.1 = (bf16[1024,512]{1,0:T(8,128)(2,1)}, bf16[1024,2048]{1,0:T(8,128)(2,1)}, bf16[1024,2048]{1,0:T(8,128)(2,1)}, bf16[1024,512]{1,0:T(8,128)(2,1)}, bf16[...) custom-call(bf16[1024,512]{1,0:T(8,128)(2,1)} %bitcast.73, ...), custom_call_target="tpu_custom_call" | custom-call | flops 20000000000 | bytes 40000000 | tf_op jit(solution)/shard_map/middle/pallas_call | solution.py:434
  104.1 1.9 collective-permute-done.6
  106.0 1.1 dynamic-slice_add_fusion
  108.2 7.0 %collective-permute-done.7 = f32[264,256]{1,0:T(8,128)S(1)} collective-permute-done((f32[264,256]{1,0:T(8,128)S(1)}, f32[264,256]{1,0:T(8,128)S(1)}, u32[]{:S(2)}, u32[]{:S(2)}) %collective-permute-start.7) | collective-permute-done | bytes 270368 | tf_op jit(solution)/shard_map/ppermute | solution.py:350
  115.3 22.4 %scores.1 = (bf16[2,512,512]{2,1,0:T(8,128)(2,1)}, f32[2,512,2048]{2,1,0:T(8,128)}, f32[2,512,512]{2,1,0:T(8,128)}) custom-call(bf16[2,512,1536]{2,1,0:T(8,128)(2,1)} %get-tuple-element.38.q_ref.v_ref.qkv_ref, bf16[2,512,1536]{2,1,0:T(8,128)(2,1)} %get-tuple-element.38.q_ref.v_ref.qkv_ref, bf16[2,512,2048]{2,1,0:T(8,128)(2,1)} %get-tuple-element.41.phiq_ref, ...), custom_call_target="tpu_custom_call" | custom-call | flops 20000000000 | bytes 30000000 | tf_op jit(solution)/shard_map/scores/pallas_call | solution.py:467
  137.8 3.2 collective-permute-start.9
  141.0 6.7 %fusion.4 = f32[2048,512]{1,0:T(8,128)} fusion(bf16[1024,2048]{1,0:T(8,128)(2,1)} %get-tuple-element.61, bf16[1024,512]{1,0:T(8,128)(2,1)S(1)} %bitcast.72), kind=kOutput, calls=%fused_computation.44 | convolution fusion | flops 2147483648 | bytes 9437184 | tf_op jit(solution)/shard_map/dot_general | solution.py:40
  147.7 4.1 collective-permute-done.9
  152.2 1.7 fusion.2
  153.9 1.7 convolution_bitcast_fusion.1
  155.6 2.6 collective-permute-done.10
  158.4 2.7 collective-permute-start.11
  161.0 4.4 %fusion.3 = f32[512,2048]{1,0:T(8,128)} fusion(bf16[1024,512]{1,0:T(8,128)(2,1)S(1)} %copy-done.7, bf16[1024,2048]{1,0:T(8,128)(2,1)S(1)} %copy-done.2), kind=kOutput, calls=%fused_computation.43 | convolution fusion | flops 2147483648 | bytes 9437184 | tf_op jit(solution)/shard_map/dot_general | solution.py:40
  166.7 15.0 %final.1 = (bf16[2,512,512]{2,1,0:T(8,128)(2,1)}, bf16[2,512,1024]{2,1,0:T(8,128)(2,1)}, f32[8,512]{1,0:T(8,128)}, f32[1,1536]{1,0:T(1,128)}) custom-call(bf16[2,512,512]{2,1,0:T(8,128)(2,1)} %x_ref.3, f32[2,512,512]{2,1,0:T(8,128)} %bitcast.85, bf16[2,512,1536]{2,1,0:T(8,128)(2,1)} %get-tuple-element.38.q_ref.v_ref.qkv_ref, ...), custom_call_target="tpu_custom_call" | custom-call | flops 8000000000 | bytes 20000000 | tf_op jit(solution)/shard_map/final/pallas_call | solution.py:485
  181.8 4.2 convolution_bitcast_fusion
  186.7 42.4 %all-reduce.2 = (f32[8,512]{1,0:T(8,128)S(1)}, f32[1536]{0:T(1024)}, f32[8,512]{1,0:T(8,128)S(1)}, f32[2048]{0:T(1024)}) all-reduce(f32[8,512]{1,0:T(8,128)S(1)} %copy-done.11, f32[1536]{0:T(1024)S(1)} %reduce, f32[8,512]{1,0:T(8,128)S(1)} %copy-done.10, f32[2048]{0:T(1024)S(1)} %bitcast.64), channel_id=1, replica_groups=mesh['dp'=2,'seq'=16] {'dp','seq'}, use_global_device_ids=true, to_apply=%region_0.1 | all-reduce | flops 11776 | bytes 94208 | tf_op jit(solution)/shard_map/psum | solution.py:514
  229.7 193.1 %all-reduce.6.cloned.1.call-done = (f32[512,1024]{1,0:T(8,128)}, f32[512,512]{1,0:T(8,128)}, f32[512,512]{1,0:T(8,128)}, f32[512,2048]{1,0:T(8,128)}, f32[2048,512]{1,0:T(8,128)}) async-done(((f32[512,1024]{1,0:T(8,128)}, f32[512,512]{1,0:T(8,128)}, f32[512,512]{1,0:T(8,128)}, f32[512,2048]{1,0:T(8,128)}, f32[2048,512]{1,0:T(8,128)}), (f32[512,1024]{1,0:T(8,128)}, f32[512,512]{1,0:T(8,128)}, ...) | async-done | bytes 12582928 | tf_op jit(solution)/shard_map/psum | solution.py:514
  422.8 3.9 pad_maximum_fusion
  427.6 2.1 copy.42
  429.8 1.6 copy-done.3
  431.3 2.0 copy.43
  (78 shorter events, 12.3 us)
Async XLA Ops:
  7.2 2.0 copy-start
  7.2 415.6 %all-reduce.6.cloned.1.call-start = ((), (), s32[]{:S(2)}) async-start(), calls=%async_computation | async-start | bytes 25165824 | tf_op jit(solution)/shard_map/psum | solution.py:514
  20.2 2.3 collective-permute-start
  23.7 7.8 %collective-permute-start.1 = (f32[264,256]{1,0:T(8,128)S(1)}, f32[264,256]{1,0:T(8,128)S(1)}, u32[]{:S(2)}, u32[]{:S(2)}) collective-permute-start(f32[264,256]{1,0:T(8,128)S(1)} %constant_dynamic-slice_fusion.2), channel_id=1, source_target_pairs={{0,2},{1,3},{2,0},{3,1},{4,6},{5,7},{6,4},{7,5},{8,10},{9,11},{10,... | collective-permute-start | bytes 811016 | tf_op jit(solution)/shard_map/ppermute | solution.py:350
  24.0 37.3 %copy-start.5 = (f32[2,528,256]{2,1,0:T(8,128)S(1)}, f32[2,528,256]{2,1,0:T(8,128)}, u32[]{:S(2)}) copy-start(f32[2,528,256]{2,1,0:T(8,128)} %get-tuple-element.42) | copy-start | bytes 3244036
  31.5 6.8 %collective-permute-start.2 = (f32[264,256]{1,0:T(8,128)S(1)}, f32[264,256]{1,0:T(8,128)S(1)}, u32[]{:S(2)}, u32[]{:S(2)}) collective-permute-start(f32[264,256]{1,0:T(8,128)S(1)} %dynamic-slice_add_fusion.3), channel_id=1, source_target_pairs={{0,4},{1,5},{2,6},{3,7},{4,0},{5,1},{6,2},{7,3},{8,12},{9,13},{10,... | collective-permute-start | bytes 811016 | tf_op jit(solution)/shard_map/ppermute | solution.py:350
  38.4 14.3 %collective-permute-start.3 = (f32[264,256]{1,0:T(8,128)S(1)}, f32[264,256]{1,0:T(8,128)S(1)}, u32[]{:S(2)}, u32[]{:S(2)}) collective-permute-start(f32[264,256]{1,0:T(8,128)S(1)} %add.113), channel_id=1, source_target_pairs={{0,8},{1,9},{2,10},{3,11},{4,12},{5,13},{6,14},{7,15},{8,0},{9,1},... | collective-permute-start | bytes 811016 | tf_op jit(solution)/shard_map/ppermute | solution.py:350
  53.4 7.8 %collective-permute-start.4 = (f32[264,256]{1,0:T(8,128)}, f32[264,256]{1,0:T(8,128)S(1)}, u32[]{:S(2)}, u32[]{:S(2)}) collective-permute-start(f32[264,256]{1,0:T(8,128)} %get-tuple-element.73), channel_id=1, source_target_pairs={{0,2},{1,3},{2,0},{3,1},{4,6},{5,7},{6,4},{7,5},{8,10},{9,11},{10,... | collective-permute-start | bytes 811016 | tf_op jit(solution)/shard_map/ppermute | solution.py:350
  61.3 12.9 %collective-permute-start.5 = (f32[528,256]{1,0:T(8,128)S(1)}, f32[528,256]{1,0:T(8,128)S(1)}, u32[]{:S(2)}, u32[]{:S(2)}) collective-permute-start(f32[528,256]{1,0:T(8,128)S(1)} %select_add_fusion.2), channel_id=1, source_target_pairs={{0,1},{1,0},{2,3},{3,2},{4,5},{5,4},{6,7},{7,6},{8,9},{9,8},{10,11... | collective-permute-start | bytes 1622024 | tf_op jit(solution)/shard_map/ppermute | solution.py:350
  104.0 2.0 collective-permute-start.6
  107.2 8.0 %collective-permute-start.7 = (f32[264,256]{1,0:T(8,128)S(1)}, f32[264,256]{1,0:T(8,128)S(1)}, u32[]{:S(2)}, u32[]{:S(2)}) collective-permute-start(f32[264,256]{1,0:T(8,128)S(1)} %constant_dynamic-slice_fusion), channel_id=1, source_target_pairs={{0,2},{1,3},{2,0},{3,1},{4,6},{5,7},{6,4},{7,5},{8,10},{9,11},{10,... | collective-permute-start | bytes 811016 | tf_op jit(solution)/shard_map/ppermute | solution.py:350
  115.2 22.5 %collective-permute-start.8 = (f32[264,256]{1,0:T(8,128)S(1)}, f32[264,256]{1,0:T(8,128)S(1)}, u32[]{:S(2)}, u32[]{:S(2)}) collective-permute-start(f32[264,256]{1,0:T(8,128)S(1)} %dynamic-slice_add_fusion.2), channel_id=1, source_target_pairs={{0,4},{1,5},{2,6},{3,7},{4,0},{5,1},{6,2},{7,3},{8,12},{9,13},{10,... | collective-permute-start | bytes 811016 | tf_op jit(solution)/shard_map/ppermute | solution.py:350
  115.3 25.7 %copy-start.14 = (bf16[2,512,512]{2,1,0:T(8,128)(2,1)S(1)}, bf16[2,512,512]{2,1,0:T(8,128)(2,1)}, u32[]{:S(2)}) copy-start(bf16[2,512,512]{2,1,0:T(8,128)(2,1)} %param.17) | copy-start | bytes 3145732
  137.8 13.9 %collective-permute-start.9 = (f32[264,256]{1,0:T(8,128)S(1)}, f32[264,256]{1,0:T(8,128)S(1)}, u32[]{:S(2)}, u32[]{:S(2)}) collective-permute-start(f32[264,256]{1,0:T(8,128)S(1)} %add.121), channel_id=1, source_target_pairs={{0,8},{1,9},{2,10},{3,11},{4,12},{5,13},{6,14},{7,15},{8,0},{9,1},... | collective-permute-start | bytes 811016 | tf_op jit(solution)/shard_map/ppermute | solution.py:350
  141.0 11.2 %copy-start.15 = (bf16[1024,512]{1,0:T(8,128)(2,1)S(1)}, bf16[1024,512]{1,0:T(8,128)(2,1)}, u32[]{:S(2)}) copy-start(bf16[1024,512]{1,0:T(8,128)(2,1)} %get-tuple-element.55) | copy-start | bytes 3145732
  141.0 11.2 %copy-start.16 = (bf16[1024,512]{1,0:T(8,128)(2,1)S(1)}, bf16[1024,512]{1,0:T(8,128)(2,1)}, u32[]{:S(2)}) copy-start(bf16[1024,512]{1,0:T(8,128)(2,1)} %get-tuple-element.56) | copy-start | bytes 3145732
  151.9 6.3 %collective-permute-start.10 = (f32[264,256]{1,0:T(8,128)S(1)}, f32[264,256]{1,0:T(8,128)S(1)}, u32[]{:S(2)}, u32[]{:S(2)}) collective-permute-start(f32[264,256]{1,0:T(8,128)S(1)} %get-tuple-element.71), channel_id=1, source_target_pairs={{0,2},{1,3},{2,0},{3,1},{4,6},{5,7},{6,4},{7,5},{8,10},{9,11},{10,... | collective-permute-start | bytes 811016 | tf_op jit(solution)/shard_map/ppermute | solution.py:350
  152.1 1.7 copy-start.8
  152.1 1.7 copy-start.17
  153.9 4.4 copy-start.6
  153.9 7.2 %copy-start.2 = (bf16[1024,2048]{1,0:T(8,128)(2,1)S(1)}, bf16[1024,2048]{1,0:T(8,128)(2,1)}, u32[]{:S(2)}) copy-start(bf16[1024,2048]{1,0:T(8,128)(2,1)} %get-tuple-element.59) | copy-start | bytes 12582916
  155.6 5.5 %copy-start.7 = (bf16[1024,512]{1,0:T(8,128)(2,1)S(1)}, bf16[1024,512]{1,0:T(8,128)(2,1)}, u32[]{:S(2)}) copy-start(bf16[1024,512]{1,0:T(8,128)(2,1)} %get-tuple-element.58) | copy-start | bytes 3145732
  158.4 7.1 %collective-permute-start.11 = (f32[528,256]{1,0:T(8,128)S(1)}, f32[528,256]{1,0:T(8,128)S(1)}, u32[]{:S(2)}, u32[]{:S(2)}) collective-permute-start(f32[528,256]{1,0:T(8,128)S(1)} %select_add_fusion), channel_id=1, source_target_pairs={{0,1},{1,0},{2,3},{3,2},{4,5},{5,4},{6,7},{7,6},{8,9},{9,8},{10,11... | collective-permute-start | bytes 1622024 | tf_op jit(solution)/shard_map/ppermute | solution.py:350
  185.9 0.7 copy-start.13
  185.9 0.7 copy-start.10
  185.9 0.7 copy-start.11
  185.9 0.7 copy-start.12
  422.8 3.9 copy-start.9
  422.8 4.9 %copy-start.4 = (f32[512,2048]{1,0:T(8,128)S(1)}, f32[512,2048]{1,0:T(8,128)}, u32[]{:S(2)}) copy-start(f32[512,2048]{1,0:T(8,128)} %get-tuple-element.105) | copy-start | bytes 12582916
  427.6 3.7 copy-start.3
  431.3 2.0 copy-start.1
Sparse Core Ops, SparseCore 0:
  186.1 236.6 all-reduce.5

commit v2 on v1

--- a/solution.py
+++ b/solution.py
@@ -13,7 +13,7 @@
 FEATS = 256
 PAIRS = HEADS // 2
 LANES = 2 * HEAD_DIM
-AXES = ("dp", "seq")
+AXES = ("x", "z", "y", "c")
 BF = jnp.bfloat16
 F32 = jnp.float32
 Z_SCALE = HEAD_DIM ** (-0.25)
@@ -120,7 +120,8 @@
     state_ref[0, STATE_ROWS + HEADS :, :] = jnp.zeros((SCAN_ROWS - STATE_ROWS - HEADS, FEATS), F32)
 
 
-def local_kernel(q_ref, v_ref, phik_ref, tab_ref, phiq_ref, num_ref):
+def local_kernel(q_ref, v_ref, phik_ref, tab_ref, *rest):
+    phiq_ref, num_ref = rest[-2:]
     phi = features(q_ref[0], (tab_ref[0], tab_ref[1]))
     ones = values_ones(v_ref[0])
     span = q_ref.shape[1]
@@ -222,8 +223,9 @@
 
 
 def score_back_kernel(
-    q_ref, v_ref, phiq_ref, phik_ref, dnum_ref, state_ref, norm_ref, tab_ref, dq_ref, dphik_ref, dv_ref
+    q_ref, v_ref, phiq_ref, phik_ref, dnum_ref, state_ref, norm_ref, tab_ref, *rest
 ):
+    dq_ref, dphik_ref, dv_ref = rest[-3:]
     span = q_ref.shape[1]
     ones = values_ones(v_ref[0])
     back, dvs = [], []
@@ -233,7 +235,7 @@
         dnum = dnum_ref[0, :, head * LANES : (head + 1) * LANES]
         state = state_pair(
             state_ref[0, head * HEAD_DIM : (head + 1) * HEAD_DIM, :].astype(BF),
-            norm_ref[0, pl.ds(2 * pl.program_id(1) + head, 1), :].astype(BF),
+            norm_ref[0, pl.ds(2 * pl.program_id(0) + head, 1), :].astype(BF),
             head,
         )
         grads = []
@@ -273,7 +275,7 @@
 
 def final_kernel(
     x_ref, dy1_ref, qkv_ref, phik_ref, dq_ref, dphik_ref, dv_ref, later_ref, tab_ref, gain_ref, shift_ref, w_ref,
-    dx_ref, dkv_ref, sums_ref, sum_qkv_ref,
+    dx_ref, dqkv_ref, sums_ref, sum_qkv_ref,
 ):
     width = x_ref.shape[-1]
     grad = dot_nt(dq_ref[0], w_ref[:, :width])
@@ -307,9 +309,10 @@
         keep = lower_half(dvs[0].shape)
         dk = finish_back(back, key).astype(BF)
         dv = (dv_ref[0, :, pair * LANES : (pair + 1) * LANES] + jnp.where(keep, dvs[0], dvs[1])).astype(BF)
-        dkv_ref[0, :, pair * LANES : (pair + 1) * LANES] = dk
-        dkv_ref[0, :, width + pair * LANES : width + (pair + 1) * LANES] = dv
-    dkv = dkv_ref[0]
+        dqkv_ref[0, :, width + pair * LANES : width + (pair + 1) * LANES] = dk
+        dqkv_ref[0, :, 2 * width + pair * LANES : 2 * width + (pair + 1) * LANES] = dv
+    dqkv_ref[0, :, :width] = dq_ref[0]
+    dkv = dqkv_ref[0, :, width:]
     grad += dot_nt(dkv, w_ref[:, width:])
     unit, scale = normalise(x_ref[0].astype(F32))
     dx_ref[0] = (dy1_ref[0] + normalise_back(grad, unit, scale, gain_ref[...])).astype(BF)
@@ -319,6 +322,85 @@
     sum_qkv_ref[:, width:] += jnp.sum(dkv.astype(F32), axis=0, keepdims=True)
 
 
+def put_chunks(out_ref, values, first, row, rows):
+    for chunk in range(values.shape[0] // rows):
+        for strip in range(values.shape[1] // LANES):
+            at = row + strip * rows
+            out_ref[first + chunk, at : at + rows, :] = values[
+                chunk * rows : (chunk + 1) * rows, strip * LANES : (strip + 1) * LANES
+            ]
+
+
+def ffn_grads_kernel(downs, ups, half_ref, hid_ref, dy_ref, h2_ref, dup_ref, att_ref, dy1_ref, out_ref):
+    step = pl.program_id(0)
+    chips = out_ref.shape[0]
+    for at in range(downs):
+
+        @pl.when(step == at)
+        def _():
+            values = dot_tn(hid_ref[...], dy_ref[...])
+            put_chunks(out_ref, values, at * chips // downs, 0, values.shape[0] * downs // chips)
+
+    base = dy_ref.shape[1] // LANES * (hid_ref.shape[1] * downs // chips)
+    rows = h2_ref.shape[1] // chips
+    block = dup_ref.shape[1] // LANES
+    for at in range(ups):
+
+        @pl.when(step == downs + at)
+        def _():
+            put_chunks(out_ref, dot_tn(h2_ref[...], dup_ref[...]), 0, base + at * block * rows, rows)
+
+    @pl.when(step == downs + ups)
+    def _():
+        put_chunks(out_ref, dot_tn(att_ref[...], dy1_ref[...]), 0, base + ups * block * rows, rows)
+
+
+def qkv_grads_kernel(steps, half_ref, h1_ref, dqkv_ref, out_ref):
+    rows = h1_ref.shape[1] // out_ref.shape[0]
+    for at in range(steps):
+
+        @pl.when(pl.program_id(0) == at)
+        def _():
+            values = dot_tn(h1_ref[...], dqkv_ref[...])
+            put_chunks(out_ref, values, 0, at * (dqkv_ref.shape[1] // LANES) * rows, rows)
+
+
+def place_kernel(counts, rows, meta_ref, *refs):
+    out_ref = refs[-1]
+    total = sum(counts)
+    half_rows = out_ref.shape[0] // 2
+    along = refs[0].shape[1]
+    for half in range(2):
+        base = half_rows * (meta_ref[0] if half == 0 else 1 - meta_ref[0])
+        for at in range(total):
+            piece = refs[half * total + at]
+            first = at < counts[0]
+            col = 0 if first else refs[half * total].shape[2] // rows
+            for inner in range(piece.shape[0]):
+                x, y = (at, inner) if first else (inner, at - counts[0])
+                row = (meta_ref[1] ^ x) * counts[1] + (meta_ref[2] ^ y)
+                for last in range(along):
+                    chip = row * along + (meta_ref[3] ^ last)
+                    where = pl.ds(pl.multiple_of(base + chip * rows, rows), rows)
+                    for strip in range(piece.shape[2] // rows):
+                        out_ref[where, (col + strip) * LANES : (col + strip + 1) * LANES] = piece[
+                            inner, last, strip * rows : (strip + 1) * rows, :
+                        ]
+
+
+def unpack_kernel(packed_ref, *out_refs):
+    row = 0
+    block = packed_ref.shape[0]
+    for out_ref in out_refs:
+        rows = out_ref.shape[0] // block
+        for strip in range(out_ref.shape[1] // LANES):
+            for chunk in range(block):
+                out_ref[chunk * rows : (chunk + 1) * rows, strip * LANES : (strip + 1) * LANES] = packed_ref[
+                    chunk, row : row + rows, :
+                ]
+            row += rows
+
+
 def whole(shape):
     return pl.BlockSpec(shape, lambda *_: (0,) * len(shape))
 
@@ -329,48 +411,288 @@
     )
 
 
-def cost(flops, moved, exps=0):
-    return pl.CostEstimate(flops=int(flops), bytes_accessed=int(moved), transcendentals=int(exps))
-
-
 def shape(dims, kind):
     return jax.ShapeDtypeStruct(dims, kind)
 
 
-def flip(bit, count):
-    return [(i, i ^ (1 << bit)) for i in range(count)]
+def place_of():
+    place = 0
+    for axis in AXES:
+        place = place * lax.axis_size(axis) + lax.axis_index(axis)
+    return place
+
+
+def send(values, mask):
+    count = math.prod(lax.axis_size(axis) for axis in AXES)
+    return lax.ppermute(values, AXES, [(i, i ^ mask) for i in range(count)])
 
 
 def bit_of(bit):
-    place = lax.axis_index("dp") * lax.axis_size("seq") + lax.axis_index("seq")
-    return (place >> bit) & 1
+    return (place_of() >> bit) & 1
 
 
 def swap_with(values, bit):
-    return lax.ppermute(values, AXES, flip(bit, lax.axis_size("dp") * lax.axis_size("seq")))
-
-
-def scan_blocks(values, bits, split, reverse):
-    if not bits:
-        return jnp.zeros_like(values)
+    return send(values, 1 << bit)
+
+
+def axis_bits(axis):
+    at = 0
+    for other in reversed(AXES):
+        size = lax.axis_size(other).bit_length() - 1
+        if other == axis:
+            return list(range(at, at + size))
+        at += size
+
+
+def value_of(bits):
+    place = place_of()
+    return sum(((place >> b) & 1) << i for i, b in enumerate(bits))
+
+
+def mask_of(bits, value):
+    return sum(((value >> i) & 1) << b for i, b in enumerate(bits))
+
+
+def place_pieces(own, meta, dims):
+    both = own[0] + own[1] + own[2]
+    chips = len(own[0]) * len(own[1]) * own[0][0].shape[1]
+    return pl.pallas_call(
+        functools.partial(place_kernel, (len(own[0]), len(own[1])), dims[0] // 2 // chips),
+        in_specs=[pl.BlockSpec(memory_space=pltpu.SMEM)] + [pl.BlockSpec(memory_space=pltpu.VMEM)] * len(both),
+        out_specs=pl.BlockSpec(memory_space=pltpu.VMEM),
+        out_shape=shape(dims, F32),
+        compiler_params=pltpu.CompilerParams(vmem_limit_bytes=VMEM),
+        name="place",
+    )(meta, *both)
+
+
+def scan_stream(values, bits, split, reverse):
     bit = bits[0]
     mine = bit_of(bit)
     far = (mine == 0) if reverse else (mine == 1)
     if split:
         half = values.shape[0] // 2
-        got = swap_with(lax.dynamic_slice_in_dim(values, (1 - mine) * half, half, 0), bit)
         kept = lax.dynamic_slice_in_dim(values, mine * half, half, 0)
-        before = scan_blocks(kept + got, bits[1:], split - 1, reverse)
+        (got,) = yield [(lax.dynamic_slice_in_dim(values, (1 - mine) * half, half, 0), 1 << bit)]
+        before = yield from scan_stream(kept + got, bits[1:], split - 1, reverse)
         ours = before + jnp.where(far, got, 0.0)
-        theirs = swap_with(before + jnp.where(far, 0.0, kept), bit)
+        (theirs,) = yield [(before + jnp.where(far, 0.0, kept), 1 << bit)]
         return jnp.concatenate(
             [jnp.where(mine == 0, ours, theirs), jnp.where(mine == 0, theirs, ours)], axis=0
         )
-    got = swap_with(values, bit)
+    (got,) = yield [(values, 1 << bit)]
     part = jnp.where(far, got, 0.0)
     if len(bits) == 1:
         return part
-    return part + scan_blocks(values + got, bits[1:], 0, reverse)
+    rest = yield from scan_stream(values + got, bits[1:], 0, reverse)
+    return part + rest
+
+
+def chunks(parts, axis, bits, rows=None):
+    mine = value_of(bits)
+    out = []
+    for value in range(1 << len(bits)):
+        cut = []
+        for part in parts:
+            start, size = [0] * part.ndim, list(part.shape)
+            start[axis], size[axis] = mine ^ value, 1
+            if rows:
+                start[-2], size[-2] = rows
+            cut.append(lax.dynamic_slice(part, start, size))
+        out.append(jnp.squeeze(add_all(cut), axis))
+    return out
+
+
+def add_all(items):
+    return functools.reduce(jnp.add, items)
+
+
+def to_partners(items, bits):
+    return [(item, mask_of(bits, value + 1)) for value, item in enumerate(items)]
+
+
+def to_all(item, bits):
+    return to_partners([item] * ((1 << len(bits)) - 1), bits)
+
+
+def scatter_stream(theirs, mine):
+    x, y, z = axis_bits("x"), axis_bits("y"), axis_bits("z")
+    (got,) = yield [(theirs, 1)]
+    parts = [
+        item.reshape(1 << len(x), 1 << len(y), 1 << len(z), *item.shape[1:]) for item in (mine()[0], got)
+    ]
+    cut = theirs.shape[1] // 2
+    a, b = chunks(parts, 0, x, (0, cut)), chunks(parts, 1, y, (cut, cut))
+    got = yield to_partners(a[1:], x) + to_partners(b[1:], y)
+    a = chunks(a[:1] + got[: len(a) - 1], 0, y)
+    b = chunks(b[:1] + got[-(len(b) - 1) :], 0, x)
+    got = yield to_partners(a[1:], y) + to_partners(b[1:], x)
+    parts = [a[:1] + got[: len(a) - 1], b[:1] + got[-(len(b) - 1) :]]
+    both = jnp.concatenate([add_all(part) for part in parts], axis=1)
+    both = chunks([both], 0, z)
+    got = yield to_partners(both[1:], z)
+    return add_all(both[:1] + got)
+
+
+def bucket_stream(theirs, mine):
+    x, y, z = axis_bits("x"), axis_bits("y"), axis_bits("z")
+    chunk = yield from scatter_stream(theirs, mine)
+    got = yield to_all(chunk, z)
+    cut = chunk.shape[0] // 2
+    a, b = [jnp.stack([item[at : at + cut] for item in [chunk] + got]) for at in (0, cut)]
+    got = yield to_all(a, y) + to_all(b, x)
+    count = (1 << len(y)) - 1
+    a, b = jnp.stack([a] + got[:count]), jnp.stack([b] + got[count:])
+    got = yield to_all(a, x) + to_all(b, y)
+    count = (1 << len(x)) - 1
+    a, b = [a] + got[:count], [b] + got[count:]
+    got = yield [(item, 1) for item in a + b]
+    return a, b, got
+
+
+def small_stream(values, bits):
+    for bit in bits:
+        (got,) = yield [(values, 1 << bit)]
+        values = values + got
+    return values
+
+
+class Stream:
+    def __init__(self, chain):
+        self.chain, self.value, self.flying = chain, None, None
+        self.pending = next(chain)
+
+    def feed(self, got):
+        self.flying = None
+        try:
+            self.pending = self.chain.send(got)
+        except StopIteration as end:
+            self.pending, self.value = None, end.value
+
+
+def phase(start=(), wait=(), work=None, inputs=()):
+    ready = [[item for item, _ in stream.pending] for stream in start]
+    ready, inputs = lax.optimization_barrier((ready, tuple(inputs)))
+    for stream, items in zip(start, ready):
+        stream.flying = [send(item, mask) for item, (_, mask) in zip(items, stream.pending)]
+    done = tuple(work(*inputs)) if work else ()
+    got, done = lax.optimization_barrier(([stream.flying for stream in wait], done))
+    for stream, items in zip(wait, got):
+        stream.feed(list(items))
+    return done
+
+
+def of_stages(stream, wait_too=()):
+    while stream.pending is not None:
+        phase([stream], [stream])
+    return stream.value
+
+
+def ffn_grads(half, chips, hid, dy, h2, dup, att, dy1):
+    rows, width = dy.shape
+    hidden = hid.shape[1]
+    downs, ups = hidden // 2 // width, hidden // width
+    packed = (hidden // 2 * width + width // 2 * hidden + width // 2 * width) // chips // LANES
+    item = lambda w, index: pl.BlockSpec((rows, w), lambda j, h: (0, index(j, h[0])))
+    return pl.pallas_call(
+        functools.partial(ffn_grads_kernel, downs, ups),
+        grid_spec=pltpu.PrefetchScalarGridSpec(
+            num_scalar_prefetch=1,
+            grid=(downs + ups + 1,),
+            in_specs=[
+                item(width, lambda j, h: h * downs + jnp.minimum(j, downs - 1)),
+                item(width, lambda j, h: 0),
+                item(width // 2, lambda j, h: h),
+                item(width, lambda j, h: jnp.clip(j - downs, 0, ups - 1)),
+                item(width // 2, lambda j, h: h),
+                item(width, lambda j, h: 0),
+            ],
+            out_specs=pl.BlockSpec((chips, packed, LANES), lambda j, h: (0, 0, 0)),
+        ),
+        out_shape=shape((chips, packed, LANES), F32),
+        compiler_params=params(1),
+        name="ffn_grads",
+    )(half.astype(jnp.int32).reshape(1), hid, dy, h2, dup, att, dy1)
+
+
+def qkv_grads(half, chips, h1, dqkv):
+    rows, width = h1.shape
+    steps = dqkv.shape[1] // width
+    packed = width // 2 * dqkv.shape[1] // chips // LANES
+    return pl.pallas_call(
+        functools.partial(qkv_grads_kernel, steps),
+        grid_spec=pltpu.PrefetchScalarGridSpec(
+            num_scalar_prefetch=1,
+            grid=(steps,),
+            in_specs=[
+                pl.BlockSpec((rows, width // 2), lambda j, h: (0, h[0])),
+                pl.BlockSpec((rows, width), lambda j, h: (0, j)),
+            ],
+            out_specs=pl.BlockSpec((chips, packed, LANES), lambda j, h: (0, 0, 0)),
+        ),
+        out_shape=shape((chips, packed, LANES), F32),
+        compiler_params=params(1),
+        name="qkv_grads",
+    )(half.astype(jnp.int32).reshape(1), h1, dqkv)
+
+
+def unpack(packed, hidden, width):
+    devices = packed.shape[0]
+    block = 4
+    dims = [(hidden, width), (width, hidden), (width, width)]
+    return pl.pallas_call(
+        unpack_kernel,
+        grid=(devices // block,),
+        in_specs=[pl.BlockSpec((block,) + packed.shape[1:], lambda t: (t, 0, 0))],
+        out_specs=[pl.BlockSpec((rows * block // devices, columns), lambda t: (t, 0)) for rows, columns in dims],
+        out_shape=[shape(item, F32) for item in dims],
+        compiler_params=params(1),
+        name="unpack",
+    )(packed)
+
+
+def seq_block(seq, span, width, at=0):
+    return pl.BlockSpec((1, span, width), lambda p: (seq, 0, at + p))
+
+
+def run_local(seq, qkv, phi_k, tab_in, *old):
+    seqs, span, _ = qkv.shape
+    block = functools.partial(seq_block, seq, span)
+    return pl.pallas_call(
+        local_kernel,
+        grid=(PAIRS,),
+        in_specs=[block(LANES), block(LANES, 2 * PAIRS), block(2 * FEATS), whole((2, FEATS, 2 * LANES))]
+        + [pl.BlockSpec(memory_space=pl.ANY)] * len(old),
+        out_specs=[block(2 * FEATS), block(2 * LANES)],
+        out_shape=[shape((seqs, span, HEADS * FEATS), BF), shape((seqs, span, HEADS * LANES), F32)],
+        input_output_aliases={4 + i: i for i in range(len(old))},
+        compiler_params=params(1),
+        name="local",
+    )(qkv, qkv, phi_k, tab_in, *old)
+
+
+def run_scores(seq, qkv, phi_q, phi_k, dnum, before, tab_back, *old):
+    seqs, span, third = qkv.shape
+    block = functools.partial(seq_block, seq, span)
+    return pl.pallas_call(
+        score_back_kernel,
+        grid=(PAIRS,),
+        in_specs=[
+            block(LANES), block(LANES, 2 * PAIRS), block(2 * FEATS), block(2 * FEATS), block(2 * LANES),
+            pl.BlockSpec((1, LANES, FEATS), lambda p: (seq, p, 0)),
+            pl.BlockSpec((1, HEADS, FEATS), lambda p: (seq, STATE_ROWS // HEADS, 0)),
+            whole((2, FEATS, LANES)),
+        ]
+        + [pl.BlockSpec(memory_space=pl.ANY)] * len(old),
+        out_specs=[block(LANES), block(2 * FEATS), block(LANES)],
+        out_shape=[
+            shape((seqs, span, third // 3), BF), shape((seqs, span, HEADS * FEATS), F32),
+            shape((seqs, span, third // 3), F32),
+        ],
+        input_output_aliases={8 + i: i for i in range(len(old))},
+        compiler_params=params(1),
+        name="scores",
+    )(qkv, qkv, phi_q, phi_k, dnum, before, before, tab_back, *old)
 
 
 def shards(
@@ -389,7 +711,7 @@
     one = jnp.ones_like(table)
     tab_back = jnp.stack([jnp.concatenate([table, one], axis=1), jnp.concatenate([one, table], axis=1)])
     row = lambda a: a.reshape(1, -1)
-    seq_bits = list(range(lax.axis_size("seq").bit_length() - 1))
+    seq_bits = axis_bits("c") + axis_bits("y") + axis_bits("z")
 
     three = lambda d: pl.BlockSpec((1,) + d, lambda s: (s, 0, 0))
     h1, qkv, phi_k, state = pl.pallas_call(
@@ -407,25 +729,17 @@
             shape((seqs, span, HEADS * FEATS), BF), shape((seqs, SCAN_ROWS, FEATS), F32),
         ],
         compiler_params=params(1),
-        cost_estimate=cost(5e9, 12e6, 2e6),
         name="keys",
     )(tokens, row(gain_attn), row(shift_attn), w_qkv, row(b_qkv), tab_in)
 
-    before = scan_blocks(state.reshape(seqs * SCAN_ROWS, FEATS), seq_bits, 2, False).reshape(
-        seqs, SCAN_ROWS, FEATS
-    )
-
-    block = lambda w, at=0: pl.BlockSpec((1, span, w), lambda s, p: (s, 0, at + p))
-    phi_q, num = pl.pallas_call(
-        local_kernel,
-        grid=(seqs, PAIRS),
-        in_specs=[block(LANES), block(LANES, 2 * PAIRS), block(2 * FEATS), whole((2, FEATS, 2 * LANES))],
-        out_specs=[block(2 * FEATS), block(2 * LANES)],
-        out_shape=[shape((seqs, span, HEADS * FEATS), BF), shape((seqs, span, HEADS * LANES), F32)],
-        compiler_params=params(2),
-        cost_estimate=cost(8e9, 16e6, 2e6),
-        name="local",
-    )(qkv, qkv, phi_k, tab_in)
+    scan = Stream(scan_stream(state.reshape(seqs * SCAN_ROWS, FEATS), seq_bits, 2, False))
+    phase([scan], [scan])
+    local = None
+    for seq in range(seqs):
+        work = lambda qkv, phi_k, *old: run_local(seq, qkv, phi_k, tab_in, *old)
+        local = phase([scan], [scan], work, (qkv, phi_k) + tuple(local or ()))
+    phi_q, num = local
+    before = of_stages(scan).reshape(seqs, SCAN_ROWS, FEATS)
 
     per = span // TILE
     tile = lambda w: pl.BlockSpec((TILE, w), lambda t: (t, 0))
@@ -450,39 +764,41 @@
             shape((1, hidden), F32),
         ],
         compiler_params=params(1),
-        cost_estimate=cost(20e9, 40e6, 2e6),
         name="middle",
     )(
         flat(tokens), flat(cotangent), flat(num), flat(phi_q), before, w_out, row(b_out), row(gain_ffn),
         row(shift_ffn), w_up, row(b_up), w_down, row(b_down),
     )
 
-    later = scan_blocks(dstate.reshape(seqs * SCAN_ROWS, FEATS), seq_bits, 2, True).reshape(
-        seqs, SCAN_ROWS, FEATS
+    chips = lax.axis_size("x") * lax.axis_size("y") * lax.axis_size("z")
+    fits = width % (16 * chips) == 0
+    core = bit_of(0)
+    meta = jnp.stack([lax.axis_index(axis) for axis in ("c", "x", "y", "z")]).astype(jnp.int32)
+    scan = Stream(scan_stream(dstate.reshape(seqs * SCAN_ROWS, FEATS), seq_bits, 2, True))
+    run_back = lambda seq: lambda dnum, *old: run_scores(
+        seq, qkv, phi_q, phi_k, dnum.reshape(seqs, span, -1), before, tab_back, *old
     )
-    grad_w_down = dot_tn(hid, flat(cotangent))
-    grad_w_up = dot_tn(h2, dup)
-    grad_w_out = dot_tn(att, dy1_low)
-
-    dq, dphik, dv = pl.pallas_call(
-        score_back_kernel,
-        grid=(seqs, PAIRS),
-        in_specs=[
-            block(LANES), block(LANES, 2 * PAIRS), block(2 * FEATS), block(2 * FEATS), block(2 * LANES),
-            pl.BlockSpec((1, LANES, FEATS), lambda s, p: (s, p, 0)),
-            pl.BlockSpec((1, HEADS, FEATS), lambda s, p: (s, STATE_ROWS // HEADS, 0)),
-            whole((2, FEATS, LANES)),
-        ],
-        out_specs=[block(LANES), block(2 * FEATS), block(LANES)],
-        out_shape=[
-            shape((seqs, span, width), BF), shape((seqs, span, HEADS * FEATS), F32), shape((seqs, span, width), F32),
-        ],
-        compiler_params=params(2),
-        cost_estimate=cost(20e9, 30e6),
-        name="scores",
-    )(qkv, qkv, phi_q, phi_k, dnum.reshape(seqs, span, -1), before, before, tab_back)
-
-    dx, dkv, sums_attn, sum_qkv = pl.pallas_call(
+    if fits:
+        kept = []
+        args = (flat(cotangent), h2, dup, att, dy1_low)
+        some = lambda half: lambda hid: (ffn_grads(half, chips, hid, *args),)
+        (theirs,) = phase([scan], [scan], some(1 - core), (hid,))
+        ffn = Stream(scatter_stream(theirs, lambda: kept))
+        kept += phase([ffn, scan], [scan], some(core), (hid,))
+        phase((), [ffn])
+        old = phase([ffn, scan], [scan], run_back(0), (dnum,))
+        old = phase([scan], [scan, ffn], run_back(1), (dnum,) + tuple(old))
+        phase([ffn, scan], [ffn, scan])
+        phase([ffn, scan], [scan])
+        later = scan.value
+    else:
+        old = phase([scan], [scan], run_back(0), (dnum,))
+        old = phase([scan], [scan], run_back(1), (dnum,) + tuple(old))
+        later = of_stages(scan)
+    dq, dphik, dv = old
+    later = later.reshape(seqs, SCAN_ROWS, FEATS)
+
+    run_final = lambda dphik: pl.pallas_call(
         final_kernel,
         grid=(seqs,),
         in_specs=[
@@ -490,42 +806,66 @@
             three((span, width)), three((span, HEADS * FEATS)), three((span, width)), three((SCAN_ROWS, FEATS)),
             whole((2, FEATS, LANES)), whole((1, width)), whole((1, width)), whole((width, 3 * width)),
         ],
-        out_specs=[three((span, width)), three((span, 2 * width)), whole((8, width)), whole((1, 3 * width))],
+        out_specs=[three((span, width)), three((span, 3 * width)), whole((8, width)), whole((1, 3 * width))],
         out_shape=[
-            shape((seqs, span, width), BF), shape((seqs, span, 2 * width), BF), shape((8, width), F32),
+            shape((seqs, span, width), BF), shape((seqs, span, 3 * width), BF), shape((8, width), F32),
             shape((1, 3 * width), F32),
         ],
         compiler_params=params(1),
-        cost_estimate=cost(8e9, 20e6),
         name="final",
     )(
         tokens, dy1.reshape(seqs, span, width), qkv, phi_k, dq, dphik, dv, later, tab_back, row(gain_attn),
         row(shift_attn), w_qkv,
     )
-    grad_w_q = dot_tn(flat(h1), flat(dq))
-    grad_w_kv = dot_tn(flat(h1), flat(dkv))
-    return finish(
-        out.reshape(seqs, span, width), dx, grad_w_down, grad_w_up, grad_w_out, grad_w_q, grad_w_kv,
-        sums, sum_up, sums_attn, sum_qkv,
+    join = lambda sums_attn, sum_qkv: jnp.concatenate(
+        [sums[:4].reshape(-1), sum_up.reshape(-1), sums_attn[:2].reshape(-1), sum_qkv.reshape(-1)]
+    ).reshape(-1, LANES)
+    all_bits = [bit for axis in reversed(AXES) for bit in axis_bits(axis)]
+    if fits:
+        dx, dqkv, sums_attn, sum_qkv = phase((), [ffn], run_final, (dphik,))
+        chunk = ffn.value
+        packed = lax.all_gather(chunk, ("c", "x", "y", "z"))
+        wide = flat(dqkv)
+        some = lambda half: lambda wide: (qkv_grads(half, chips, flat(h1), wide),)
+        (theirs,) = some(1 - core)(wide)
+        more = []
+        qkv_sum = Stream(bucket_stream(theirs, lambda: more))
+        small = Stream(small_stream(join(sums_attn, sum_qkv), all_bits))
+        more += phase([qkv_sum, small], [small], some(core), (wide,))
+        phase((), [qkv_sum])
+        while qkv_sum.pending is not None or small.pending is not None:
+            both = [item for item in (qkv_sum, small) if item.pending is not None]
+            phase(both, both)
+        grad_w_qkv = place_pieces(qkv_sum.value, meta, (width, 3 * width))
+        small = small.value
+        grad_w_down, grad_w_up, grad_w_out = unpack(packed, hidden, width)
+    else:
+        dx, dqkv, sums_attn, sum_qkv = run_final(dphik)
+        grad_w_down, grad_w_up, grad_w_out, grad_w_qkv = lax.psum(
+            (
+                dot_tn(hid, flat(cotangent)), dot_tn(h2, dup), dot_tn(att, dy1_low),
+                dot_tn(flat(h1), flat(dqkv)),
+            ),
+            AXES,
+        )
+        small = of_stages(Stream(small_stream(join(sums_attn, sum_qkv), all_bits)))
+    small = small.reshape(-1)
+    cuts = [width * i for i in range(1, 5)]
+    cuts += [cuts[-1] + hidden, cuts[-1] + hidden + width, cuts[-1] + hidden + 2 * width]
+    b_down_g, b_out_g, gain_f, shift_f, b_up_g, gain_a, shift_a, b_qkv_g = jnp.split(small, cuts)
+    return (
+        out.reshape(seqs, span, width), dx, gain_a, shift_a, grad_w_qkv, b_qkv_g,
+        grad_w_out, b_out_g, gain_f, shift_f, grad_w_up, b_up_g, grad_w_down, b_down_g,
     )
 
 
-def finish(out, dx, grad_w_down, grad_w_up, grad_w_out, grad_w_q, grad_w_kv, sums, sum_up, sums_attn, sum_qkv):
-    total = lax.psum(
-        (grad_w_down, grad_w_up, grad_w_out, grad_w_q, grad_w_kv, sums, sum_up, sums_attn, sum_qkv), AXES
-    )
-    grad_w_down, grad_w_up, grad_w_out, grad_w_q, grad_w_kv, sums, sum_up, sums_attn, sum_qkv = total
-    return (
-        out, dx, sums_attn[0], sums_attn[1], jnp.concatenate([grad_w_q, grad_w_kv], axis=1), sum_qkv[0],
-        grad_w_out, sums[1], sums[2], sums[3], grad_w_up, sum_up[0], grad_w_down, sums[0],
-    )
-
-
 def solution(mesh):
-    split = P("dp", "seq", None)
+    dp, seq = mesh.shape["dp"], mesh.shape["seq"]
+    cut = jax.sharding.Mesh(mesh.devices.reshape(dp, 4, seq // 8, 2), AXES)
+    split = P("x", ("z", "y", "c"), None)
     return jax.shard_map(
         shards,
-        mesh=mesh,
+        mesh=cut,
         in_specs=(split, split) + (P(),) * 14,
         out_specs=(split, split) + (P(),) * 12,
         check_vma=False,

time: 443 us -> 336 us (0.76)
  waiting for transfers between devices: 244 us -> 96 us
  Pallas kernels: 85.3 us -> 133 us
  blocking collectives: 42.4 us -> 0 us
  starting transfers between devices: 11.8 us -> 53.9 us
  matrix products: 18.8 us -> 0 us
  other arithmetic: 11.4 us -> 26.5 us
    psum x1 -> x0, waiting for transfers between devices: 193 us -> none  [finish(): lax.psum((grad_w_down, grad_w_up, grad_w_out, grad_w_q, grad_w_kv, sums,...]
    pallas_call x2 -> x10, Pallas kernels: 34 us -> 81.3 us  [the longest x2 24.6 us: run_scores(): pl.pallas_call(score_back_kernel, grid=(PAIRS,), in_specs=[block(LANES),...]
    ppermute x12 -> x44, waiting for transfers between devices: 50.6 us -> 96 us  [send(): return lax.ppermute(values, AXES, [(i, i ^ mask) for i in range(count)])]
    psum x1 -> x0, blocking collectives: 42.4 us -> none  [finish(): lax.psum((grad_w_down, grad_w_up, grad_w_out, grad_w_q, grad_w_kv, sums,...]
    ppermute x12 -> x44, starting transfers between devices: 11.8 us -> 53.8 us  [send(): return lax.ppermute(values, AXES, [(i, i ^ mask) for i in range(count)])]
    dot_general x5 -> x0, matrix products: 18.8 us -> none  [dot_tn(): lax.dot_general(a, b, (((0,), (0,)), ((), ())), preferred_element_type=F32)]
    add x10 -> x24, other arithmetic: 3.4 us -> 14.7 us  [the longest x9 11.7 us: add_all(): return functools.reduce(jnp.add, items)]
    squeeze x0 -> x7, other arithmetic: none -> 5.84 us  [chunks(): out.append(jnp.squeeze(add_all(cut), axis))]
  transfers between devices with their start and end apart: 13 -> 45, of which waited for: 10 -> 22; matrix products, arithmetic and copies ran while one was open for 4% -> 3% of each run, Pallas kernels for 8% -> 26%
where the time goes in v2:
time: 336 us; the launch traced here: 334 us
  Pallas kernels  133 us (40%)
  waiting for transfers between devices  96 us (29%)
  starting transfers between devices  53.9 us (16%)
  other arithmetic  26.5 us (8%)
  between operations  15.2 us (5%)
  local copies, waits for them, and re-layouts  9.22 us (3%)
    ppermute x44, waiting for transfers between devices, send(): return lax.ppermute(values, AXES, [(i, i ^ mask) for i in range(count)])  96 us
    ppermute x44, starting transfers between devices, send(): return lax.ppermute(values, AXES, [(i, i ^ mask) for i in range(count)])  53.8 us
    pallas_call x1, Pallas kernels, shards(): pl.pallas_call(functools.partial(middle_kernel, per), grid=(seqs * per,),...  27.5 us
    pallas_call x2, Pallas kernels, run_scores(): pl.pallas_call(score_back_kernel, grid=(PAIRS,), in_specs=[block(LANES),...  24.6 us
    pallas_call x2, Pallas kernels, ffn_grads(): pl.pallas_call(functools.partial(ffn_grads_kernel, downs, ups), grid_spec...  20.6 us
    pallas_call x1, Pallas kernels, shards(): pl.pallas_call(final_kernel, grid=(seqs,), in_specs=[three((span, width))...  15.8 us
    pallas_call x2, Pallas kernels, run_local(): pl.pallas_call(local_kernel, grid=(PAIRS,), in_specs=[block(LANES), block...  13.1 us
    add x9, other arithmetic, add_all(): return functools.reduce(jnp.add, items)  11.7 us
  transfers between devices with their start and end apart: 45, of which 22 were waited for; matrix products, arithmetic and copies ran while one was open for 3% of the time, Pallas kernels for 26%

profile of v2, /device:TPU:13, one launch (start us, length us, event | category | flops | bytes accessed | tf_op | source)
XLA Modules:
  0.0 334.3 jit_solution(9826214387347268288)
XLA Ops:
  10.3 8.9 %keys.1 = (bf16[2,512,512]{2,1,0:T(8,128)(2,1)}, bf16[2,512,1536]{2,1,0:T(8,128)(2,1)}, bf16[2,512,2048]{2,1,0:T(8,128)(2,1)}, f32[2,528,256]{2,1,0:T(8,128)}) custom-call(bf16[2,512,512]{2,1,0:T(8,128)(2,1)} %x_ref.3, f32[1,512]{1,0:T(1,128)} %bitcast.234, f32[1,512]{1,0:T(1,128)} %bitcast.236, bf16[512,1536]{1,0:T(8,128)(2,1)} %w_ref.3, ...), custom_call_target="tpu_custom_call" | custom-call | tf_op jit(solution)/shard_map/keys/pallas_call | solution.py:717
  23.1 6.6 %local.2 = (bf16[2,512,2048]{2,1,0:T(8,128)(2,1)}, f32[2,512,1024]{2,1,0:T(8,128)}) custom-call(bf16[2,512,1536]{2,1,0:T(8,128)(2,1)} %get-tuple-element.166.q_ref.v_ref.qkv_ref, bf16[2,512,1536]{2,1,0:T(8,128)(2,1)} %get-tuple-element.166.q_ref.v_ref.qkv_ref, bf16[2,512,2048]{2,1,0:T(8,128)(2,1)} %get-tuple-element.167.phik_ref, ...), custom_call_target="tpu_custom_call" | custom-call | tf_op jit(solution)/shard_map/local/pallas_call | solution.py:661
  30.8 6.6 %local.3 = (bf16[2,512,2048]{2,1,0:T(8,128)(2,1)}, f32[2,512,1024]{2,1,0:T(8,128)}) custom-call(bf16[2,512,1536]{2,1,0:T(8,128)(2,1)} %get-tuple-element.166.q_ref.v_ref.qkv_ref, bf16[2,512,1536]{2,1,0:T(8,128)(2,1)} %get-tuple-element.166.q_ref.v_ref.qkv_ref, ...), custom_call_target="tpu_custom_call", output_to_operand_aliasing={{0}: (4, {}), {1}: (5, {})} | custom-call | tf_op jit(solution)/shard_map/local/pallas_call | solution.py:661
  37.4 2.4 collective-permute-start.3
  39.8 10.9 %collective-permute-done.3 = f32[264,256]{1,0:T(8,128)S(1)} collective-permute-done((f32[264,256]{1,0:T(8,128)S(1)}, f32[264,256]{1,0:T(8,128)S(1)}, u32[]{:S(2)}, u32[]{:S(2)}) %collective-permute-start.3) | collective-permute-done | bytes 270368 | tf_op jit(solution)/shard_map/ppermute | solution.py:427
  51.6 5.7 %collective-permute-done.4 = f32[264,256]{1,0:T(8,128)S(1)} collective-permute-done((f32[264,256]{1,0:T(8,128)S(1)}, f32[264,256]{1,0:T(8,128)S(1)}, u32[]{:S(2)}, u32[]{:S(2)}) %collective-permute-start.4) | collective-permute-done | bytes 270368 | tf_op jit(solution)/shard_map/ppermute | solution.py:427
  57.5 2.5 collective-permute-start.5
  62.8 27.5 %middle.1 = (bf16[1024,512]{1,0:T(8,128)(2,1)}, bf16[1024,2048]{1,0:T(8,128)(2,1)}, bf16[1024,2048]{1,0:T(8,128)(2,1)}, bf16[1024,512]{1,0:T(8,128)(2,1)}, bf16[...) custom-call(bf16[1024,512]{1,0:T(8,128)(2,1)} %bitcast.200, ...), custom_call_target="tpu_custom_call" | custom-call | tf_op jit(solution)/shard_map/middle/pallas_call | solution.py:748
  91.9 10.4 %ffn_grads.2 = f32[16,576,128]{2,1,0:T(8,128)} custom-call(s32[1]{0:T(128)} %bitcast.19.half_ref, bf16[1024,2048]{1,0:T(8,128)(2,1)} %get-tuple-element.187.hid_ref, bf16[1024,512]{1,0:T(8,128)(2,1)} %bitcast.198, bf16[1024,512]{1,0:T(8,128)(2,1)} %get-tuple-element.180.h2_ref, bf16[1024,2048]{1,0:T(8,128)(2,1)} %get-tuple-element.181.dup_ref, ...), custom_call_target="tpu_custom_call" | custom-call | tf_op jit(solution)/shard_map/ffn_grads/pallas_call | solution.py:597
  104.1 10.3 %ffn_grads.3 = f32[16,576,128]{2,1,0:T(8,128)} custom-call(s32[1]{0:T(128)} %bitcast.20.half_ref, bf16[1024,2048]{1,0:T(8,128)(2,1)} %get-tuple-element.187.hid_ref, bf16[1024,512]{1,0:T(8,128)(2,1)} %bitcast.199, bf16[1024,512]{1,0:T(8,128)(2,1)} %get-tuple-element.180.h2_ref, bf16[1024,2048]{1,0:T(8,128)(2,1)} %get-tuple-element.181.dup_ref, ...), custom_call_target="tpu_custom_call" | custom-call | tf_op jit(solution)/shard_map/ffn_grads/pallas_call | solution.py:597
  114.4 3.8 %dynamic-slice_add_fusion = (f32[2,1,4,288,128]{4,3,2,1,0:T(8,128)S(1)}, f32[2,4,288,128]{3,2,1,0:T(8,128)}) fusion(f32[2,2,4,576,128]{4,3,2,1,0:T(8,128)} %bitcast.22, s32[]{:T(128)S(6)} %select_n.214, f32[2,2,4,576,128]{4,3,2,1,0:T(8,128)} %bitcast.192, s32[]{:T(128)S(6)} %select_n.216), kind=kLoop, calls=%fused_computation.8 | loop fusion | flops 589824 | bytes 7077896 | tf_op jit(solution)/shard_map/add | solution.py:507
  118.5 3.0 dynamic-slice_add_fusion.1
  123.5 3.0 collective-permute-start.9
  127.3 12.3 %scores.2 = (bf16[2,512,512]{2,1,0:T(8,128)(2,1)}, f32[2,512,2048]{2,1,0:T(8,128)}, f32[2,512,512]{2,1,0:T(8,128)}) custom-call(bf16[2,512,1536]{2,1,0:T(8,128)(2,1)} %get-tuple-element.166.q_ref.v_ref.qkv_ref, bf16[2,512,1536]{2,1,0:T(8,128)(2,1)} %get-tuple-element.166.q_ref.v_ref.qkv_ref, bf16[2,512,2048]{2,1,0:T(8,128)(2,1)} %get-tuple-element.173.phiq_ref, ...), custom_call_target="tpu_custom_call" | custom-call | tf_op jit(solution)/shard_map/scores/pallas_call | solution.py:677
  140.4 12.3 %scores.3 = (bf16[2,512,512]{2,1,0:T(8,128)(2,1)}, f32[2,512,2048]{2,1,0:T(8,128)}, f32[2,512,512]{2,1,0:T(8,128)}) custom-call(bf16[2,512,1536]{2,1,0:T(8,128)(2,1)} %get-tuple-element.166.q_ref.v_ref.qkv_ref, bf16[2,512,1536]{2,1,0:T(8,128)(2,1)} %get-tuple-element.166.q_ref.v_ref.qkv_ref, ...), custom_call_target="tpu_custom_call", output_to_operand_aliasing={{0}: (8, {}), {1}: (9, {}), {2}: (10, {})} | custom-call | tf_op jit(solution)/shard_map/scores/pallas_call | solution.py:677
  159.3 17.8 %collective-permute-done.15 = f32[264,256]{1,0:T(8,128)} collective-permute-done((f32[264,256]{1,0:T(8,128)}, f32[264,256]{1,0:T(8,128)}, u32[]{:S(2)}, u32[]{:S(2)}) %collective-permute-start.15) | collective-permute-done | bytes 270368 | tf_op jit(solution)/shard_map/ppermute | solution.py:427
  182.5 2.3 collective-permute-start.19
  188.9 15.8 %final.1 = (bf16[2,512,512]{2,1,0:T(8,128)(2,1)}, bf16[2,512,1536]{2,1,0:T(8,128)(2,1)}, f32[8,512]{1,0:T(8,128)}, f32[1,1536]{1,0:T(1,128)}) custom-call(bf16[2,512,512]{2,1,0:T(8,128)(2,1)} %x_ref.3, f32[2,512,512]{2,1,0:T(8,128)} %bitcast.216, bf16[2,512,1536]{2,1,0:T(8,128)(2,1)} %get-tuple-element.166.q_ref.v_ref.qkv_ref, ...), custom_call_target="tpu_custom_call" | custom-call | tf_op jit(solution)/shard_map/final/pallas_call | solution.py:801
  204.8 9.0 %collective-permute-done.18 = f32[576,128]{1,0:T(8,128)S(1)} collective-permute-done((f32[576,128]{1,0:T(8,128)S(1)}, f32[576,128]{1,0:T(8,128)S(1)}, u32[]{:S(2)}, u32[]{:S(2)}) %collective-permute-start.18) | collective-permute-done | bytes 294944 | tf_op jit(solution)/shard_map/ppermute | solution.py:427
  215.4 4.7 %qkv_grads.2 = f32[16,192,128]{2,1,0:T(8,128)} custom-call(s32[1]{0:T(128)} %bitcast.19.half_ref, bf16[1024,512]{1,0:T(8,128)(2,1)} %bitcast.208, bf16[1024,1536]{1,0:T(8,128)(2,1)} %bitcast.195), custom_call_target="tpu_custom_call" | custom-call | tf_op jit(solution)/shard_map/qkv_grads/pallas_call | solution.py:622
  221.1 4.8 %qkv_grads.3 = f32[16,192,128]{2,1,0:T(8,128)} custom-call(s32[1]{0:T(128)} %bitcast.20.half_ref, bf16[1024,512]{1,0:T(8,128)(2,1)} %bitcast.209, bf16[1024,1536]{1,0:T(8,128)(2,1)} %bitcast.196), custom_call_target="tpu_custom_call" | custom-call | tf_op jit(solution)/shard_map/qkv_grads/pallas_call | solution.py:622
  231.0 8.0 %collective-permute-done.24 = f32[52,128]{1,0:T(8,128)S(1)} collective-permute-done((f32[52,128]{1,0:T(8,128)S(1)}, f32[52,128]{1,0:T(8,128)S(1)}, u32[]{:S(2)}, u32[]{:S(2)}) %collective-permute-start.24) | collective-permute-done | bytes 26656 | tf_op jit(solution)/shard_map/ppermute | solution.py:427
  241.0 3.5 %collective-permute-done.27 = f32[52,128]{1,0:T(8,128)S(1)} collective-permute-done((f32[52,128]{1,0:T(8,128)S(1)}, f32[52,128]{1,0:T(8,128)S(1)}, u32[]{:S(2)}, u32[]{:S(2)}) %collective-permute-start.27) | collective-permute-done | bytes 26656 | tf_op jit(solution)/shard_map/ppermute | solution.py:427
  250.3 10.6 %collective-permute-done.31 = f32[52,128]{1,0:T(8,128)S(1)} collective-permute-done((f32[52,128]{1,0:T(8,128)S(1)}, f32[52,128]{1,0:T(8,128)S(1)}, u32[]{:S(2)}, u32[]{:S(2)}) %collective-permute-start.31) | collective-permute-done | bytes 26656 | tf_op jit(solution)/shard_map/ppermute | solution.py:427
  264.4 4.2 %collective-permute-start.32 = (f32[192,128]{1,0:T(8,128)S(1)}, f32[192,128]{1,0:T(8,128)S(1)}, u32[]{:S(2)}, u32[]{:S(2)}) collective-permute-start(f32[192,128]{1,0:T(8,128)S(1)} %fusion.20), channel_id=1, source_target_pairs={{0,4},{1,5},{2,6},{3,7},{4,0},{5,1},{6,2},{7,3},{8,12},{9,13},{10,... | collective-permute-start | bytes 294920 | tf_op jit(solution)/shard_map/ppermute | solution.py:427
  270.6 3.4 %collective-permute-done.33 = f32[192,128]{1,0:T(8,128)S(1)} collective-permute-done((f32[192,128]{1,0:T(8,128)S(1)}, f32[192,128]{1,0:T(8,128)S(1)}, u32[]{:S(2)}, u32[]{:S(2)}) %collective-permute-start.33) | collective-permute-done | bytes 98336 | tf_op jit(solution)/shard_map/ppermute | solution.py:427
  274.4 9.2 %collective-permute-start.36 = (f32[4,96,128]{2,1,0:T(8,128)S(1)}, f32[4,96,128]{2,1,0:T(8,128)S(1)}, u32[]{:S(2)}, u32[]{:S(2)}) collective-permute-start(f32[4,96,128]{2,1,0:T(8,128)S(1)} %get-tuple-element.272), channel_id=1, source_target_pairs={{0,2},{1,3},{2,0},{3,1},{4,6},{5,7},{6,4},{7,5},{8,10},{9,11},{10,... | collective-permute-start | bytes 589832 | tf_op jit(solution)/shard_map/ppermute | solution.py:427
  283.5 7.6 %collective-permute-done.36 = f32[4,96,128]{2,1,0:T(8,128)S(1)} collective-permute-done((f32[4,96,128]{2,1,0:T(8,128)S(1)}, f32[4,96,128]{2,1,0:T(8,128)S(1)}, u32[]{:S(2)}, u32[]{:S(2)}) %collective-permute-start.36) | collective-permute-done | bytes 196640 | tf_op jit(solution)/shard_map/ppermute | solution.py:427
  294.2 7.7 %collective-permute-done.38.refs_1_ = f32[2,4,96,128]{3,2,1,0:T(8,128)S(1)} collective-permute-done((f32[2,4,96,128]{3,2,1,0:T(8,128)S(1)}, f32[2,4,96,128]{3,2,1,0:T(8,128)S(1)}, u32[]{:S(2)}, u32[]{:S(2)}) %collective-permute-start.38) | collective-permute-done | bytes 393248 | tf_op jit(solution)/shard_map/ppermute | solution.py:427
  301.9 8.1 %collective-permute-start.40 = (f32[2,4,96,128]{3,2,1,0:T(8,128)S(1)}, f32[2,4,96,128]{3,2,1,0:T(8,128)S(1)}, u32[]{:S(2)}, u32[]{:S(2)}) collective-permute-start(f32[2,4,96,128]{3,2,1,0:T(8,128)S(1)} %pad_maximum_fusion.4.refs_0_), channel_id=1, source_target_pairs={{0,1},{1,0},{2,3},{3,2},{4,5},{5,4},{6,7},{7,6},{8,9},{9,8},{10,11... | collective-permute-start | bytes 1179656 | tf_op jit(solution)/shard_map/ppermute | solution.py:427
  314.1 3.7 %place.1 = f32[512,1536]{1,0:T(8,128)} custom-call(s32[4]{0:T(128)} %pad_add_fusion.meta_ref, f32[2,4,96,128]{3,2,1,0:T(8,128)} %copy-done.12, f32[2,4,96,128]{3,2,1,0:T(8,128)} %copy-done.17, f32[2,4,96,128]{3,2,1,0:T(8,128)} %copy-done.13, f32[2,4,96,128]{3,2,1,0:T(8,128)} %copy-done.18, f32[2,4,96,128]{3,2,1,0:T(8,128)} %copy-done.19, ...), custom_call_target="tpu_custom_call" | custom-call | tf_op jit(solution)/shard_map/place/pallas_call | solution.py:459
  317.8 9.7 %unpack.1 = (f32[2048,512]{1,0:T(8,128)}, f32[512,2048]{1,0:T(8,128)}, f32[512,512]{1,0:T(8,128)}) custom-call(f32[32,576,128]{2,1,0:T(8,128)} %bitcast.201), custom_call_target="tpu_custom_call" | custom-call | tf_op jit(solution)/shard_map/unpack/pallas_call | solution.py:643
  (193 shorter events, 62.8 us)
Async XLA Ops:
  7.2 310.6 %all-gather.3.cloned.1.call-start = ((), (), s32[]{:S(2)}) async-start(), calls=%async_computation | async-start | bytes 9732096 | tf_op jit(solution)/shard_map/all_gather | solution.py:827
  22.8 7.8 %collective-permute-start.1 = (f32[264,256]{1,0:T(8,128)S(1)}, f32[264,256]{1,0:T(8,128)S(1)}, u32[]{:S(2)}, u32[]{:S(2)}) collective-permute-start(f32[264,256]{1,0:T(8,128)S(1)} %constant_dynamic-slice_fusion.2), channel_id=1, source_target_pairs={{0,2},{1,3},{2,0},{3,1},{4,6},{5,7},{6,4},{7,5},{8,10},{9,11},{10,... | collective-permute-start | bytes 811016 | tf_op jit(solution)/shard_map/ppermute | solution.py:427
  30.6 6.8 %collective-permute-start.2 = (f32[264,256]{1,0:T(8,128)S(1)}, f32[264,256]{1,0:T(8,128)S(1)}, u32[]{:S(2)}, u32[]{:S(2)}) collective-permute-start(f32[264,256]{1,0:T(8,128)S(1)} %dynamic-slice_add_fusion.7), channel_id=1, source_target_pairs={{0,4},{1,5},{2,6},{3,7},{4,0},{5,1},{6,2},{7,3},{8,12},{9,13},{10,... | collective-permute-start | bytes 811016 | tf_op jit(solution)/shard_map/ppermute | solution.py:427
  37.4 13.3 %collective-permute-start.3 = (f32[264,256]{1,0:T(8,128)S(1)}, f32[264,256]{1,0:T(8,128)S(1)}, u32[]{:S(2)}, u32[]{:S(2)}) collective-permute-start(f32[264,256]{1,0:T(8,128)S(1)} %add.149), channel_id=1, source_target_pairs={{0,8},{1,9},{2,10},{3,11},{4,12},{5,13},{6,14},{7,15},{8,0},{9,1},... | collective-permute-start | bytes 811016 | tf_op jit(solution)/shard_map/ppermute | solution.py:427
  50.8 6.5 %collective-permute-start.4 = (f32[264,256]{1,0:T(8,128)S(1)}, f32[264,256]{1,0:T(8,128)S(1)}, u32[]{:S(2)}, u32[]{:S(2)}) collective-permute-start(f32[264,256]{1,0:T(8,128)S(1)} %get-tuple-element.296), channel_id=1, source_target_pairs={{0,2},{1,3},{2,0},{3,1},{4,6},{5,7},{6,4},{7,5},{8,10},{9,11},{10,... | collective-permute-start | bytes 811016 | tf_op jit(solution)/shard_map/ppermute | solution.py:427
  91.4 10.8 %collective-permute-start.6 = (f32[528,256]{1,0:T(8,128)S(1)}, f32[528,256]{1,0:T(8,128)S(1)}, u32[]{:S(2)}, u32[]{:S(2)}) collective-permute-start(f32[528,256]{1,0:T(8,128)S(1)} %constant_dynamic-slice_fusion.1), channel_id=1, source_target_pairs={{0,1},{1,0},{2,3},{3,2},{4,5},{5,4},{6,7},{7,6},{8,9},{9,8},{10,11... | collective-permute-start | bytes 1622024 | tf_op jit(solution)/shard_map/ppermute | solution.py:427
  103.1 11.4 %collective-permute-start.8 = (f32[16,576,128]{2,1,0:T(8,128)}, f32[16,576,128]{2,1,0:T(8,128)}, u32[]{:S(2)}, u32[]{:S(2)}) collective-permute-start(f32[16,576,128]{2,1,0:T(8,128)} %ffn_grads.2), channel_id=1, source_target_pairs={{0,1},{1,0},{2,3},{3,2},{4,5},{5,4},{6,7},{7,6},{8,9},{9,8},{10,11... | collective-permute-start | bytes 14155784 | tf_op jit(solution)/shard_map/ppermute | solution.py:427
  103.4 11.0 %collective-permute-start.7 = (f32[264,256]{1,0:T(8,128)S(1)}, f32[264,256]{1,0:T(8,128)S(1)}, u32[]{:S(2)}, u32[]{:S(2)}) collective-permute-start(f32[264,256]{1,0:T(8,128)S(1)} %constant_dynamic-slice_fusion), channel_id=1, source_target_pairs={{0,2},{1,3},{2,0},{3,1},{4,6},{5,7},{6,4},{7,5},{8,10},{9,11},{10,... | collective-permute-start | bytes 811016 | tf_op jit(solution)/shard_map/ppermute | solution.py:427
  121.5 31.2 %collective-permute-start.11 = (f32[2,4,288,128]{3,2,1,0:T(8,128)}, f32[2,4,288,128]{3,2,1,0:T(8,128)}, u32[]{:S(2)}, u32[]{:S(2)}) collective-permute-start(f32[2,4,288,128]{3,2,1,0:T(8,128)} %get-tuple-element.202), channel_id=1, source_target_pairs={{0,16},{1,17},{2,18},{3,19},{4,20},{5,21},{6,22},{7,23},{8,24},{9,... | collective-permute-start | bytes 3538952 | tf_op jit(solution)/shard_map/ppermute | solution.py:427
  122.7 30.0 %collective-permute-start.12 = (f32[2,4,288,128]{3,2,1,0:T(8,128)}, f32[2,4,288,128]{3,2,1,0:T(8,128)}, u32[]{:S(2)}, u32[]{:S(2)}) collective-permute-start(f32[2,4,288,128]{3,2,1,0:T(8,128)} %get-tuple-element.203), channel_id=1, source_target_pairs={{0,2},{1,3},{2,0},{3,1},{4,6},{5,7},{6,4},{7,5},{8,10},{9,11},{10,... | collective-permute-start | bytes 3538952 | tf_op jit(solution)/shard_map/ppermute | solution.py:427
  123.5 16.1 %collective-permute-start.9 = (f32[264,256]{1,0:T(8,128)S(1)}, f32[264,256]{1,0:T(8,128)S(1)}, u32[]{:S(2)}, u32[]{:S(2)}) collective-permute-start(f32[264,256]{1,0:T(8,128)S(1)} %dynamic-slice_add_fusion.6), channel_id=1, source_target_pairs={{0,4},{1,5},{2,6},{3,7},{4,0},{5,1},{6,2},{7,3},{8,12},{9,13},{10,... | collective-permute-start | bytes 811016 | tf_op jit(solution)/shard_map/ppermute | solution.py:427
  140.4 12.4 %collective-permute-start.10 = (f32[264,256]{1,0:T(8,128)}, f32[264,256]{1,0:T(8,128)S(1)}, u32[]{:S(2)}, u32[]{:S(2)}) collective-permute-start(f32[264,256]{1,0:T(8,128)} %add.318), channel_id=1, source_target_pairs={{0,8},{1,9},{2,10},{3,11},{4,12},{5,13},{6,14},{7,15},{8,0},{9,1},... | collective-permute-start | bytes 811016 | tf_op jit(solution)/shard_map/ppermute | solution.py:427
  157.6 19.5 %collective-permute-start.13 = (f32[4,288,128]{2,1,0:T(8,128)}, f32[4,288,128]{2,1,0:T(8,128)}, u32[]{:S(2)}, u32[]{:S(2)}) collective-permute-start(f32[4,288,128]{2,1,0:T(8,128)} %fusion.1), channel_id=1, source_target_pairs={{0,2},{1,3},{2,0},{3,1},{4,6},{5,7},{6,4},{7,5},{8,10},{9,11},{10,... | collective-permute-start | bytes 1769480 | tf_op jit(solution)/shard_map/ppermute | solution.py:427
  158.3 18.8 %collective-permute-start.14 = (f32[4,288,128]{2,1,0:T(8,128)}, f32[4,288,128]{2,1,0:T(8,128)}, u32[]{:S(2)}, u32[]{:S(2)}) collective-permute-start(f32[4,288,128]{2,1,0:T(8,128)} %fusion), channel_id=1, source_target_pairs={{0,16},{1,17},{2,18},{3,19},{4,20},{5,21},{6,22},{7,23},{8,24},{9,... | collective-permute-start | bytes 1769480 | tf_op jit(solution)/shard_map/ppermute | solution.py:427
  158.5 18.5 %collective-permute-start.15 = (f32[264,256]{1,0:T(8,128)}, f32[264,256]{1,0:T(8,128)}, u32[]{:S(2)}, u32[]{:S(2)}) collective-permute-start(f32[264,256]{1,0:T(8,128)} %get-tuple-element.216), channel_id=1, source_target_pairs={{0,2},{1,3},{2,0},{3,1},{4,6},{5,7},{6,4},{7,5},{8,10},{9,11},{10,... | collective-permute-start | bytes 811016 | tf_op jit(solution)/shard_map/ppermute | solution.py:427
  184.8 19.9 %collective-permute-start.16 = (f32[576,128]{1,0:T(8,128)}, f32[576,128]{1,0:T(8,128)S(1)}, u32[]{:S(2)}, u32[]{:S(2)}) collective-permute-start(f32[576,128]{1,0:T(8,128)} %get-tuple-element.220), channel_id=1, source_target_pairs={{0,4},{1,5},{2,6},{3,7},{4,0},{5,1},{6,2},{7,3},{8,12},{9,13},{10,... | collective-permute-start | bytes 884744 | tf_op jit(solution)/shard_map/ppermute | solution.py:427
  186.5 18.3 %collective-permute-start.17 = (f32[576,128]{1,0:T(8,128)S(1)}, f32[576,128]{1,0:T(8,128)S(1)}, u32[]{:S(2)}, u32[]{:S(2)}) collective-permute-start(f32[576,128]{1,0:T(8,128)S(1)} %get-tuple-element.221), channel_id=1, source_target_pairs={{0,8},{1,9},{2,10},{3,11},{4,12},{5,13},{6,14},{7,15},{8,0},{9,1},... | collective-permute-start | bytes 884744 | tf_op jit(solution)/shard_map/ppermute | solution.py:427
  187.1 26.7 %collective-permute-start.18 = (f32[576,128]{1,0:T(8,128)S(1)}, f32[576,128]{1,0:T(8,128)S(1)}, u32[]{:S(2)}, u32[]{:S(2)}) collective-permute-start(f32[576,128]{1,0:T(8,128)S(1)} %get-tuple-element.222), channel_id=1, source_target_pairs={{0,12},{1,13},{2,14},{3,15},{4,8},{5,9},{6,10},{7,11},{8,4},{9,5},... | collective-permute-start | bytes 884744 | tf_op jit(solution)/shard_map/ppermute | solution.py:427
  228.2 10.8 %collective-permute-start.22 = (f32[2,4,96,128]{3,2,1,0:T(8,128)S(1)}, f32[2,4,96,128]{3,2,1,0:T(8,128)S(1)}, u32[]{:S(2)}, u32[]{:S(2)}) collective-permute-start(f32[2,4,96,128]{3,2,1,0:T(8,128)S(1)} %get-tuple-element.244), channel_id=1, source_target_pairs={{0,16},{1,17},{2,18},{3,19},{4,20},{5,21},{6,22},{7,23},{8,24},{9,... | collective-permute-start | bytes 1179656 | tf_op jit(solution)/shard_map/ppermute | solution.py:427
  228.5 10.5 %collective-permute-start.23 = (f32[2,4,96,128]{3,2,1,0:T(8,128)S(1)}, f32[2,4,96,128]{3,2,1,0:T(8,128)S(1)}, u32[]{:S(2)}, u32[]{:S(2)}) collective-permute-start(f32[2,4,96,128]{3,2,1,0:T(8,128)S(1)} %fusion.2), channel_id=1, source_target_pairs={{0,2},{1,3},{2,0},{3,1},{4,6},{5,7},{6,4},{7,5},{8,10},{9,11},{10,... | collective-permute-start | bytes 1179656 | tf_op jit(solution)/shard_map/ppermute | solution.py:427
  229.1 9.9 %collective-permute-start.24 = (f32[52,128]{1,0:T(8,128)S(1)}, f32[52,128]{1,0:T(8,128)S(1)}, u32[]{:S(2)}, u32[]{:S(2)}) collective-permute-start(f32[52,128]{1,0:T(8,128)S(1)} %fusion.27), channel_id=1, source_target_pairs={{0,2},{1,3},{2,0},{3,1},{4,6},{5,7},{6,4},{7,5},{8,10},{9,11},{10,... | collective-permute-start | bytes 79880 | tf_op jit(solution)/shard_map/ppermute | solution.py:427
  239.8 6.7 %collective-permute-start.26 = (f32[4,96,128]{2,1,0:T(8,128)S(1)}, f32[4,96,128]{2,1,0:T(8,128)S(1)}, u32[]{:S(2)}, u32[]{:S(2)}) collective-permute-start(f32[4,96,128]{2,1,0:T(8,128)S(1)} %fusion.14), channel_id=1, source_target_pairs={{0,16},{1,17},{2,18},{3,19},{4,20},{5,21},{6,22},{7,23},{8,24},{9,... | collective-permute-start | bytes 589832 | tf_op jit(solution)/shard_map/ppermute | solution.py:427
  246.7 14.2 %collective-permute-start.28 = (f32[192,128]{1,0:T(8,128)S(1)}, f32[192,128]{1,0:T(8,128)S(1)}, u32[]{:S(2)}, u32[]{:S(2)}) collective-permute-start(f32[192,128]{1,0:T(8,128)S(1)} %get-tuple-element.256), channel_id=1, source_target_pairs={{0,4},{1,5},{2,6},{3,7},{4,0},{5,1},{6,2},{7,3},{8,12},{9,13},{10,... | collective-permute-start | bytes 294920 | tf_op jit(solution)/shard_map/ppermute | solution.py:427
  246.7 14.1 %collective-permute-start.29 = (f32[192,128]{1,0:T(8,128)S(1)}, f32[192,128]{1,0:T(8,128)S(1)}, u32[]{:S(2)}, u32[]{:S(2)}) collective-permute-start(f32[192,128]{1,0:T(8,128)S(1)} %get-tuple-element.257), channel_id=1, source_target_pairs={{0,8},{1,9},{2,10},{3,11},{4,12},{5,13},{6,14},{7,15},{8,0},{9,1},... | collective-permute-start | bytes 294920 | tf_op jit(solution)/shard_map/ppermute | solution.py:427
  247.8 14.9 %collective-permute-start.30 = (f32[192,128]{1,0:T(8,128)S(1)}, f32[192,128]{1,0:T(8,128)S(1)}, u32[]{:S(2)}, u32[]{:S(2)}) collective-permute-start(f32[192,128]{1,0:T(8,128)S(1)} %get-tuple-element.258), channel_id=1, source_target_pairs={{0,12},{1,13},{2,14},{3,15},{4,8},{5,9},{6,10},{7,11},{8,4},{9,5},... | collective-permute-start | bytes 294920 | tf_op jit(solution)/shard_map/ppermute | solution.py:427
  249.4 11.5 %collective-permute-start.31 = (f32[52,128]{1,0:T(8,128)S(1)}, f32[52,128]{1,0:T(8,128)S(1)}, u32[]{:S(2)}, u32[]{:S(2)}) collective-permute-start(f32[52,128]{1,0:T(8,128)S(1)} %add.343), channel_id=1, source_target_pairs={{0,8},{1,9},{2,10},{3,11},{4,12},{5,13},{6,14},{7,15},{8,0},{9,1},... | collective-permute-start | bytes 79880 | tf_op jit(solution)/shard_map/ppermute | solution.py:427
  262.7 7.1 %collective-permute-start.35 = (f32[52,128]{1,0:T(8,128)S(1)}, f32[52,128]{1,0:T(8,128)S(1)}, u32[]{:S(2)}, u32[]{:S(2)}) collective-permute-start(f32[52,128]{1,0:T(8,128)S(1)} %add.348), channel_id=1, source_target_pairs={{0,16},{1,17},{2,18},{3,19},{4,20},{5,21},{6,22},{7,23},{8,24},{9,... | collective-permute-start | bytes 79880 | tf_op jit(solution)/shard_map/ppermute | solution.py:427
  274.4 16.8 %collective-permute-start.36 = (f32[4,96,128]{2,1,0:T(8,128)S(1)}, f32[4,96,128]{2,1,0:T(8,128)S(1)}, u32[]{:S(2)}, u32[]{:S(2)}) collective-permute-start(f32[4,96,128]{2,1,0:T(8,128)S(1)} %get-tuple-element.272), channel_id=1, source_target_pairs={{0,2},{1,3},{2,0},{3,1},{4,6},{5,7},{6,4},{7,5},{8,10},{9,11},{10,... | collective-permute-start | bytes 589832 | tf_op jit(solution)/shard_map/ppermute | solution.py:427
  283.5 9.1 %collective-permute-start.37 = (f32[4,96,128]{2,1,0:T(8,128)S(1)}, f32[4,96,128]{2,1,0:T(8,128)S(1)}, u32[]{:S(2)}, u32[]{:S(2)}) collective-permute-start(f32[4,96,128]{2,1,0:T(8,128)S(1)} %get-tuple-element.273), channel_id=1, source_target_pairs={{0,16},{1,17},{2,18},{3,19},{4,20},{5,21},{6,22},{7,23},{8,24},{9,... | collective-permute-start | bytes 589832 | tf_op jit(solution)/shard_map/ppermute | solution.py:427
  292.7 9.2 %collective-permute-start.38 = (f32[2,4,96,128]{3,2,1,0:T(8,128)S(1)}, f32[2,4,96,128]{3,2,1,0:T(8,128)S(1)}, u32[]{:S(2)}, u32[]{:S(2)}) collective-permute-start(f32[2,4,96,128]{3,2,1,0:T(8,128)S(1)} %pad_maximum_fusion.4.refs_0_), channel_id=1, source_target_pairs={{0,16},{1,17},{2,18},{3,19},{4,20},{5,21},{6,22},{7,23},{8,24},{9,... | collective-permute-start | bytes 1179656 | tf_op jit(solution)/shard_map/ppermute | solution.py:427
  292.8 9.1 %collective-permute-start.39 = (f32[2,4,96,128]{3,2,1,0:T(8,128)S(1)}, f32[2,4,96,128]{3,2,1,0:T(8,128)S(1)}, u32[]{:S(2)}, u32[]{:S(2)}) collective-permute-start(f32[2,4,96,128]{3,2,1,0:T(8,128)S(1)} %pad_maximum_fusion.5.refs_2_), channel_id=1, source_target_pairs={{0,2},{1,3},{2,0},{3,1},{4,6},{5,7},{6,4},{7,5},{8,10},{9,11},{10,... | collective-permute-start | bytes 1179656 | tf_op jit(solution)/shard_map/ppermute | solution.py:427
  301.9 9.9 %collective-permute-start.40 = (f32[2,4,96,128]{3,2,1,0:T(8,128)S(1)}, f32[2,4,96,128]{3,2,1,0:T(8,128)S(1)}, u32[]{:S(2)}, u32[]{:S(2)}) collective-permute-start(f32[2,4,96,128]{3,2,1,0:T(8,128)S(1)} %pad_maximum_fusion.4.refs_0_), channel_id=1, source_target_pairs={{0,1},{1,0},{2,3},{3,2},{4,5},{5,4},{6,7},{7,6},{8,9},{9,8},{10,11... | collective-permute-start | bytes 1179656 | tf_op jit(solution)/shard_map/ppermute | solution.py:427
  (39 other events, 223.5 us)
Sparse Core Ops, SparseCore 0:
  214.7 95.7 all-gather.2

commit v3 on v2

v3 whole, which is shorter than its diff:
```python
import functools
import math

import jax
import jax.numpy as jnp
from jax import lax
from jax.experimental import pallas as pl
from jax.experimental.pallas import tpu as pltpu
from jax.sharding import PartitionSpec as P

HEADS = 8
HEAD_DIM = 64
FEATS = 256
PAIRS = HEADS // 2
LANES = 2 * HEAD_DIM
AXES = ("x", "z", "y", "c")
BF = jnp.bfloat16
F32 = jnp.float32
Z_SCALE = HEAD_DIM ** (-0.25)
SQ_SCALE = 0.5 * HEAD_DIM ** (-0.5) / Z_SCALE
EXP_SCALE = Z_SCALE * math.log2(math.e)
EXP_SHIFT = 0.5 * math.log2(FEATS)
STATE_ROWS = PAIRS * LANES
SCAN_ROWS = STATE_ROWS + 32
TILE = 256
MID_TILE = 512
GELU_A = math.sqrt(2.0 / math.pi)
GELU_B = 0.044715
LIMITS = {
    "keys": 56, "local": 56, "middle": 60, "scores": 56, "final": 30, "qkv_grads": 16, "place": 16, "unpack": 16,
}


def dot(a, b):
    return lax.dot_general(a, b, (((1,), (0,)), ((), ())), preferred_element_type=F32)


def dot_nt(a, b):
    return lax.dot_general(a, b, (((1,), (1,)), ((), ())), preferred_element_type=F32)


def dot_tn(a, b):
    return lax.dot_general(a, b, (((0,), (0,)), ((), ())), preferred_element_type=F32)


def lower_half(shape):
    return lax.broadcasted_iota(jnp.int32, shape, 1) < HEAD_DIM


def swap_halves(values):
    return pltpu.roll(values, HEAD_DIM, 1)


def normalise(values):
    center = values - jnp.mean(values, axis=-1, keepdims=True)
    spread = jnp.mean(center * center, axis=-1, keepdims=True)
    scale = lax.rsqrt(spread + 1e-05)
    return center * scale, scale


def normalise_back(grad, unit, scale, gain):
    inner = grad * gain
    first = jnp.mean(inner, axis=-1, keepdims=True)
    second = jnp.mean(inner * unit, axis=-1, keepdims=True)
    return scale * (inner - first - unit * second)


def features(pair, tabs):
    wide = pair.astype(F32)
    square = wide * wide * SQ_SCALE
    high = square.astype(BF).astype(F32)
    low = swap_halves(square - high)
    keep = lower_half(wide.shape)
    even = jnp.where(keep, high, low).astype(BF)
    odd = jnp.where(keep, low, high).astype(BF)
    out = []
    for block, tab in ((even, tabs[0]), (odd, tabs[1])):
        proj = dot_nt(jnp.concatenate([pair, block], axis=1), tab)
        out.append(jnp.exp2(proj * EXP_SCALE - EXP_SHIFT).astype(BF))
    return out


def values_ones(pair):
    keep = lower_half(pair.shape)
    one = jnp.ones_like(pair)
    return jnp.where(keep, pair, one), jnp.where(keep, one, pair)


def causal_rows(first_row, rows, cols):
    return (
        lax.broadcasted_iota(jnp.int32, (rows, cols), 0) + first_row
        >= lax.broadcasted_iota(jnp.int32, (rows, cols), 1)
    )


def state_pair(state, norm, parity):
    wide = jnp.broadcast_to(norm, (HEAD_DIM, norm.shape[1]))
    return jnp.concatenate([state, wide] if parity == 0 else [wide, state], axis=0)


def kv_kernel(x_ref, gain_ref, shift_ref, w_ref, b_ref, tab_ref, h_ref, kv_ref, phik_ref, state_ref):
    width = x_ref.shape[-1]
    unit, _ = normalise(x_ref[0].astype(F32))
    low = (unit * gain_ref[...] + shift_ref[...]).astype(BF)
    h_ref[0] = low
    kv_ref[0] = (dot(low, w_ref[:, width:]) + b_ref[:, width:]).astype(BF)
    tabs = (tab_ref[0], tab_ref[1])
    norms = []
    for pair in range(PAIRS):
        key = kv_ref[0, :, pair * LANES : (pair + 1) * LANES]
        value = kv_ref[0, :, width + pair * LANES : width + (pair + 1) * LANES]
        phi = features(key, tabs)
        ones = values_ones(value)
        full = []
        for head in range(2):
            at = (2 * pair + head) * FEATS
            phik_ref[0, :, at : at + FEATS] = phi[head]
            full.append(dot_tn(ones[head], phi[head]))
        state_ref[0, pair * LANES : pair * LANES + HEAD_DIM, :] = full[0][:HEAD_DIM]
        state_ref[0, pair * LANES + HEAD_DIM : (pair + 1) * LANES, :] = full[1][HEAD_DIM:]
        norms += [full[0][HEAD_DIM : HEAD_DIM + 1], full[1][0:1]]
    state_ref[0, STATE_ROWS : STATE_ROWS + HEADS, :] = jnp.concatenate(norms, axis=0)
    state_ref[0, STATE_ROWS + HEADS :, :] = jnp.zeros((SCAN_ROWS - STATE_ROWS - HEADS, FEATS), F32)


def local_kernel(h_ref, w_ref, b_ref, v_ref, phik_ref, tab_ref, *rest):
    q_ref, phiq_ref, num_ref = rest[-3:]
    query = (dot(h_ref[0], w_ref[...]) + b_ref[...]).astype(BF)
    q_ref[0] = query
    phi = features(query, (tab_ref[0], tab_ref[1]))
    ones = values_ones(v_ref[0])
    span = h_ref.shape[1]
    for head in range(2):
        phiq_ref[0, :, head * FEATS : (head + 1) * FEATS] = phi[head]
        for row in range(0, span, TILE):
            cols = row + TILE
            keys = phik_ref[0, :cols, head * FEATS : (head + 1) * FEATS]
            scores = dot_nt(phi[head][row : row + TILE], keys)
            scores = jnp.where(causal_rows(row, TILE, cols), scores, 0.0).astype(BF)
            num_ref[0, row : row + TILE, head * LANES : (head + 1) * LANES] = dot(scores, ones[head][:cols])


def middle_kernel(
    per, chips, core_ref, x_ref, dy_ref, num_ref, phiq_ref, state_ref, w_out_ref, b_out_ref, gain_ref, shift_ref,
    w_up_ref, b_up_ref, w_down_ref, b_down_ref,
    out_ref, dy1_ref, dnum_ref, dstate_ref, sums_ref, sum_up_ref, *grads,
):
    down_ref, up_ref, wout_ref = grads[-3:]
    step = pl.program_id(0)
    width = x_ref.shape[-1]
    att_parts, den_parts = [], []
    for pair in range(PAIRS):
        nums = []
        for head in range(2):
            at = 2 * pair + head
            rows = pair * LANES + head * HEAD_DIM
            state = state_pair(
                state_ref[0, rows : rows + HEAD_DIM, :].astype(BF),
                state_ref[0, STATE_ROWS + at : STATE_ROWS + at + 1, :].astype(BF),
                head,
            )
            nums.append(
                num_ref[:, at * LANES : (at + 1) * LANES]
                + dot_nt(phiq_ref[:, at * FEATS : (at + 1) * FEATS], state)
            )
        keep = lower_half(nums[0].shape)
        den = swap_halves(jnp.where(keep, nums[1], nums[0]))
        recip = 1.0 / den
        att_parts.append(jnp.where(keep, nums[0], nums[1]) * recip)
        den_parts.append(recip)
    mixed = jnp.concatenate([part.astype(BF) for part in att_parts], axis=1)
    middle = x_ref[...].astype(F32) + dot(mixed, w_out_ref[...]) + b_out_ref[...]
    unit, scale = normalise(middle)
    low = (unit * gain_ref[...] + shift_ref[...]).astype(BF)
    grad_out = dy_ref[...]
    hidden = w_up_ref.shape[1]
    chunk = 1024
    result = middle + b_down_ref[...]
    grad_low = jnp.zeros(middle.shape, F32)

    @pl.when(step == 0)
    def _():
        sums_ref[...] = jnp.zeros_like(sums_ref)
        sum_up_ref[...] = jnp.zeros_like(sum_up_ref)

    for at in range(0, hidden, chunk):
        up = dot(low, w_up_ref[:, at : at + chunk]) + b_up_ref[:, at : at + chunk]
        square = up * up
        tanh = jnp.tanh(up * (GELU_A + GELU_A * GELU_B * square))
        half = 0.5 + 0.5 * tanh
        act = (up * half).astype(BF)
        add_to(down_ref, slice(at, at + chunk), slice(None), step, dot_tn(act, grad_out))
        slope = half + (0.5 * up) * (1.0 - tanh * tanh) * (GELU_A + 3.0 * GELU_A * GELU_B * square)
        result += dot(act, w_down_ref[at : at + chunk, :])
        dup = (dot_nt(grad_out, w_down_ref[at : at + chunk, :]) * slope).astype(BF)
        add_to(up_ref, slice(None), slice(at, at + chunk), step, dot_tn(low, dup))
        grad_low += dot_nt(dup, w_up_ref[:, at : at + chunk])
        sum_up_ref[:, at : at + chunk] += jnp.sum(dup.astype(F32), axis=0, keepdims=True)
    out_ref[...] = result.astype(BF)
    wide = grad_out.astype(F32)
    grad_mid = wide + normalise_back(grad_low, unit, scale, gain_ref[...])
    dy1_ref[...] = grad_mid
    grad_mid_low = grad_mid.astype(BF)
    add_to(wout_ref, slice(None), slice(None), step, dot_tn(mixed, grad_mid_low))
    for row, item in enumerate((wide, grad_mid, grad_low * unit, grad_low)):
        sums_ref[row : row + 1, :] += jnp.sum(item, axis=0, keepdims=True)
    grad_att = dot_nt(grad_mid_low, w_out_ref[...])

    @pl.when(lax.rem(step, per) == 0)
    def _():
        dstate_ref[...] = jnp.zeros_like(dstate_ref)

    for pair in range(PAIRS):
        grad = grad_att[:, pair * LANES : (pair + 1) * LANES] * den_parts[pair]
        keep = lower_half(grad.shape)
        prod = swap_halves(-(grad * att_parts[pair]))
        both = (jnp.where(keep, grad, prod).astype(BF), jnp.where(keep, prod, grad).astype(BF))
        for head in range(2):
            at = 2 * pair + head
            dnum_ref[:, at * LANES : (at + 1) * LANES] = both[head]
            full = dot_tn(both[head], phiq_ref[:, at * FEATS : (at + 1) * FEATS])
            rows = pair * LANES + head * HEAD_DIM
            main = full[:HEAD_DIM] if head == 0 else full[HEAD_DIM:]
            rest = full[HEAD_DIM:] if head == 0 else full[:HEAD_DIM]
            dstate_ref[0, rows : rows + HEAD_DIM, :] += main
            dstate_ref[0, STATE_ROWS + at : STATE_ROWS + at + 1, :] += jnp.sum(rest, axis=0, keepdims=True)

    if len(grads) > 3:

        @pl.when(step == pl.num_programs(0) - 1)
        def _():
            for half, packed_ref in ((1 - core_ref[0], grads[0]), (core_ref[0], grads[1])):
                pack_half(half, chips, packed_ref, down_ref, up_ref, wout_ref)


def add_to(total_ref, rows, cols, step, values):
    total_ref[rows, cols] = jnp.where(step == 0, 0.0, total_ref[rows, cols]) + values


def pack_half(half, chips, packed_ref, down_ref, up_ref, wout_ref):
    rows = down_ref.shape[0] // 2 // chips
    first = half * (down_ref.shape[0] // 2)
    for chip in range(chips):
        for strip in range(down_ref.shape[1] // LANES):
            packed_ref[chip, strip * rows : (strip + 1) * rows, :] = down_ref[
                pl.ds(pl.multiple_of(first + chip * rows, rows), rows), strip * LANES : (strip + 1) * LANES
            ]
    base = rows * (down_ref.shape[1] // LANES)
    for total_ref in (up_ref, wout_ref):
        rows = total_ref.shape[0] // chips
        strips = total_ref.shape[1] // 2 // LANES
        for strip in range(strips):
            col = pl.multiple_of((half * strips + strip) * LANES, LANES)
            for chip in range(chips):
                packed_ref[chip, base : base + rows, :] = total_ref[
                    chip * rows : (chip + 1) * rows, pl.ds(col, LANES)
                ]
            base += rows


def score_back_kernel(
    first, q_ref, v_ref, phiq_ref, phik_ref, dnum_ref, state_ref, norm_ref, tab_ref, *rest
):
    dq_ref, dphik_ref, dv_ref = rest[-3:]
    span = q_ref.shape[1]
    ones = values_ones(v_ref[0])
    back, dvs = [], []
    for head in range(2):
        phiq = phiq_ref[0, :, head * FEATS : (head + 1) * FEATS]
        phik = phik_ref[0, :, head * FEATS : (head + 1) * FEATS]
        dnum = dnum_ref[0, :, head * LANES : (head + 1) * LANES]
        state = state_pair(
            state_ref[0, head * HEAD_DIM : (head + 1) * HEAD_DIM, :].astype(BF),
            norm_ref[0, pl.ds(2 * (first + pl.program_id(0)) + head, 1), :].astype(BF),
            head,
        )
        grads = []
        for row in range(0, span, TILE):
            cols = row + TILE
            mine = dnum[row : row + TILE]
            grad = dot_nt(mine, ones[head][:cols])
            grad = jnp.where(causal_rows(row, TILE, cols), grad, 0.0).astype(BF)
            grad_phi = dot(mine, state) + dot(grad, phik[:cols])
            grads.append((grad_phi * phiq[row : row + TILE].astype(F32)).astype(BF))
        back.append(dot(jnp.concatenate(grads, axis=0), tab_ref[head]))
        dv = []
        for row in range(0, span, TILE):
            count = span - row
            seen = (
                lax.broadcasted_iota(jnp.int32, (TILE, count), 0)
                <= lax.broadcasted_iota(jnp.int32, (TILE, count), 1)
            )
            turned = dot_nt(ones[head][row : row + TILE], dnum[row:])
            turned = jnp.where(seen, turned, 0.0).astype(BF)
            dphik_ref[0, row : row + TILE, head * FEATS : (head + 1) * FEATS] = dot(turned, phiq[row:]).astype(BF)
            scores = dot_nt(phik[row : row + TILE], phiq[row:])
            scores = jnp.where(seen, scores, 0.0).astype(BF)
            dv.append(dot(scores, dnum[row:]))
        dvs.append(jnp.concatenate(dv, axis=0))
    keep = lower_half(dvs[0].shape)
    dv_ref[0] = jnp.where(keep, dvs[0], dvs[1])
    dq_ref[0] = finish_back(back, q_ref[0]).astype(BF)


def finish_back(back, pair):
    keep = lower_half(back[0].shape)
    main = jnp.where(keep, back[0], back[1])
    total = swap_halves(jnp.where(keep, back[1], back[0]))
    return main * Z_SCALE - total * pair.astype(F32) * (HEAD_DIM ** (-0.5))


def final_kernel(
    x_ref, dy1_ref, kv_ref, phik_ref, dq_ref, dphik_ref, dv_ref, later_ref, tab_ref, gain_ref, shift_ref, w_ref,
    *rest,
):
    dx_ref, dqkv_ref, sums_ref, sum_qkv_ref = rest[-4:]
    width = x_ref.shape[-1]
    grad = dot_nt(dq_ref[0], w_ref[:, :width])

    sums_ref[...] = jnp.zeros_like(sums_ref)
    for pair in range(PAIRS):
        key = kv_ref[0, :, pair * LANES : (pair + 1) * LANES]
        value = kv_ref[0, :, width + pair * LANES : width + (pair + 1) * LANES]
        ones = values_ones(value)
        back, dvs = [], []
        for head in range(2):
            at = 2 * pair + head
            rows = pair * LANES + head * HEAD_DIM
            state = later_ref[0, rows : rows + HEAD_DIM, :].astype(BF)
            norm = later_ref[0, STATE_ROWS + at : STATE_ROWS + at + 1, :]
            high = norm.astype(BF)
            low = (norm - high.astype(F32)).astype(BF)
            rest = jnp.concatenate(
                [high.astype(F32), low.astype(F32), jnp.zeros((HEAD_DIM - 2, FEATS), F32)], axis=0
            ).astype(BF)
            full = jnp.concatenate([state, rest] if head == 0 else [rest, state], axis=0)
            phik = phik_ref[0, :, at * FEATS : (at + 1) * FEATS]
            grad_phi = dphik_ref[0, :, at * FEATS : (at + 1) * FEATS].astype(F32) + dot(ones[head], full)
            inner = (grad_phi * phik.astype(F32)).astype(BF)
            back.append(dot(inner, tab_ref[head]))
            dvs.append(dot_nt(phik, full))
        keep = lower_half(dvs[0].shape)
        dk = finish_back(back, key).astype(BF)
        dv = (dv_ref[0, :, pair * LANES : (pair + 1) * LANES] + jnp.where(keep, dvs[0], dvs[1])).astype(BF)
        dqkv_ref[0, :, width + pair * LANES : width + (pair + 1) * LANES] = dk
        dqkv_ref[0, :, 2 * width + pair * LANES : 2 * width + (pair + 1) * LANES] = dv
    dqkv_ref[0, :, :width] = dq_ref[0]
    dkv = dqkv_ref[0, :, width:]
    grad += dot_nt(dkv, w_ref[:, width:])
    unit, scale = normalise(x_ref[0].astype(F32))
    dx_ref[0] = (dy1_ref[0] + normalise_back(grad, unit, scale, gain_ref[...])).astype(BF)
    sums_ref[0:1, :] = jnp.sum(grad * unit, axis=0, keepdims=True)
    sums_ref[1:2, :] = jnp.sum(grad, axis=0, keepdims=True)
    sum_qkv_ref[:, :width] = jnp.sum(dq_ref[0].astype(F32), axis=0, keepdims=True)
    sum_qkv_ref[:, width:] = jnp.sum(dkv.astype(F32), axis=0, keepdims=True)


def put_chunks(out_ref, values):
    chips = out_ref.shape[0]
    rows = values.shape[0] // chips
    for chunk in range(chips):
        for strip in range(values.shape[1] // LANES):
            out_ref[chunk, strip * rows : (strip + 1) * rows, :] = values[
                chunk * rows : (chunk + 1) * rows, strip * LANES : (strip + 1) * LANES
            ]


def qkv_grads_kernel(half_ref, h1_ref, dqkv_ref, out_ref):
    put_chunks(out_ref, dot_tn(h1_ref[...], dqkv_ref[...]))


def place_kernel(counts, rows, meta_ref, *refs):
    out_ref = refs[-1]
    total = sum(counts)
    along = refs[0].shape[1]
    for core in range(2):

        @pl.when(meta_ref[0] == core)
        def _():
            for half in range(2):
                base = out_ref.shape[1] // LANES // 2 * (half ^ core)
                for at in range(total):
                    piece = refs[half * total + at]
                    first = at < counts[0]
                    col = base if first else base + refs[half * total].shape[2] // rows
                    for inner in range(piece.shape[0]):
                        x, y = (at, inner) if first else (inner, at - counts[0])
                        row = (meta_ref[1] ^ x) * counts[1] + (meta_ref[2] ^ y)
                        for last in range(along):
                            chip = row * along + (meta_ref[3] ^ last)
                            where = pl.ds(pl.multiple_of(chip * rows, rows), rows)
                            for strip in range(piece.shape[2] // rows):
                                out_ref[where, (col + strip) * LANES : (col + strip + 1) * LANES] = piece[
                                    inner, last, strip * rows : (strip + 1) * rows, :
                                ]


def unpack_kernel(packed_ref, *out_refs):
    row = 0
    block = packed_ref.shape[0]
    for out_ref in out_refs:
        rows = out_ref.shape[0] // block
        for strip in range(out_ref.shape[1] // LANES):
            for chunk in range(block):
                out_ref[chunk * rows : (chunk + 1) * rows, strip * LANES : (strip + 1) * LANES] = packed_ref[
                    chunk, row : row + rows, :
                ]
            row += rows


def whole(shape):
    return pl.BlockSpec(shape, lambda *_: (0,) * len(shape))


def params(count, name):
    return pltpu.CompilerParams(
        dimension_semantics=("arbitrary",) * count if count else None, vmem_limit_bytes=LIMITS[name] * 1024 * 1024
    )


def shape(dims, kind):
    return jax.ShapeDtypeStruct(dims, kind)


def place_of():
    place = 0
    for axis in AXES:
        place = place * lax.axis_size(axis) + lax.axis_index(axis)
    return place


def send(values, mask):
    count = math.prod(lax.axis_size(axis) for axis in AXES)
    return lax.ppermute(values, AXES, [(i, i ^ mask) for i in range(count)])


def bit_of(bit):
    return (place_of() >> bit) & 1


def swap_with(values, bit):
    return send(values, 1 << bit)


def axis_bits(axis):
    at = 0
    for other in reversed(AXES):
        size = lax.axis_size(other).bit_length() - 1
        if other == axis:
            return list(range(at, at + size))
        at += size


def value_of(bits):
    place = place_of()
    return sum(((place >> b) & 1) << i for i, b in enumerate(bits))


def mask_of(bits, value):
    return sum(((value >> i) & 1) << b for i, b in enumerate(bits))


def place_pieces(own, meta, dims):
    both = own[0] + own[1] + own[2]
    chips = len(own[0]) * len(own[1]) * own[0][0].shape[1]
    return pl.pallas_call(
        functools.partial(place_kernel, (len(own[0]), len(own[1])), dims[0] // chips),
        in_specs=[pl.BlockSpec(memory_space=pltpu.SMEM)] + [pl.BlockSpec(memory_space=pltpu.VMEM)] * len(both),
        out_specs=pl.BlockSpec(memory_space=pltpu.VMEM),
        out_shape=shape(dims, F32),
        compiler_params=params(0, "place"),
        name="place",
    )(meta, *both)


def scan_stream(values, bits, split, reverse):
    bit = bits[0]
    mine = bit_of(bit)
    far = (mine == 0) if reverse else (mine == 1)
    if split:
        half = values.shape[0] // 2
        kept = lax.dynamic_slice_in_dim(values, mine * half, half, 0)
        (got,) = yield [(lax.dynamic_slice_in_dim(values, (1 - mine) * half, half, 0), 1 << bit)]
        before = yield from scan_stream(kept + got, bits[1:], split - 1, reverse)
        ours = before + jnp.where(far, got, 0.0)
        (theirs,) = yield [(before + jnp.where(far, 0.0, kept), 1 << bit)]
        return jnp.concatenate(
            [jnp.where(mine == 0, ours, theirs), jnp.where(mine == 0, theirs, ours)], axis=0
        )
    (got,) = yield [(values, 1 << bit)]
    part = jnp.where(far, got, 0.0)
    if len(bits) == 1:
        return part
    rest = yield from scan_stream(values + got, bits[1:], 0, reverse)
    return part + rest


def chunks(parts, axis, bits, rows=None):
    mine = value_of(bits)
    out = []
    for value in range(1 << len(bits)):
        cut = []
        for part in parts:
            start, size = [0] * part.ndim, list(part.shape)
            start[axis], size[axis] = mine ^ value, 1
            if rows:
                start[-2], size[-2] = rows
            cut.append(lax.dynamic_slice(part, start, size))
        out.append(jnp.squeeze(add_all(cut), axis))
    return out


def add_all(items):
    return functools.reduce(jnp.add, items)


def to_partners(items, bits):
    return [(item, mask_of(bits, value + 1)) for value, item in enumerate(items)]


def to_all(item, bits):
    return to_partners([item] * ((1 << len(bits)) - 1), bits)


def scatter_stream(theirs, mine):
    x, y, z = axis_bits("x"), axis_bits("y"), axis_bits("z")
    (got,) = yield [(theirs, 1)]
    parts = [mine() if callable(mine) else mine, got]
    cut = parts[0].shape[1] // 2
    parts = [item.reshape(1 << len(x), 1 << len(y), 1 << len(z), *item.shape[1:]) for item in parts]
    a, b = chunks(parts, 0, x, (0, cut)), chunks(parts, 1, y, (cut, cut))
    got = yield to_partners(a[1:], x) + to_partners(b[1:], y)
    a = chunks(a[:1] + got[: len(a) - 1], 0, y)
    b = chunks(b[:1] + got[-(len(b) - 1) :], 0, x)
    got = yield to_partners(a[1:], y) + to_partners(b[1:], x)
    parts = [a[:1] + got[: len(a) - 1], b[:1] + got[-(len(b) - 1) :]]
    both = jnp.concatenate([add_all(part) for part in parts], axis=1)
    both = chunks([both], 0, z)
    got = yield to_partners(both[1:], z)
    return add_all(both[:1] + got)


def bucket_stream(theirs, mine):
    x, y, z = axis_bits("x"), axis_bits("y"), axis_bits("z")
    chunk = yield from scatter_stream(theirs, mine)
    got = yield to_all(chunk, z)
    cut = chunk.shape[0] // 2
    a, b = [jnp.stack([item[at : at + cut] for item in [chunk] + got]) for at in (0, cut)]
    got = yield to_all(a, y) + to_all(b, x)
    count = (1 << len(y)) - 1
    a, b = jnp.stack([a] + got[:count]), jnp.stack([b] + got[count:])
    got = yield to_all(a, x) + to_all(b, y)
    count = (1 << len(x)) - 1
    a, b = [a] + got[:count], [b] + got[count:]
    got = yield [(item, 1) for item in a + b]
    return a, b, got


def small_stream(values, bits):
    for bit in bits:
        (got,) = yield [(values, 1 << bit)]
        values = values + got
    return values


class Stream:
    def __init__(self, chain):
        self.chain, self.value, self.flying = chain, None, None
        self.pending = next(chain)

    def feed(self, got):
        self.flying = None
        try:
            self.pending = self.chain.send(got)
        except StopIteration as end:
            self.pending, self.value = None, end.value


def phase(start=(), wait=(), work=None, inputs=()):
    ready = [[item for item, _ in stream.pending] for stream in start]
    ready, inputs = lax.optimization_barrier((ready, tuple(inputs)))
    for stream, items in zip(start, ready):
        stream.flying = [send(item, mask) for item, (_, mask) in zip(items, stream.pending)]
    done = tuple(work(*inputs)) if work else ()
    got, done = lax.optimization_barrier(([stream.flying for stream in wait], done))
    for stream, items in zip(wait, got):
        stream.feed(list(items))
    return done


def of_stages(stream, wait_too=()):
    while stream.pending is not None:
        phase([stream], [stream])
    return stream.value


def half_of(half):
    return half.astype(jnp.int32).reshape(1)


def qkv_grads(half, chips, h1, dqkv):
    rows, width = h1.shape
    block = 2 * LANES
    steps = dqkv.shape[1] // 2 // block
    own = width * block // chips // LANES
    return pl.pallas_call(
        qkv_grads_kernel,
        grid_spec=pltpu.PrefetchScalarGridSpec(
            num_scalar_prefetch=1,
            grid=(steps,),
            in_specs=[
                pl.BlockSpec((rows, width), lambda j, h: (0, 0)),
                pl.BlockSpec((rows, block), lambda j, h: (0, h[0] * steps + j)),
            ],
            out_specs=pl.BlockSpec((chips, own, LANES), lambda j, h: (0, j, 0)),
        ),
        out_shape=shape((chips, own * steps, LANES), F32),
        compiler_params=params(1, "qkv_grads"),
        name="qkv_grads",
    )(half_of(half), h1, dqkv)


def unpack(packed, hidden, width):
    devices = packed.shape[0]
    block = 4
    per = devices // 2 // block
    rows = width // (devices // 2) * block
    return pl.pallas_call(
        unpack_kernel,
        grid=(devices // block,),
        in_specs=[pl.BlockSpec((block,) + packed.shape[1:], lambda t: (t, 0, 0))],
        out_specs=[
            pl.BlockSpec((hidden * block // devices, width), lambda t: (t, 0)),
            pl.BlockSpec((rows, hidden // 2), lambda t: (t % per, t // per)),
            pl.BlockSpec((rows, width // 2), lambda t: (t % per, t // per)),
        ],
        out_shape=[shape((hidden, width), F32), shape((width, hidden), F32), shape((width, width), F32)],
        compiler_params=params(1, "unpack"),
        name="unpack",
    )(packed)


def seq_block(seq, span, width, at=0):
    return pl.BlockSpec((1, span, width), lambda p: (seq, 0, at + p))


def run_local(seq, h1, w_qkv, b_qkv, kv, phi_k, tab_in, *old):
    seqs, span, width = h1.shape
    block = functools.partial(seq_block, seq, span)
    return pl.pallas_call(
        local_kernel,
        grid=(PAIRS,),
        in_specs=[
            pl.BlockSpec((1, span, width), lambda p: (seq, 0, 0)), pl.BlockSpec((width, LANES), lambda p: (0, p)),
            pl.BlockSpec((1, LANES), lambda p: (0, p)), block(LANES, PAIRS), block(2 * FEATS),
            whole((2, FEATS, 2 * LANES)),
        ]
        + [pl.BlockSpec(memory_space=pl.ANY)] * len(old),
        out_specs=[block(LANES), block(2 * FEATS), block(2 * LANES)],
        out_shape=[
            shape((seqs, span, width), BF), shape((seqs, span, HEADS * FEATS), BF),
            shape((seqs, span, HEADS * LANES), F32),
        ],
        input_output_aliases={6 + i: i for i in range(len(old))},
        compiler_params=params(1, "local"),
        name="local",
    )(h1, w_qkv, b_qkv, kv, phi_k, tab_in, *old)


def run_scores(seq, first, count, q, kv, phi_q, phi_k, dnum, before, tab_back, *old):
    seqs, span, width = q.shape
    block = lambda w, at=0: seq_block(seq, span, w, at + first)
    return pl.pallas_call(
        functools.partial(score_back_kernel, first),
        grid=(count,),
        in_specs=[
            block(LANES), block(LANES, PAIRS), block(2 * FEATS), block(2 * FEATS), block(2 * LANES),
            pl.BlockSpec((1, LANES, FEATS), lambda p: (seq, first + p, 0)),
            pl.BlockSpec((1, HEADS, FEATS), lambda p: (seq, STATE_ROWS // HEADS, 0)),
            whole((2, FEATS, LANES)),
        ]
        + [pl.BlockSpec(memory_space=pl.ANY)] * len(old),
        out_specs=[block(LANES), block(2 * FEATS), block(LANES)],
        out_shape=[
            shape((seqs, span, width), BF), shape((seqs, span, HEADS * FEATS), BF),
            shape((seqs, span, width), F32),
        ],
        input_output_aliases={8 + i: i for i in range(len(old))},
        compiler_params=params(1, "scores"),
        name="scores",
    )(q, kv, phi_q, phi_k, dnum, before, before, tab_back, *old)


def run_keys(x, gain, bias, w_qkv, b_qkv, tab_in):
    seqs, span, width = x.shape
    three = lambda d: pl.BlockSpec((1,) + d, lambda s: (s, 0, 0))
    return pl.pallas_call(
        kv_kernel,
        grid=(seqs,),
        in_specs=[
            three((span, width)), whole((1, width)), whole((1, width)), whole((width, 3 * width)),
            whole((1, 3 * width)), whole((2, FEATS, 2 * LANES)),
        ],
        out_specs=[
            three((span, width)), three((span, 2 * width)), three((span, HEADS * FEATS)), three((SCAN_ROWS, FEATS)),
        ],
        out_shape=[
            shape((seqs, span, width), BF), shape((seqs, span, 2 * width), BF),
            shape((seqs, span, HEADS * FEATS), BF), shape((seqs, SCAN_ROWS, FEATS), F32),
        ],
        compiler_params=params(1, "keys"),
        name="keys",
    )(x, gain, bias, w_qkv, b_qkv, tab_in)


def run_middle(seqs, chips, core, x, dy, num, phi_q, before, w_out, b_out, gain, bias, w_up, b_up, w_down, b_down):
    rows, width = x.shape
    hidden = w_up.shape[1]
    per = rows // seqs // MID_TILE
    tile = lambda w: pl.BlockSpec((MID_TILE, w), lambda t, c: (t, 0))
    of_seq = lambda d: pl.BlockSpec((1,) + d, lambda t, c: (t // per, 0, 0))
    once = lambda d: pl.BlockSpec(d, lambda t, c: (0,) * len(d), pipeline_mode=pl.Buffered(1))
    sums = [(hidden, width), (width, hidden), (width, width)]
    packed = (hidden * width * 2 + width * width) // 2 // max(chips, 1) // LANES
    grads = [(chips, packed, LANES)] * 2 if chips else sums
    return pl.pallas_call(
        functools.partial(middle_kernel, per, chips),
        grid_spec=pltpu.PrefetchScalarGridSpec(
            num_scalar_prefetch=1,
            grid=(seqs * per,),
            in_specs=[
                tile(width), tile(width), tile(HEADS * LANES), tile(HEADS * FEATS), of_seq((SCAN_ROWS, FEATS)),
                once((width, width)), once((1, width)), once((1, width)), once((1, width)),
                once((width, hidden)), once((1, hidden)), once((hidden, width)), once((1, width)),
            ],
            out_specs=[
                tile(width), tile(width), tile(HEADS * LANES), of_seq((SCAN_ROWS, FEATS)),
                once((8, width)), once((1, hidden)),
            ]
            + [once(item) for item in grads],
            scratch_shapes=[pltpu.VMEM(item, F32) for item in sums] if chips else [],
        ),
        out_shape=[
            shape((rows, width), BF), shape((rows, width), F32), shape((rows, HEADS * LANES), BF),
            shape((seqs, SCAN_ROWS, FEATS), F32), shape((8, width), F32), shape((1, hidden), F32),
        ]
        + [shape(item, F32) for item in grads],
        compiler_params=params(1, "middle"),
        name="middle",
    )(half_of(core), x, dy, num, phi_q, before, w_out, b_out, gain, bias, w_up, b_up, w_down, b_down)


def run_final(seq, x, dy1, kv, phi_k, dq, dphik, dv, later, tab_back, gain, bias, w_qkv, *old):
    seqs, span, width = x.shape
    three = lambda d: pl.BlockSpec((1,) + d, lambda t: (seq, 0, 0))
    return pl.pallas_call(
        final_kernel,
        grid=(1,),
        in_specs=[
            three((span, width)), three((span, width)), three((span, 2 * width)), three((span, HEADS * FEATS)),
            three((span, width)), three((span, HEADS * FEATS)), three((span, width)), three((SCAN_ROWS, FEATS)),
            whole((2, FEATS, LANES)), whole((1, width)), whole((1, width)), whole((width, 3 * width)),
        ]
        + [pl.BlockSpec(memory_space=pl.ANY)] * len(old),
        out_specs=[three((span, width)), three((span, 3 * width)), whole((8, width)), whole((1, 3 * width))],
        out_shape=[
            shape((seqs, span, width), BF), shape((seqs, span, 3 * width), BF), shape((8, width), F32),
            shape((1, 3 * width), F32),
        ],
        input_output_aliases={12 + i: i for i in range(len(old))},
        compiler_params=params(1, "final"),
        name="final",
    )(x, dy1, kv, phi_k, dq, dphik, dv, later, tab_back, gain, bias, w_qkv, *old)


def shards(
    tokens, cotangent, gain_attn, shift_attn, w_qkv, b_qkv, w_out, b_out,
    gain_ffn, shift_ffn, w_up, b_up, w_down, b_down, tables, pick,
):
    seqs, span, width = tokens.shape
    hidden = w_up.shape[1]
    rows = seqs * span
    table = lax.dynamic_index_in_dim(tables, pick[0] % 2, 0, keepdims=False)
    none = jnp.zeros_like(table)
    minus = jnp.full((FEATS, LANES), -1.0, BF)
    tab_in = jnp.stack(
        [jnp.concatenate([table, none, minus], axis=1), jnp.concatenate([none, table, minus], axis=1)]
    )
    one = jnp.ones_like(table)
    tab_back = jnp.stack([jnp.concatenate([table, one], axis=1), jnp.concatenate([one, table], axis=1)])
    row = lambda a: a.reshape(1, -1)
    seq_bits = axis_bits("c") + axis_bits("y") + axis_bits("z")

    h1, kv, phi_k, state = run_keys(tokens, row(gain_attn), row(shift_attn), w_qkv, row(b_qkv), tab_in)

    scan = Stream(scan_stream(state.reshape(seqs * SCAN_ROWS, FEATS), seq_bits, len(seq_bits) - 1, False))
    phase([scan], [scan])
    local = None
    for seq in range(seqs):
        work = lambda kv, phi_k, *old: run_local(seq, h1, w_qkv, row(b_qkv), kv, phi_k, tab_in, *old)
        local = phase([scan], [scan], work, (kv, phi_k) + tuple(local or ()))
        if seq == 0:
            phase([scan], [scan])
    q, phi_q, num = local
    before = of_stages(scan).reshape(seqs, SCAN_ROWS, FEATS)

    flat = lambda a: a.reshape(rows, a.shape[-1])
    chips = lax.axis_size("x") * lax.axis_size("y") * lax.axis_size("z")
    fits = width % (16 * chips) == 0
    core = bit_of(0)
    meta = jnp.stack([lax.axis_index(axis) for axis in ("c", "x", "y", "z")]).astype(jnp.int32)
    out, dy1, dnum, dstate, sums, sum_up, *grads = run_middle(
        seqs, chips if fits else 0, core, flat(tokens), flat(cotangent), flat(num), flat(phi_q), before, w_out,
        row(b_out), row(gain_ffn), row(shift_ffn), w_up, row(b_up), w_down, row(b_down),
    )
    scan = Stream(scan_stream(dstate.reshape(seqs * SCAN_ROWS, FEATS), seq_bits, len(seq_bits) - 1, True))
    def back(seq, first, count):
        return lambda dnum, *old: run_scores(
            seq, first, count, q, kv, phi_q, phi_k, dnum.reshape(seqs, span, -1), before, tab_back, *old
        )

    def last(seq):
        return lambda dphik, *old: run_final(
            seq, tokens, dy1.reshape(seqs, span, width), kv, phi_k, dq, dphik, dv, later, tab_back,
            row(gain_attn), row(shift_attn), w_qkv, *old
        )

    half_pairs = PAIRS // 2
    if fits:
        theirs, mine = grads
        ffn = Stream(scatter_stream(theirs, mine))
        phase([scan, ffn], [scan])
        old = phase([scan], [scan, ffn], back(0, 0, half_pairs), (dnum,))
        phase([scan])
        phase([ffn], [scan])
        old = phase([scan], [scan], back(0, half_pairs, half_pairs), (dnum,) + tuple(old))
        phase([scan], [scan])
        old = phase([scan], [scan, ffn], back(1, 0, half_pairs), (dnum,) + tuple(old))
        phase([scan, ffn], [scan])
        old = phase((), [ffn], back(1, half_pairs, half_pairs), (dnum,) + tuple(old))
        later = scan.value
    else:
        old = phase([scan], [scan], back(0, 0, PAIRS), (dnum,))
        old = phase([scan], [scan], back(1, 0, PAIRS), (dnum,) + tuple(old))
        later = of_stages(scan)
    dq, dphik, dv = old
    later = later.reshape(seqs, SCAN_ROWS, FEATS)

    def join(*items):
        sums_attn, sum_qkv = items[0] + items[2], items[1] + items[3]
        return jnp.concatenate(
            [sums[:4].reshape(-1), sum_up.reshape(-1), sums_attn[:2].reshape(-1), sum_qkv.reshape(-1)]
        ).reshape(-1, LANES)

    all_bits = [bit for axis in reversed(AXES) for bit in axis_bits(axis)]
    if fits:
        some = lambda half, dqkv: qkv_grads(half, chips, flat(h1), flat(dqkv))

        def both(dphik):
            dx, dqkv, *parts = last(0)(dphik)
            dx, dqkv, *more = last(1)(dphik, dx, dqkv)
            theirs = some(1 - core, dqkv)
            return dx, dqkv, theirs, *parts, *more

        dx, dqkv, theirs, *parts = phase([ffn], [ffn], both, (dphik,))
        more = []
        qkv_sum = Stream(bucket_stream(theirs, lambda: more[0]))
        packed = lax.all_gather(ffn.value, ("c", "x", "y", "z"))
        small = Stream(small_stream(join(*parts), all_bits))
        more += phase([qkv_sum, small], [small], lambda dqkv: (some(core, dqkv),), (dqkv,))
        phase((), [qkv_sum])
        while qkv_sum.pending is not None or small.pending is not None:
            both = [item for item in (qkv_sum, small) if item.pending is not None]
            phase(both, both)
        grad_w_qkv = place_pieces(qkv_sum.value, meta, (width, 3 * width))
        small = small.value
        grad_w_down, grad_w_up, grad_w_out = unpack(packed, hidden, width)
    else:
        dx, dqkv, *parts = last(0)(dphik)
        dx, dqkv, *more = last(1)(dphik, dx, dqkv)
        grad_w_down, grad_w_up, grad_w_out, grad_w_qkv = lax.psum(
            (
                *grads, dot_tn(flat(h1), flat(dqkv)),
            ),
            AXES,
        )
        small = of_stages(Stream(small_stream(join(*parts, *more), all_bits)))
    small = small.reshape(-1)
    cuts = [width * i for i in range(1, 5)]
    cuts += [cuts[-1] + hidden, cuts[-1] + hidden + width, cuts[-1] + hidden + 2 * width]
    b_down_g, b_out_g, gain_f, shift_f, b_up_g, gain_a, shift_a, b_qkv_g = jnp.split(small, cuts)
    return (
        out.reshape(seqs, span, width), dx, gain_a, shift_a, grad_w_qkv, b_qkv_g,
        grad_w_out, b_out_g, gain_f, shift_f, grad_w_up, b_up_g, grad_w_down, b_down_g,
    )


def solution(mesh):
    dp, seq = mesh.shape["dp"], mesh.shape["seq"]
    cut = jax.sharding.Mesh(mesh.devices.reshape(dp, 4, seq // 8, 2), AXES)
    split = P("x", ("z", "y", "c"), None)
    return jax.shard_map(
        shards,
        mesh=cut,
        in_specs=(split, split) + (P(),) * 14,
        out_specs=(split, split) + (P(),) * 12,
        check_vma=False,
    )
```

time: 336 us -> 323 us (0.961); the launches traced: 334 us -> 318 us
  Pallas kernels: 133 us -> 105 us
  waiting for transfers between devices: 96 us -> 110 us
  local copies, waits for them, and re-layouts: 9.22 us -> 16.1 us
  other arithmetic: 26.5 us -> 21.4 us
  starting transfers between devices: 53.9 us -> 49.4 us
    pallas_call x11 -> x12, Pallas kernels: 120 us -> 97.3 us  [the longest x1 32.1 us: run_middle(): pl.pallas_call(functools.partial(middle_kernel, per, chips), grid_spec=pl...]
    ppermute x44 -> x46, waiting for transfers between devices: 96 us -> 108 us  [send(): return lax.ppermute(values, AXES, [(i, i ^ mask) for i in range(count)])]
    unnamed x56 -> x63, local copies, waits for them, and re-layouts: 3.55 us -> 10.3 us
    pallas_call x1, Pallas kernels: 9.7 us -> 4.84 us  [unpack(): pl.pallas_call(unpack_kernel, grid=(devices // block,), in_specs=[pl.Bloc...]
    ppermute x44 -> x46, starting transfers between devices: 53.8 us -> 49.3 us  [send(): return lax.ppermute(values, AXES, [(i, i ^ mask) for i in range(count)])]
  transfers between devices with their start and end apart: 45 -> 47, of which waited for: 22 -> 27; matrix products, arithmetic and copies ran while one was open for 3% -> 4% of each run, Pallas kernels for 26% -> 19%
where the time goes in v3:
time: 323 us; the launch traced here: 318 us
  waiting for transfers between devices  110 us (34%)
  Pallas kernels  105 us (33%)
  starting transfers between devices  49.4 us (15%)
  other arithmetic  21.4 us (7%)
  local copies, waits for them, and re-layouts  16.1 us (5%)
  between operations  15.8 us (5%)
    ppermute x46, waiting for transfers between devices, send(): return lax.ppermute(values, AXES, [(i, i ^ mask) for i in range(count)])  108 us
    ppermute x46, starting transfers between devices, send(): return lax.ppermute(values, AXES, [(i, i ^ mask) for i in range(count)])  49.3 us
    pallas_call x1, Pallas kernels, run_middle(): pl.pallas_call(functools.partial(middle_kernel, per, chips), grid_spec=pl...  32.1 us
    pallas_call x4, Pallas kernels, run_scores(): pl.pallas_call(functools.partial(score_back_kernel, first), grid=(count,)...  29.6 us
    pallas_call x2, Pallas kernels, run_local(): pl.pallas_call(local_kernel, grid=(PAIRS,), in_specs=[pl.BlockSpec((1, sp...  15 us
    unnamed x63, local copies, waits for them, and re-layouts  10.3 us
    pallas_call x2, Pallas kernels, run_final(): pl.pallas_call(final_kernel, grid=(1,), in_specs=[three((span, width)), t...  8.81 us
    add x9, other arithmetic, add_all(): return functools.reduce(jnp.add, items)  8.77 us
  transfers between devices with their start and end apart: 47, of which 27 were waited for; matrix products, arithmetic and copies ran while one was open for 4% of the time, Pallas kernels for 19%

profile of v3, /device:TPU:13, one launch (start us, length us, event | category | flops | bytes accessed | tf_op | source)
XLA Modules:
  0.0 317.6 jit_solution(11410659728042044498)
XLA Ops:
  10.3 8.3 %keys.1 = (bf16[2,512,512]{2,1,0:T(8,128)(2,1)}, bf16[2,512,1024]{2,1,0:T(8,128)(2,1)}, bf16[2,512,2048]{2,1,0:T(8,128)(2,1)}, f32[2,544,256]{2,1,0:T(8,128)}) custom-call(bf16[2,512,512]{2,1,0:T(8,128)(2,1)} %x_ref.5, f32[1,512]{1,0:T(1,128)} %bitcast.202, f32[1,512]{1,0:T(1,128)} %bitcast.205, bf16[512,1536]{1,0:T(8,128)(2,1)} %w_ref.9, ...), custom_call_target="tpu_custom_call" | custom-call | tf_op jit(solution)/shard_map/keys/pallas_call | solution.py:697
  22.5 7.5 %local.2 = (bf16[2,512,512]{2,1,0:T(8,128)(2,1)}, bf16[2,512,2048]{2,1,0:T(8,128)(2,1)}, f32[2,512,1024]{2,1,0:T(8,128)}) custom-call(bf16[2,512,512]{2,1,0:T(8,128)(2,1)} %get-tuple-element.182.h_ref, bf16[512,1536]{1,0:T(8,128)(2,1)} %w_ref.9, f32[1,1536]{1,0:T(1,128)} %reshape.167.b_ref, bf16[2,512,1024]{2,1,0:T(8,128)(2,1)} %get-tuple-element.193.v_ref.kv_ref, ...), custom_call_target="tpu_custom_call" | custom-call | tf_op jit(solution)/shard_map/local/pallas_call | solution.py:650
  30.5 3.7 %collective-permute-done.2 = f32[136,256]{1,0:T(8,128)S(1)} collective-permute-done((f32[136,256]{1,0:T(8,128)S(1)}, f32[136,256]{1,0:T(8,128)S(1)}, u32[]{:S(2)}, u32[]{:S(2)}) %collective-permute-start.2) | collective-permute-done | bytes 139296 | tf_op jit(solution)/shard_map/ppermute | solution.py:434
  36.6 7.5 %local.3 = (bf16[2,512,512]{2,1,0:T(8,128)(2,1)}, bf16[2,512,2048]{2,1,0:T(8,128)(2,1)}, f32[2,512,1024]{2,1,0:T(8,128)}) custom-call(bf16[2,512,512]{2,1,0:T(8,128)(2,1)} %get-tuple-element.182.h_ref, bf16[512,1536]{1,0:T(8,128)(2,1)} %w_ref.9, f32[1,1536]{1,0:T(1,128)} %reshape.167.b_ref, ...), custom_call_target="tpu_custom_call", output_to_operand_aliasing={{0}: (6, {}), {1}: (7, {}), {2}: (8, {})} | custom-call | tf_op jit(solution)/shard_map/local/pallas_call | solution.py:650
  44.4 3.7 %collective-permute-done.4 = f32[136,256]{1,0:T(8,128)S(1)} collective-permute-done((f32[136,256]{1,0:T(8,128)S(1)}, f32[136,256]{1,0:T(8,128)S(1)}, u32[]{:S(2)}, u32[]{:S(2)}) %collective-permute-start.4) | collective-permute-done | bytes 139296 | tf_op jit(solution)/shard_map/ppermute | solution.py:434
  50.0 3.9 %collective-permute-done.5 = f32[272,256]{1,0:T(8,128)S(1)} collective-permute-done((f32[272,256]{1,0:T(8,128)S(1)}, f32[272,256]{1,0:T(8,128)S(1)}, u32[]{:S(2)}, u32[]{:S(2)}) %collective-permute-start.5) | collective-permute-done | bytes 278560 | tf_op jit(solution)/shard_map/ppermute | solution.py:434
  54.1 4.7 %collective-permute-start.6 = (f32[544,256]{1,0:T(8,128)S(1)}, f32[544,256]{1,0:T(8,128)S(1)}, u32[]{:S(2)}, u32[]{:S(2)}) collective-permute-start(f32[544,256]{1,0:T(8,128)S(1)} %select_add_fusion.2), channel_id=1, source_target_pairs={{0,1},{1,0},{2,3},{3,2},{4,5},{5,4},{6,7},{7,6},{8,9},{9,8},{10,11... | collective-permute-start | bytes 1671176 | tf_op jit(solution)/shard_map/ppermute | solution.py:434
  61.6 32.1 %middle.1 = (bf16[1024,512]{1,0:T(8,128)(2,1)}, f32[1024,512]{1,0:T(8,128)}, bf16[1024,1024]{1,0:T(8,128)(2,1)}, f32[2,544,256]{2,1,0:T(8,128)}, f32[8,512]{1,0:...) custom-call(s32[1]{0:T(128)} %bitcast.core_ref.half_ref, ...), custom_call_target="tpu_custom_call" | custom-call | tf_op jit(solution)/shard_map/middle/pallas_call | solution.py:726
  95.5 5.8 %collective-permute-done.7 = f32[544,256]{1,0:T(8,128)S(1)} collective-permute-done((f32[544,256]{1,0:T(8,128)S(1)}, f32[544,256]{1,0:T(8,128)S(1)}, u32[]{:S(2)}, u32[]{:S(2)}) %collective-permute-start.7) | collective-permute-done | bytes 557088 | tf_op jit(solution)/shard_map/ppermute | solution.py:434
  103.3 7.6 %scores.4 = (bf16[2,512,512]{2,1,0:T(8,128)(2,1)}, bf16[2,512,2048]{2,1,0:T(8,128)(2,1)}, f32[2,512,512]{2,1,0:T(8,128)}) custom-call(bf16[2,512,512]{2,1,0:T(8,128)(2,1)} %get-tuple-element.212.q_ref, bf16[2,512,1024]{2,1,0:T(8,128)(2,1)} %get-tuple-element.193.v_ref.kv_ref, bf16[2,512,2048]{2,1,0:T(8,128)(2,1)} %get-tuple-element.202.phiq_ref, ...), custom_call_target="tpu_custom_call" | custom-call | tf_op jit(solution)/shard_map/scores/pallas_call | solution.py:673
  120.7 7.3 %scores.5 = (bf16[2,512,512]{2,1,0:T(8,128)(2,1)}, bf16[2,512,2048]{2,1,0:T(8,128)(2,1)}, f32[2,512,512]{2,1,0:T(8,128)}) custom-call(bf16[2,512,512]{2,1,0:T(8,128)(2,1)} %get-tuple-element.212.q_ref, bf16[2,512,1024]{2,1,0:T(8,128)(2,1)} %get-tuple-element.193.v_ref.kv_ref, ...), custom_call_target="tpu_custom_call", output_to_operand_aliasing={{0}: (8, {}), {1}: (9, {}), {2}: (10, {})} | custom-call | tf_op jit(solution)/shard_map/scores/pallas_call | solution.py:673
  131.1 3.0 collective-permute-done.12
  136.2 7.3 %scores.6 = (bf16[2,512,512]{2,1,0:T(8,128)(2,1)}, bf16[2,512,2048]{2,1,0:T(8,128)(2,1)}, f32[2,512,512]{2,1,0:T(8,128)}) custom-call(bf16[2,512,512]{2,1,0:T(8,128)(2,1)} %get-tuple-element.212.q_ref, bf16[2,512,1024]{2,1,0:T(8,128)(2,1)} %get-tuple-element.193.v_ref.kv_ref, ...), custom_call_target="tpu_custom_call", output_to_operand_aliasing={{0}: (8, {}), {1}: (9, {}), {2}: (10, {})} | custom-call | tf_op jit(solution)/shard_map/scores/pallas_call | solution.py:673
  143.4 8.2 %collective-permute-done.13 = f32[272,256]{1,0:T(8,128)S(1)} collective-permute-done((f32[272,256]{1,0:T(8,128)S(1)}, f32[272,256]{1,0:T(8,128)S(1)}, u32[]{:S(2)}, u32[]{:S(2)}) %collective-permute-start.13) | collective-permute-done | bytes 278560 | tf_op jit(solution)/shard_map/ppermute | solution.py:434
  159.3 7.5 %scores.7 = (bf16[2,512,512]{2,1,0:T(8,128)(2,1)}, bf16[2,512,2048]{2,1,0:T(8,128)(2,1)}, f32[2,512,512]{2,1,0:T(8,128)}) custom-call(bf16[2,512,512]{2,1,0:T(8,128)(2,1)} %get-tuple-element.212.q_ref, bf16[2,512,1024]{2,1,0:T(8,128)(2,1)} %get-tuple-element.193.v_ref.kv_ref, ...), custom_call_target="tpu_custom_call", output_to_operand_aliasing={{0}: (8, {}), {1}: (9, {}), {2}: (10, {})} | custom-call | tf_op jit(solution)/shard_map/scores/pallas_call | solution.py:673
  166.9 3.2 %collective-permute-done.16 = f32[4,288,128]{2,1,0:T(8,128)} collective-permute-done((f32[4,288,128]{2,1,0:T(8,128)}, f32[4,288,128]{2,1,0:T(8,128)}, u32[]{:S(2)}, u32[]{:S(2)}) %collective-permute-start.16) | collective-permute-done | bytes 589856 | tf_op jit(solution)/shard_map/ppermute | solution.py:434
  180.6 4.4 %final.2 = (bf16[2,512,512]{2,1,0:T(8,128)(2,1)}, bf16[2,512,1536]{2,1,0:T(8,128)(2,1)S(1)}, f32[8,512]{1,0:T(8,128)S(1)}, f32[1,1536]{1,0:T(1,128)S(1)}) custom-call(bf16[2,512,512]{2,1,0:T(8,128)(2,1)S(1)} %copy-done.10, f32[2,512,512]{2,1,0:T(8,128)S(1)} %bitcast.197, bf16[2,512,1024]{2,1,0:T(8,128)(2,1)S(1)} %copy-done.3, ...), custom_call_target="tpu_custom_call" | custom-call | tf_op jit(solution)/shard_map/final/pallas_call | solution.py:756
  185.0 4.4 %final.3 = (bf16[2,512,512]{2,1,0:T(8,128)(2,1)}, bf16[2,512,1536]{2,1,0:T(8,128)(2,1)S(1)}, f32[8,512]{1,0:T(8,128)S(1)}, f32[1,1536]{1,0:T(1,128)S(1)}) custom-call(bf16[2,512,512]{2,1,0:T(8,128)(2,1)S(1)} %copy-done.10, f32[2,512,512]{2,1,0:T(8,128)S(1)} %bitcast.198, ...), custom_call_target="tpu_custom_call", output_to_operand_aliasing={{0}: (12, {}), {1}: (13, {})} | custom-call | tf_op jit(solution)/shard_map/final/pallas_call | solution.py:756
  191.2 7.7 %collective-permute-done.20 = f32[576,128]{1,0:T(8,128)S(1)} collective-permute-done((f32[576,128]{1,0:T(8,128)S(1)}, f32[576,128]{1,0:T(8,128)S(1)}, u32[]{:S(2)}, u32[]{:S(2)}) %collective-permute-start.20) | collective-permute-done | bytes 294944 | tf_op jit(solution)/shard_map/ppermute | solution.py:434
  199.8 3.0 collective-permute-start.23
  208.5 11.3 %collective-permute-done.26 = f32[52,128]{1,0:T(8,128)S(1)} collective-permute-done((f32[52,128]{1,0:T(8,128)S(1)}, f32[52,128]{1,0:T(8,128)S(1)}, u32[]{:S(2)}, u32[]{:S(2)}) %collective-permute-start.26) | collective-permute-done | bytes 26656 | tf_op jit(solution)/shard_map/ppermute | solution.py:434
  222.3 3.0 collective-permute-done.29
  229.6 13.5 %collective-permute-done.33 = f32[52,128]{1,0:T(8,128)S(1)} collective-permute-done((f32[52,128]{1,0:T(8,128)S(1)}, f32[52,128]{1,0:T(8,128)S(1)}, u32[]{:S(2)}, u32[]{:S(2)}) %collective-permute-start.33) | collective-permute-done | bytes 26656 | tf_op jit(solution)/shard_map/ppermute | solution.py:434
  243.1 4.3 %collective-permute-done.32 = f32[192,128]{1,0:T(8,128)S(1)} collective-permute-done((f32[192,128]{1,0:T(8,128)S(1)}, f32[192,128]{1,0:T(8,128)S(1)}, u32[]{:S(2)}, u32[]{:S(2)}) %collective-permute-start.32) | collective-permute-done | bytes 98336 | tf_op jit(solution)/shard_map/ppermute | solution.py:434
  248.7 3.1 collective-permute-start.34
  253.8 3.4 %collective-permute-done.35 = f32[192,128]{1,0:T(8,128)S(1)} collective-permute-done((f32[192,128]{1,0:T(8,128)S(1)}, f32[192,128]{1,0:T(8,128)S(1)}, u32[]{:S(2)}, u32[]{:S(2)}) %collective-permute-start.35) | collective-permute-done | bytes 98336 | tf_op jit(solution)/shard_map/ppermute | solution.py:434
  257.2 5.0 %collective-permute-done.36 = f32[192,128]{1,0:T(8,128)S(1)} collective-permute-done((f32[192,128]{1,0:T(8,128)S(1)}, f32[192,128]{1,0:T(8,128)S(1)}, u32[]{:S(2)}, u32[]{:S(2)}) %collective-permute-start.36) | collective-permute-done | bytes 98336 | tf_op jit(solution)/shard_map/ppermute | solution.py:434
  262.4 9.0 %collective-permute-done.38 = f32[4,96,128]{2,1,0:T(8,128)S(1)} collective-permute-done((f32[4,96,128]{2,1,0:T(8,128)S(1)}, f32[4,96,128]{2,1,0:T(8,128)S(1)}, u32[]{:S(2)}, u32[]{:S(2)}) %collective-permute-start.38) | collective-permute-done | bytes 196640 | tf_op jit(solution)/shard_map/ppermute | solution.py:434
  273.8 11.8 %collective-permute-done.40.refs_1_ = f32[2,4,96,128]{3,2,1,0:T(8,128)S(1)} collective-permute-done((f32[2,4,96,128]{3,2,1,0:T(8,128)S(1)}, f32[2,4,96,128]{3,2,1,0:T(8,128)S(1)}, u32[]{:S(2)}, u32[]{:S(2)}) %collective-permute-start.40) | collective-permute-done | bytes 393248 | tf_op jit(solution)/shard_map/ppermute | solution.py:434
  285.6 7.0 %collective-permute-start.42 = (f32[2,4,96,128]{3,2,1,0:T(8,128)S(1)}, f32[2,4,96,128]{3,2,1,0:T(8,128)S(1)}, u32[]{:S(2)}, u32[]{:S(2)}) collective-permute-start(f32[2,4,96,128]{3,2,1,0:T(8,128)S(1)} %pad_maximum_fusion.4.refs_0_), channel_id=1, source_target_pairs={{0,1},{1,0},{2,3},{3,2},{4,5},{5,4},{6,7},{7,6},{8,9},{9,8},{10,11... | collective-permute-start | bytes 1179656 | tf_op jit(solution)/shard_map/ppermute | solution.py:434
  301.8 3.7 %copy-done.12 = f32[18432,128]{1,0:T(8,128)S(1)} copy-done((f32[18432,128]{1,0:T(8,128)S(1)}, f32[18432,128]{1,0:T(8,128)}, u32[]{:S(2)}) %copy-start.12) | copy-done | bytes 9437208
  305.5 4.8 %unpack.1 = (f32[2048,512]{1,0:T(8,128)}, f32[512,2048]{1,0:T(8,128)}, f32[512,512]{1,0:T(8,128)}) custom-call(f32[32,576,128]{2,1,0:T(8,128)S(1)} %bitcast.196), custom_call_target="tpu_custom_call" | custom-call | tf_op jit(solution)/shard_map/unpack/pallas_call | solution.py:628
  (213 shorter events, 81.1 us)
Async XLA Ops:
  7.2 294.6 %all-gather.3.cloned.1.call-start = ((), (), s32[]{:S(2)}) async-start(), calls=%async_computation | async-start | bytes 9732096 | tf_op jit(solution)/shard_map/all_gather | solution.py:868
  22.2 7.9 %collective-permute-start.1 = (f32[272,256]{1,0:T(8,128)S(1)}, f32[272,256]{1,0:T(8,128)S(1)}, u32[]{:S(2)}, u32[]{:S(2)}) collective-permute-start(f32[272,256]{1,0:T(8,128)S(1)} %constant_dynamic-slice_fusion.4), channel_id=1, source_target_pairs={{0,2},{1,3},{2,0},{3,1},{4,6},{5,7},{6,4},{7,5},{8,10},{9,11},{10,... | collective-permute-start | bytes 835592 | tf_op jit(solution)/shard_map/ppermute | solution.py:434
  34.2 9.9 %collective-permute-start.3 = (f32[136,256]{1,0:T(8,128)S(1)}, f32[136,256]{1,0:T(8,128)S(1)}, u32[]{:S(2)}, u32[]{:S(2)}) collective-permute-start(f32[136,256]{1,0:T(8,128)S(1)} %dynamic-slice_add_fusion.9), channel_id=1, source_target_pairs={{0,8},{1,9},{2,10},{3,11},{4,12},{5,13},{6,14},{7,15},{8,0},{9,1},... | collective-permute-start | bytes 417800 | tf_op jit(solution)/shard_map/ppermute | solution.py:434
  54.1 6.2 %collective-permute-start.6 = (f32[544,256]{1,0:T(8,128)S(1)}, f32[544,256]{1,0:T(8,128)S(1)}, u32[]{:S(2)}, u32[]{:S(2)}) collective-permute-start(f32[544,256]{1,0:T(8,128)S(1)} %select_add_fusion.2), channel_id=1, source_target_pairs={{0,1},{1,0},{2,3},{3,2},{4,5},{5,4},{6,7},{7,6},{8,9},{9,8},{10,11... | collective-permute-start | bytes 1671176 | tf_op jit(solution)/shard_map/ppermute | solution.py:434
  94.9 16.0 %collective-permute-start.9 = (f32[16,576,128]{2,1,0:T(8,128)}, f32[16,576,128]{2,1,0:T(8,128)}, u32[]{:S(2)}, u32[]{:S(2)}) collective-permute-start(f32[16,576,128]{2,1,0:T(8,128)} %get-tuple-element.211), channel_id=1, source_target_pairs={{0,1},{1,0},{2,3},{3,2},{4,5},{5,4},{6,7},{7,6},{8,9},{9,8},{10,11... | collective-permute-start | bytes 14155784 | tf_op jit(solution)/shard_map/ppermute | solution.py:434
  95.3 5.9 %collective-permute-start.7 = (f32[544,256]{1,0:T(8,128)S(1)}, f32[544,256]{1,0:T(8,128)S(1)}, u32[]{:S(2)}, u32[]{:S(2)}) collective-permute-start(f32[544,256]{1,0:T(8,128)S(1)} %constant_dynamic-slice_fusion.2), channel_id=1, source_target_pairs={{0,1},{1,0},{2,3},{3,2},{4,5},{5,4},{6,7},{7,6},{8,9},{9,8},{10,11... | collective-permute-start | bytes 1671176 | tf_op jit(solution)/shard_map/ppermute | solution.py:434
  101.4 9.5 %collective-permute-start.8 = (f32[272,256]{1,0:T(8,128)S(1)}, f32[272,256]{1,0:T(8,128)S(1)}, u32[]{:S(2)}, u32[]{:S(2)}) collective-permute-start(f32[272,256]{1,0:T(8,128)S(1)} %constant_dynamic-slice_fusion.1), channel_id=1, source_target_pairs={{0,2},{1,3},{2,0},{3,1},{4,6},{5,7},{6,4},{7,5},{8,10},{9,11},{10,... | collective-permute-start | bytes 835592 | tf_op jit(solution)/shard_map/ppermute | solution.py:434
  110.9 8.1 %collective-permute-start.10 = (f32[136,256]{1,0:T(8,128)S(1)}, f32[136,256]{1,0:T(8,128)S(1)}, u32[]{:S(2)}, u32[]{:S(2)}) collective-permute-start(f32[136,256]{1,0:T(8,128)S(1)} %constant_dynamic-slice_fusion), channel_id=1, source_target_pairs={{0,4},{1,5},{2,6},{3,7},{4,0},{5,1},{6,2},{7,3},{8,12},{9,13},{10,... | collective-permute-start | bytes 417800 | tf_op jit(solution)/shard_map/ppermute | solution.py:434
  117.4 34.2 %collective-permute-start.14 = (f32[2,4,288,128]{3,2,1,0:T(8,128)}, f32[2,4,288,128]{3,2,1,0:T(8,128)}, u32[]{:S(2)}, u32[]{:S(2)}) collective-permute-start(f32[2,4,288,128]{3,2,1,0:T(8,128)} %get-tuple-element.235), channel_id=1, source_target_pairs={{0,16},{1,17},{2,18},{3,19},{4,20},{5,21},{6,22},{7,23},{8,24},{9,... | collective-permute-start | bytes 3538952 | tf_op jit(solution)/shard_map/ppermute | solution.py:434
  118.6 33.0 %collective-permute-start.15 = (f32[2,4,288,128]{3,2,1,0:T(8,128)}, f32[2,4,288,128]{3,2,1,0:T(8,128)}, u32[]{:S(2)}, u32[]{:S(2)}) collective-permute-start(f32[2,4,288,128]{3,2,1,0:T(8,128)} %get-tuple-element.236), channel_id=1, source_target_pairs={{0,2},{1,3},{2,0},{3,1},{4,6},{5,7},{6,4},{7,5},{8,10},{9,11},{10,... | collective-permute-start | bytes 3538952 | tf_op jit(solution)/shard_map/ppermute | solution.py:434
  119.8 8.2 %collective-permute-start.11 = (f32[136,256]{1,0:T(8,128)}, f32[136,256]{1,0:T(8,128)}, u32[]{:S(2)}, u32[]{:S(2)}) collective-permute-start(f32[136,256]{1,0:T(8,128)} %dynamic-slice_add_fusion.8), channel_id=1, source_target_pairs={{0,8},{1,9},{2,10},{3,11},{4,12},{5,13},{6,14},{7,15},{8,0},{9,1},... | collective-permute-start | bytes 417800 | tf_op jit(solution)/shard_map/ppermute | solution.py:434
  135.1 16.5 %collective-permute-start.13 = (f32[272,256]{1,0:T(8,128)S(1)}, f32[272,256]{1,0:T(8,128)S(1)}, u32[]{:S(2)}, u32[]{:S(2)}) collective-permute-start(f32[272,256]{1,0:T(8,128)S(1)} %select_add_fusion.5), channel_id=1, source_target_pairs={{0,2},{1,3},{2,0},{3,1},{4,6},{5,7},{6,4},{7,5},{8,10},{9,11},{10,... | collective-permute-start | bytes 835592 | tf_op jit(solution)/shard_map/ppermute | solution.py:434
  156.5 13.6 %collective-permute-start.16 = (f32[4,288,128]{2,1,0:T(8,128)}, f32[4,288,128]{2,1,0:T(8,128)}, u32[]{:S(2)}, u32[]{:S(2)}) collective-permute-start(f32[4,288,128]{2,1,0:T(8,128)} %fusion.1), channel_id=1, source_target_pairs={{0,2},{1,3},{2,0},{3,1},{4,6},{5,7},{6,4},{7,5},{8,10},{9,11},{10,... | collective-permute-start | bytes 1769480 | tf_op jit(solution)/shard_map/ppermute | solution.py:434
  156.9 13.3 %collective-permute-start.17 = (f32[4,288,128]{2,1,0:T(8,128)}, f32[4,288,128]{2,1,0:T(8,128)}, u32[]{:S(2)}, u32[]{:S(2)}) collective-permute-start(f32[4,288,128]{2,1,0:T(8,128)} %fusion), channel_id=1, source_target_pairs={{0,16},{1,17},{2,18},{3,19},{4,20},{5,21},{6,22},{7,23},{8,24},{9,... | collective-permute-start | bytes 1769480 | tf_op jit(solution)/shard_map/ppermute | solution.py:434
  157.1 9.7 %collective-permute-start.21 = (f32[544,256]{1,0:T(8,128)}, f32[544,256]{1,0:T(8,128)}, u32[]{:S(2)}, u32[]{:S(2)}) collective-permute-start(f32[544,256]{1,0:T(8,128)} %select_add_fusion.1), channel_id=1, source_target_pairs={{0,1},{1,0},{2,3},{3,2},{4,5},{5,4},{6,7},{7,6},{8,9},{9,8},{10,11... | collective-permute-start | bytes 1671176 | tf_op jit(solution)/shard_map/ppermute | solution.py:434
  172.2 19.0 %collective-permute-start.18 = (f32[576,128]{1,0:T(8,128)S(1)}, f32[576,128]{1,0:T(8,128)S(1)}, u32[]{:S(2)}, u32[]{:S(2)}) collective-permute-start(f32[576,128]{1,0:T(8,128)S(1)} %get-tuple-element.262), channel_id=1, source_target_pairs={{0,4},{1,5},{2,6},{3,7},{4,0},{5,1},{6,2},{7,3},{8,12},{9,13},{10,... | collective-permute-start | bytes 884744 | tf_op jit(solution)/shard_map/ppermute | solution.py:434
  172.5 18.7 %collective-permute-start.19 = (f32[576,128]{1,0:T(8,128)S(1)}, f32[576,128]{1,0:T(8,128)S(1)}, u32[]{:S(2)}, u32[]{:S(2)}) collective-permute-start(f32[576,128]{1,0:T(8,128)S(1)} %get-tuple-element.263), channel_id=1, source_target_pairs={{0,8},{1,9},{2,10},{3,11},{4,12},{5,13},{6,14},{7,15},{8,0},{9,1},... | collective-permute-start | bytes 884744 | tf_op jit(solution)/shard_map/ppermute | solution.py:434
  173.6 25.3 %collective-permute-start.20 = (f32[576,128]{1,0:T(8,128)S(1)}, f32[576,128]{1,0:T(8,128)S(1)}, u32[]{:S(2)}, u32[]{:S(2)}) collective-permute-start(f32[576,128]{1,0:T(8,128)S(1)} %get-tuple-element.264), channel_id=1, source_target_pairs={{0,12},{1,13},{2,14},{3,15},{4,8},{5,9},{6,10},{7,11},{8,4},{9,5},... | collective-permute-start | bytes 884744 | tf_op jit(solution)/shard_map/ppermute | solution.py:434
  199.8 6.7 %collective-permute-start.23 = (f32[16,192,128]{2,1,0:T(8,128)S(1)}, f32[16,192,128]{2,1,0:T(8,128)S(1)}, u32[]{:S(2)}, u32[]{:S(2)}) collective-permute-start(f32[16,192,128]{2,1,0:T(8,128)S(1)} %qkv_grads.2), channel_id=1, source_target_pairs={{0,1},{1,0},{2,3},{3,2},{4,5},{5,4},{6,7},{7,6},{8,9},{9,8},{10,11... | collective-permute-start | bytes 4718600 | tf_op jit(solution)/shard_map/ppermute | solution.py:434
  206.7 13.1 %collective-permute-start.24 = (f32[2,4,96,128]{3,2,1,0:T(8,128)S(1)}, f32[2,4,96,128]{3,2,1,0:T(8,128)S(1)}, u32[]{:S(2)}, u32[]{:S(2)}) collective-permute-start(f32[2,4,96,128]{3,2,1,0:T(8,128)S(1)} %get-tuple-element.292), channel_id=1, source_target_pairs={{0,16},{1,17},{2,18},{3,19},{4,20},{5,21},{6,22},{7,23},{8,24},{9,... | collective-permute-start | bytes 1179656 | tf_op jit(solution)/shard_map/ppermute | solution.py:434
  207.0 12.8 %collective-permute-start.25 = (f32[2,4,96,128]{3,2,1,0:T(8,128)S(1)}, f32[2,4,96,128]{3,2,1,0:T(8,128)S(1)}, u32[]{:S(2)}, u32[]{:S(2)}) collective-permute-start(f32[2,4,96,128]{3,2,1,0:T(8,128)S(1)} %fusion.2), channel_id=1, source_target_pairs={{0,2},{1,3},{2,0},{3,1},{4,6},{5,7},{6,4},{7,5},{8,10},{9,11},{10,... | collective-permute-start | bytes 1179656 | tf_op jit(solution)/shard_map/ppermute | solution.py:434
  208.1 11.7 %collective-permute-start.26 = (f32[52,128]{1,0:T(8,128)S(1)}, f32[52,128]{1,0:T(8,128)S(1)}, u32[]{:S(2)}, u32[]{:S(2)}) collective-permute-start(f32[52,128]{1,0:T(8,128)S(1)} %fusion.28), channel_id=1, source_target_pairs={{0,2},{1,3},{2,0},{3,1},{4,6},{5,7},{6,4},{7,5},{8,10},{9,11},{10,... | collective-permute-start | bytes 79880 | tf_op jit(solution)/shard_map/ppermute | solution.py:434
  226.0 17.1 %collective-permute-start.30 = (f32[192,128]{1,0:T(8,128)S(1)}, f32[192,128]{1,0:T(8,128)S(1)}, u32[]{:S(2)}, u32[]{:S(2)}) collective-permute-start(f32[192,128]{1,0:T(8,128)S(1)} %get-tuple-element.304), channel_id=1, source_target_pairs={{0,4},{1,5},{2,6},{3,7},{4,0},{5,1},{6,2},{7,3},{8,12},{9,13},{10,... | collective-permute-start | bytes 294920 | tf_op jit(solution)/shard_map/ppermute | solution.py:434
  226.1 17.0 %collective-permute-start.31 = (f32[192,128]{1,0:T(8,128)S(1)}, f32[192,128]{1,0:T(8,128)S(1)}, u32[]{:S(2)}, u32[]{:S(2)}) collective-permute-start(f32[192,128]{1,0:T(8,128)S(1)} %get-tuple-element.305), channel_id=1, source_target_pairs={{0,8},{1,9},{2,10},{3,11},{4,12},{5,13},{6,14},{7,15},{8,0},{9,1},... | collective-permute-start | bytes 294920 | tf_op jit(solution)/shard_map/ppermute | solution.py:434
  227.5 19.9 %collective-permute-start.32 = (f32[192,128]{1,0:T(8,128)S(1)}, f32[192,128]{1,0:T(8,128)S(1)}, u32[]{:S(2)}, u32[]{:S(2)}) collective-permute-start(f32[192,128]{1,0:T(8,128)S(1)} %get-tuple-element.306), channel_id=1, source_target_pairs={{0,12},{1,13},{2,14},{3,15},{4,8},{5,9},{6,10},{7,11},{8,4},{9,5},... | collective-permute-start | bytes 294920 | tf_op jit(solution)/shard_map/ppermute | solution.py:434
  228.7 14.4 %collective-permute-start.33 = (f32[52,128]{1,0:T(8,128)S(1)}, f32[52,128]{1,0:T(8,128)S(1)}, u32[]{:S(2)}, u32[]{:S(2)}) collective-permute-start(f32[52,128]{1,0:T(8,128)S(1)} %add.369), channel_id=1, source_target_pairs={{0,8},{1,9},{2,10},{3,11},{4,12},{5,13},{6,14},{7,15},{8,0},{9,1},... | collective-permute-start | bytes 79880 | tf_op jit(solution)/shard_map/ppermute | solution.py:434
  251.8 10.4 %collective-permute-start.36 = (f32[192,128]{1,0:T(8,128)S(1)}, f32[192,128]{1,0:T(8,128)S(1)}, u32[]{:S(2)}, u32[]{:S(2)}) collective-permute-start(f32[192,128]{1,0:T(8,128)S(1)} %fusion.20), channel_id=1, source_target_pairs={{0,12},{1,13},{2,14},{3,15},{4,8},{5,9},{6,10},{7,11},{8,4},{9,5},... | collective-permute-start | bytes 294920 | tf_op jit(solution)/shard_map/ppermute | solution.py:434
  262.3 9.2 %collective-permute-start.38 = (f32[4,96,128]{2,1,0:T(8,128)S(1)}, f32[4,96,128]{2,1,0:T(8,128)S(1)}, u32[]{:S(2)}, u32[]{:S(2)}) collective-permute-start(f32[4,96,128]{2,1,0:T(8,128)S(1)} %get-tuple-element.320), channel_id=1, source_target_pairs={{0,2},{1,3},{2,0},{3,1},{4,6},{5,7},{6,4},{7,5},{8,10},{9,11},{10,... | collective-permute-start | bytes 589832 | tf_op jit(solution)/shard_map/ppermute | solution.py:434
  262.3 9.2 %collective-permute-start.39 = (f32[4,96,128]{2,1,0:T(8,128)S(1)}, f32[4,96,128]{2,1,0:T(8,128)S(1)}, u32[]{:S(2)}, u32[]{:S(2)}) collective-permute-start(f32[4,96,128]{2,1,0:T(8,128)S(1)} %get-tuple-element.321), channel_id=1, source_target_pairs={{0,16},{1,17},{2,18},{3,19},{4,20},{5,21},{6,22},{7,23},{8,24},{9,... | collective-permute-start | bytes 589832 | tf_op jit(solution)/shard_map/ppermute | solution.py:434
  271.6 14.0 %collective-permute-start.40 = (f32[2,4,96,128]{3,2,1,0:T(8,128)S(1)}, f32[2,4,96,128]{3,2,1,0:T(8,128)S(1)}, u32[]{:S(2)}, u32[]{:S(2)}) collective-permute-start(f32[2,4,96,128]{3,2,1,0:T(8,128)S(1)} %pad_maximum_fusion.4.refs_0_), channel_id=1, source_target_pairs={{0,16},{1,17},{2,18},{3,19},{4,20},{5,21},{6,22},{7,23},{8,24},{9,... | collective-permute-start | bytes 1179656 | tf_op jit(solution)/shard_map/ppermute | solution.py:434
  271.6 13.9 %collective-permute-start.41 = (f32[2,4,96,128]{3,2,1,0:T(8,128)S(1)}, f32[2,4,96,128]{3,2,1,0:T(8,128)S(1)}, u32[]{:S(2)}, u32[]{:S(2)}) collective-permute-start(f32[2,4,96,128]{3,2,1,0:T(8,128)S(1)} %pad_maximum_fusion.5.refs_2_), channel_id=1, source_target_pairs={{0,2},{1,3},{2,0},{3,1},{4,6},{5,7},{6,4},{7,5},{8,10},{9,11},{10,... | collective-permute-start | bytes 1179656 | tf_op jit(solution)/shard_map/ppermute | solution.py:434
  285.6 8.7 %collective-permute-start.42 = (f32[2,4,96,128]{3,2,1,0:T(8,128)S(1)}, f32[2,4,96,128]{3,2,1,0:T(8,128)S(1)}, u32[]{:S(2)}, u32[]{:S(2)}) collective-permute-start(f32[2,4,96,128]{3,2,1,0:T(8,128)S(1)} %pad_maximum_fusion.4.refs_0_), channel_id=1, source_target_pairs={{0,1},{1,0},{2,3},{3,2},{4,5},{5,4},{6,7},{7,6},{8,9},{9,8},{10,11... | collective-permute-start | bytes 1179656 | tf_op jit(solution)/shard_map/ppermute | solution.py:434
  (45 other events, 225.0 us)
Sparse Core Ops, SparseCore 0:
  199.8 101.9 all-gather.2

commit v4 on v3

--- a/solution.py
+++ b/solution.py
@@ -142,10 +142,21 @@
 
 def middle_kernel(
     per, chips, core_ref, x_ref, dy_ref, num_ref, phiq_ref, state_ref, w_out_ref, b_out_ref, gain_ref, shift_ref,
-    w_up_ref, b_up_ref, w_down_ref, b_down_ref,
-    out_ref, dy1_ref, dnum_ref, dstate_ref, sums_ref, sum_up_ref, *grads,
+    w_up_from, b_up_ref, w_down_from, b_down_ref,
+    out_ref, dy1_ref, dnum_ref, dstate_ref, sums_ref, sum_up_ref, *rest,
 ):
-    down_ref, up_ref, wout_ref = grads[-3:]
+    *grads, w_up_ref, w_down_ref, w_sems = rest
+    down_ref, up_ref, wout_ref = grads[2:5] if chips else grads
+    loads = [
+        pltpu.make_async_copy(source, place, w_sems.at[at])
+        for at, (source, place) in enumerate(((w_up_from, w_up_ref), (w_down_from, w_down_ref)))
+    ]
+
+    @pl.when(pl.program_id(0) == 0)
+    def _():
+        for load in loads:
+            load.start()
+
     step = pl.program_id(0)
     width = x_ref.shape[-1]
     att_parts, den_parts = [], []
@@ -175,6 +186,12 @@
     grad_out = dy_ref[...]
     hidden = w_up_ref.shape[1]
     chunk = 1024
+
+    @pl.when(step == 0)
+    def _():
+        for load in loads:
+            load.wait()
+
     result = middle + b_down_ref[...]
     grad_low = jnp.zeros(middle.shape, F32)
 
@@ -197,6 +214,29 @@
         grad_low += dot_nt(dup, w_up_ref[:, at : at + chunk])
         sum_up_ref[:, at : at + chunk] += jnp.sum(dup.astype(F32), axis=0, keepdims=True)
     out_ref[...] = result.astype(BF)
+    if chips:
+        packed_ref, sems = grads[5:]
+        behind = packed_ref.shape[2] * 2 * hidden // (2 * hidden + middle.shape[1])
+        parts = [
+            (half, first, count)
+            for first, count in ((0, behind), (behind, packed_ref.shape[2] - behind))
+            for half in range(2)
+        ]
+        stores = [
+            pltpu.make_async_copy(
+                packed_ref.at[half, :, pl.ds(first, count), :],
+                grads[half].at[:, pl.ds(first, count), :],
+                sems.at[at],
+            )
+            for at, (half, first, count) in enumerate(parts)
+        ]
+
+        @pl.when(step == pl.num_programs(0) - 1)
+        def _():
+            for half in range(2):
+                pack_half(core_ref[0] if half else 1 - core_ref[0], chips, packed_ref.at[half], 0, down_ref, up_ref)
+                stores[half].start()
+
     wide = grad_out.astype(F32)
     grad_mid = wide + normalise_back(grad_low, unit, scale, gain_ref[...])
     dy1_ref[...] = grad_mid
@@ -225,28 +265,32 @@
             dstate_ref[0, rows : rows + HEAD_DIM, :] += main
             dstate_ref[0, STATE_ROWS + at : STATE_ROWS + at + 1, :] += jnp.sum(rest, axis=0, keepdims=True)
 
-    if len(grads) > 3:
+    if chips:
 
         @pl.when(step == pl.num_programs(0) - 1)
         def _():
-            for half, packed_ref in ((1 - core_ref[0], grads[0]), (core_ref[0], grads[1])):
-                pack_half(half, chips, packed_ref, down_ref, up_ref, wout_ref)
+            for half in range(2):
+                pack_half(core_ref[0] if half else 1 - core_ref[0], chips, packed_ref.at[half], behind, None, wout_ref)
+                stores[2 + half].start()
+            for store in stores:
+                store.wait()
 
 
 def add_to(total_ref, rows, cols, step, values):
     total_ref[rows, cols] = jnp.where(step == 0, 0.0, total_ref[rows, cols]) + values
 
 
-def pack_half(half, chips, packed_ref, down_ref, up_ref, wout_ref):
-    rows = down_ref.shape[0] // 2 // chips
-    first = half * (down_ref.shape[0] // 2)
-    for chip in range(chips):
-        for strip in range(down_ref.shape[1] // LANES):
-            packed_ref[chip, strip * rows : (strip + 1) * rows, :] = down_ref[
-                pl.ds(pl.multiple_of(first + chip * rows, rows), rows), strip * LANES : (strip + 1) * LANES
-            ]
-    base = rows * (down_ref.shape[1] // LANES)
-    for total_ref in (up_ref, wout_ref):
+def pack_half(half, chips, packed_ref, base, down_ref, *wide_refs):
+    if down_ref is not None:
+        rows = down_ref.shape[0] // 2 // chips
+        first = half * (down_ref.shape[0] // 2)
+        for chip in range(chips):
+            for strip in range(down_ref.shape[1] // LANES):
+                packed_ref[chip, base + strip * rows : base + (strip + 1) * rows, :] = down_ref[
+                    pl.ds(pl.multiple_of(first + chip * rows, rows), rows), strip * LANES : (strip + 1) * LANES
+                ]
+        base += rows * (down_ref.shape[1] // LANES)
+    for total_ref in wide_refs:
         rows = total_ref.shape[0] // chips
         strips = total_ref.shape[1] // 2 // LANES
         for strip in range(strips):
@@ -495,19 +539,21 @@
     return part + rest
 
 
+def cut_part(part, axis, at, rows):
+    start, size = [0] * part.ndim, list(part.shape)
+    start[axis], size[axis] = at, 1
+    if rows:
+        start[-2], size[-2] = rows
+    return jnp.squeeze(lax.dynamic_slice(part, start, size), axis)
+
+
 def chunks(parts, axis, bits, rows=None):
     mine = value_of(bits)
-    out = []
-    for value in range(1 << len(bits)):
-        cut = []
-        for part in parts:
-            start, size = [0] * part.ndim, list(part.shape)
-            start[axis], size[axis] = mine ^ value, 1
-            if rows:
-                start[-2], size[-2] = rows
-            cut.append(lax.dynamic_slice(part, start, size))
-        out.append(jnp.squeeze(add_all(cut), axis))
-    return out
+    own = [cut_part(part, axis, mine, rows) for part in parts]
+    others = [
+        add_all([cut_part(part, axis, mine ^ value, rows) for part in parts]) for value in range(1, 1 << len(bits))
+    ]
+    return own, others
 
 
 def add_all(items):
@@ -528,16 +574,16 @@
     parts = [mine() if callable(mine) else mine, got]
     cut = parts[0].shape[1] // 2
     parts = [item.reshape(1 << len(x), 1 << len(y), 1 << len(z), *item.shape[1:]) for item in parts]
-    a, b = chunks(parts, 0, x, (0, cut)), chunks(parts, 1, y, (cut, cut))
-    got = yield to_partners(a[1:], x) + to_partners(b[1:], y)
-    a = chunks(a[:1] + got[: len(a) - 1], 0, y)
-    b = chunks(b[:1] + got[-(len(b) - 1) :], 0, x)
-    got = yield to_partners(a[1:], y) + to_partners(b[1:], x)
-    parts = [a[:1] + got[: len(a) - 1], b[:1] + got[-(len(b) - 1) :]]
+    (a, a_out), (b, b_out) = chunks(parts, 0, x, (0, cut)), chunks(parts, 1, y, (cut, cut))
+    got = yield to_partners(a_out, x) + to_partners(b_out, y)
+    a, a_out = chunks(a + got[: len(a_out)], 0, y)
+    b, b_out = chunks(b + got[-len(b_out) :], 0, x)
+    got = yield to_partners(a_out, y) + to_partners(b_out, x)
+    parts = [a + got[: len(a_out)], b + got[-len(b_out) :]]
     both = jnp.concatenate([add_all(part) for part in parts], axis=1)
-    both = chunks([both], 0, z)
-    got = yield to_partners(both[1:], z)
-    return add_all(both[:1] + got)
+    own, out = chunks([both], 0, z)
+    got = yield to_partners(out, z)
+    return add_all(own + got)
 
 
 def bucket_stream(theirs, mine):
@@ -723,6 +769,13 @@
     sums = [(hidden, width), (width, hidden), (width, width)]
     packed = (hidden * width * 2 + width * width) // 2 // max(chips, 1) // LANES
     grads = [(chips, packed, LANES)] * 2 if chips else sums
+    anywhere = pl.BlockSpec(memory_space=pl.ANY)
+    scratch = [pltpu.VMEM((width, hidden), BF), pltpu.VMEM((hidden, width), BF), pltpu.SemaphoreType.DMA((2,))]
+    if chips:
+        scratch = [
+            *(pltpu.VMEM(item, F32) for item in sums), pltpu.VMEM((2, chips, packed, LANES), F32),
+            pltpu.SemaphoreType.DMA((4,)), *scratch,
+        ]
     return pl.pallas_call(
         functools.partial(middle_kernel, per, chips),
         grid_spec=pltpu.PrefetchScalarGridSpec(
@@ -731,14 +784,14 @@
             in_specs=[
                 tile(width), tile(width), tile(HEADS * LANES), tile(HEADS * FEATS), of_seq((SCAN_ROWS, FEATS)),
                 once((width, width)), once((1, width)), once((1, width)), once((1, width)),
-                once((width, hidden)), once((1, hidden)), once((hidden, width)), once((1, width)),
+                anywhere, once((1, hidden)), anywhere, once((1, width)),
             ],
             out_specs=[
                 tile(width), tile(width), tile(HEADS * LANES), of_seq((SCAN_ROWS, FEATS)),
                 once((8, width)), once((1, hidden)),
             ]
-            + [once(item) for item in grads],
-            scratch_shapes=[pltpu.VMEM(item, F32) for item in sums] if chips else [],
+            + [anywhere if chips else once(item) for item in grads],
+            scratch_shapes=scratch,
         ),
         out_shape=[
             shape((rows, width), BF), shape((rows, width), F32), shape((rows, HEADS * LANES), BF),
@@ -829,15 +882,15 @@
     if fits:
         theirs, mine = grads
         ffn = Stream(scatter_stream(theirs, mine))
-        phase([scan, ffn], [scan])
-        old = phase([scan], [scan, ffn], back(0, 0, half_pairs), (dnum,))
+        phase([scan], [scan])
+        old = phase([scan, ffn], [scan, ffn], back(0, 0, half_pairs), (dnum,))
         phase([scan])
         phase([ffn], [scan])
         old = phase([scan], [scan], back(0, half_pairs, half_pairs), (dnum,) + tuple(old))
         phase([scan], [scan])
-        old = phase([scan], [scan, ffn], back(1, 0, half_pairs), (dnum,) + tuple(old))
-        phase([scan, ffn], [scan])
-        old = phase((), [ffn], back(1, half_pairs, half_pairs), (dnum,) + tuple(old))
+        old = phase([scan], [ffn], back(1, 0, half_pairs), (dnum,) + tuple(old))
+        old = phase([ffn], [scan], back(1, half_pairs, half_pairs), (dnum,) + tuple(old))
+        phase([scan], [scan, ffn])
         later = scan.value
     else:
         old = phase([scan], [scan], back(0, 0, PAIRS), (dnum,))

time: 323 us -> 319 us (0.988)
  waiting for transfers between devices: 110 us -> 99.9 us
  starting transfers between devices: 49.4 us -> 57.8 us
    ppermute x46, waiting for transfers between devices: 108 us -> 97.4 us  [send(): return lax.ppermute(values, AXES, [(i, i ^ mask) for i in range(count)])]
    ppermute x46, starting transfers between devices: 49.3 us -> 57.8 us  [send(): return lax.ppermute(values, AXES, [(i, i ^ mask) for i in range(count)])]
    squeeze x7 -> x2, other arithmetic: 4.15 us -> 0.1 us  [cut_part(): return jnp.squeeze(lax.dynamic_slice(part, start, size), axis)]
    add x9 -> x10, other arithmetic: 8.77 us -> 11.6 us  [add_all(): return functools.reduce(jnp.add, items)]
    unnamed x63 -> x55, local copies, waits for them, and re-layouts: 10.3 us -> 10.4 us
  transfers between devices with their start and end apart: 47 -> 47, of which waited for: 27 -> 28; matrix products, arithmetic and copies ran while one was open for 4% -> 4% of each run, Pallas kernels for 19% -> 19%
where the time goes in v4:
time: 319 us; the launch traced here: 313 us
  Pallas kernels  103 us (32%)
  waiting for transfers between devices  99.9 us (31%)
  starting transfers between devices  57.8 us (18%)
  other arithmetic  20.7 us (6%)
  local copies, waits for them, and re-layouts  16.1 us (5%)
  between operations  15.9 us (5%)
    ppermute x46, waiting for transfers between devices, send(): return lax.ppermute(values, AXES, [(i, i ^ mask) for i in range(count)])  97.4 us
    ppermute x46, starting transfers between devices, send(): return lax.ppermute(values, AXES, [(i, i ^ mask) for i in range(count)])  57.8 us
    pallas_call x1, Pallas kernels, run_middle(): pl.pallas_call(functools.partial(middle_kernel, per, chips), grid_spec=pl...  30.2 us
    pallas_call x4, Pallas kernels, run_scores(): pl.pallas_call(functools.partial(score_back_kernel, first), grid=(count,)...  29.5 us
    pallas_call x2, Pallas kernels, run_local(): pl.pallas_call(local_kernel, grid=(PAIRS,), in_specs=[pl.BlockSpec((1, sp...  15.1 us
    add x10, other arithmetic, add_all(): return functools.reduce(jnp.add, items)  11.6 us
    unnamed x55, local copies, waits for them, and re-layouts  10.4 us
    pallas_call x2, Pallas kernels, run_final(): pl.pallas_call(final_kernel, grid=(1,), in_specs=[three((span, width)), t...  8.8 us
  transfers between devices with their start and end apart: 47, of which 28 were waited for; matrix products, arithmetic and copies ran while one was open for 4% of the time, Pallas kernels for 19%

profile of v4, /device:TPU:13, one launch (start us, length us, event | category | flops | bytes accessed | tf_op | source)
XLA Modules:
  0.0 313.2 jit_solution(5804376659927712476)
XLA Ops:
  10.3 8.3 %keys.1 = (bf16[2,512,512]{2,1,0:T(8,128)(2,1)}, bf16[2,512,1024]{2,1,0:T(8,128)(2,1)}, bf16[2,512,2048]{2,1,0:T(8,128)(2,1)}, f32[2,544,256]{2,1,0:T(8,128)}) custom-call(bf16[2,512,512]{2,1,0:T(8,128)(2,1)} %x_ref.5, f32[1,512]{1,0:T(1,128)} %bitcast.189, f32[1,512]{1,0:T(1,128)} %bitcast.192, bf16[512,1536]{1,0:T(8,128)(2,1)} %w_ref.9, ...), custom_call_target="tpu_custom_call" | custom-call | tf_op jit(solution)/shard_map/keys/pallas_call | solution.py:743
  23.5 7.6 %local.2 = (bf16[2,512,512]{2,1,0:T(8,128)(2,1)}, bf16[2,512,2048]{2,1,0:T(8,128)(2,1)}, f32[2,512,1024]{2,1,0:T(8,128)}) custom-call(bf16[2,512,512]{2,1,0:T(8,128)(2,1)} %get-tuple-element.181.h_ref, bf16[512,1536]{1,0:T(8,128)(2,1)} %w_ref.9, f32[1,1536]{1,0:T(1,128)} %reshape.203.b_ref, bf16[2,512,1024]{2,1,0:T(8,128)(2,1)} %get-tuple-element.192.v_ref.kv_ref, ...), custom_call_target="tpu_custom_call" | custom-call | tf_op jit(solution)/shard_map/local/pallas_call | solution.py:696
  31.4 3.8 %collective-permute-done.2 = f32[136,256]{1,0:T(8,128)S(1)} collective-permute-done((f32[136,256]{1,0:T(8,128)S(1)}, f32[136,256]{1,0:T(8,128)S(1)}, u32[]{:S(2)}, u32[]{:S(2)}) %collective-permute-start.2) | collective-permute-done | bytes 139296 | tf_op jit(solution)/shard_map/ppermute | solution.py:478
  37.6 7.5 %local.3 = (bf16[2,512,512]{2,1,0:T(8,128)(2,1)}, bf16[2,512,2048]{2,1,0:T(8,128)(2,1)}, f32[2,512,1024]{2,1,0:T(8,128)}) custom-call(bf16[2,512,512]{2,1,0:T(8,128)(2,1)} %get-tuple-element.181.h_ref, bf16[512,1536]{1,0:T(8,128)(2,1)} %w_ref.9, f32[1,1536]{1,0:T(1,128)} %reshape.203.b_ref, ...), custom_call_target="tpu_custom_call", output_to_operand_aliasing={{0}: (6, {}), {1}: (7, {}), {2}: (8, {})} | custom-call | tf_op jit(solution)/shard_map/local/pallas_call | solution.py:696
  45.4 3.7 %collective-permute-done.4 = f32[136,256]{1,0:T(8,128)S(1)} collective-permute-done((f32[136,256]{1,0:T(8,128)S(1)}, f32[136,256]{1,0:T(8,128)S(1)}, u32[]{:S(2)}, u32[]{:S(2)}) %collective-permute-start.4) | collective-permute-done | bytes 139296 | tf_op jit(solution)/shard_map/ppermute | solution.py:478
  51.1 4.0 %collective-permute-done.5 = f32[272,256]{1,0:T(8,128)} collective-permute-done((f32[272,256]{1,0:T(8,128)S(1)}, f32[272,256]{1,0:T(8,128)}, u32[]{:S(2)}, u32[]{:S(2)}) %collective-permute-start.5) | collective-permute-done | bytes 278560 | tf_op jit(solution)/shard_map/ppermute | solution.py:478
  56.2 4.6 %collective-permute-start.6 = (f32[544,256]{1,0:T(8,128)S(1)}, f32[544,256]{1,0:T(8,128)S(1)}, u32[]{:S(2)}, u32[]{:S(2)}) collective-permute-start(f32[544,256]{1,0:T(8,128)S(1)} %select_add_fusion.2), channel_id=1, source_target_pairs={{0,1},{1,0},{2,3},{3,2},{4,5},{5,4},{6,7},{7,6},{8,9},{9,8},{10,11... | collective-permute-start | bytes 1671176 | tf_op jit(solution)/shard_map/ppermute | solution.py:478
  63.7 30.2 %middle.1 = (bf16[1024,512]{1,0:T(8,128)(2,1)}, f32[1024,512]{1,0:T(8,128)}, bf16[1024,1024]{1,0:T(8,128)(2,1)}, f32[2,544,256]{2,1,0:T(8,128)}, f32[8,512]{1,0:...) custom-call(s32[1]{0:T(128)} %bitcast.core_ref.half_ref, ...), custom_call_target="tpu_custom_call" | custom-call | tf_op jit(solution)/shard_map/middle/pallas_call | solution.py:779
  101.2 7.5 %scores.4 = (bf16[2,512,512]{2,1,0:T(8,128)(2,1)}, bf16[2,512,2048]{2,1,0:T(8,128)(2,1)}, f32[2,512,512]{2,1,0:T(8,128)}) custom-call(bf16[2,512,512]{2,1,0:T(8,128)(2,1)} %get-tuple-element.210.q_ref, bf16[2,512,1024]{2,1,0:T(8,128)(2,1)} %get-tuple-element.192.v_ref.kv_ref, bf16[2,512,2048]{2,1,0:T(8,128)(2,1)} %get-tuple-element.201.phiq_ref, ...), custom_call_target="tpu_custom_call" | custom-call | tf_op jit(solution)/shard_map/scores/pallas_call | solution.py:719
  116.6 7.2 %scores.5 = (bf16[2,512,512]{2,1,0:T(8,128)(2,1)}, bf16[2,512,2048]{2,1,0:T(8,128)(2,1)}, f32[2,512,512]{2,1,0:T(8,128)}) custom-call(bf16[2,512,512]{2,1,0:T(8,128)(2,1)} %get-tuple-element.210.q_ref, bf16[2,512,1024]{2,1,0:T(8,128)(2,1)} %get-tuple-element.192.v_ref.kv_ref, ...), custom_call_target="tpu_custom_call", output_to_operand_aliasing={{0}: (8, {}), {1}: (9, {}), {2}: (10, {})} | custom-call | tf_op jit(solution)/shard_map/scores/pallas_call | solution.py:719
  126.4 2.9 collective-permute-done.14
  130.3 7.2 %scores.6 = (bf16[2,512,512]{2,1,0:T(8,128)(2,1)}, bf16[2,512,2048]{2,1,0:T(8,128)(2,1)}, f32[2,512,512]{2,1,0:T(8,128)}) custom-call(bf16[2,512,512]{2,1,0:T(8,128)(2,1)} %get-tuple-element.210.q_ref, bf16[2,512,1024]{2,1,0:T(8,128)(2,1)} %get-tuple-element.192.v_ref.kv_ref, ...), custom_call_target="tpu_custom_call", output_to_operand_aliasing={{0}: (8, {}), {1}: (9, {}), {2}: (10, {})} | custom-call | tf_op jit(solution)/shard_map/scores/pallas_call | solution.py:719
  137.5 3.6 %collective-permute-done.10 = f32[2,4,288,128]{3,2,1,0:T(8,128)S(1)} collective-permute-done((f32[2,4,288,128]{3,2,1,0:T(8,128)}, f32[2,4,288,128]{3,2,1,0:T(8,128)S(1)}, u32[]{:S(2)}, u32[]{:S(2)}) %collective-permute-start.10) | collective-permute-done | bytes 1179680 | tf_op jit(solution)/shard_map/ppermute | solution.py:478
  142.0 3.0 bitcast_add_fusion.1
  144.9 7.5 %scores.7 = (bf16[2,512,512]{2,1,0:T(8,128)(2,1)}, bf16[2,512,2048]{2,1,0:T(8,128)(2,1)}, f32[2,512,512]{2,1,0:T(8,128)}) custom-call(bf16[2,512,512]{2,1,0:T(8,128)(2,1)} %get-tuple-element.210.q_ref, bf16[2,512,1024]{2,1,0:T(8,128)(2,1)} %get-tuple-element.192.v_ref.kv_ref, ...), custom_call_target="tpu_custom_call", output_to_operand_aliasing={{0}: (8, {}), {1}: (9, {}), {2}: (10, {})} | custom-call | tf_op jit(solution)/shard_map/scores/pallas_call | solution.py:719
  154.7 3.5 %collective-permute-start.16 = (f32[544,256]{1,0:T(8,128)}, f32[544,256]{1,0:T(8,128)}, u32[]{:S(2)}, u32[]{:S(2)}) collective-permute-start(f32[544,256]{1,0:T(8,128)} %select_add_fusion.1), channel_id=1, source_target_pairs={{0,1},{1,0},{2,3},{3,2},{4,5},{5,4},{6,7},{7,6},{8,9},{9,8},{10,11... | collective-permute-start | bytes 1671176 | tf_op jit(solution)/shard_map/ppermute | solution.py:478
  160.2 4.2 %collective-permute-done.17 = f32[4,288,128]{2,1,0:T(8,128)} collective-permute-done((f32[4,288,128]{2,1,0:T(8,128)}, f32[4,288,128]{2,1,0:T(8,128)}, u32[]{:S(2)}, u32[]{:S(2)}) %collective-permute-start.17) | collective-permute-done | bytes 589856 | tf_op jit(solution)/shard_map/ppermute | solution.py:478
  164.6 2.7 fusion
  175.4 4.4 %final.2 = (bf16[2,512,512]{2,1,0:T(8,128)(2,1)}, bf16[2,512,1536]{2,1,0:T(8,128)(2,1)S(1)}, f32[8,512]{1,0:T(8,128)S(1)}, f32[1,1536]{1,0:T(1,128)S(1)}) custom-call(bf16[2,512,512]{2,1,0:T(8,128)(2,1)S(1)} %copy-done.10, f32[2,512,512]{2,1,0:T(8,128)S(1)} %bitcast.183, bf16[2,512,1024]{2,1,0:T(8,128)(2,1)S(1)} %copy-done.3, ...), custom_call_target="tpu_custom_call" | custom-call | tf_op jit(solution)/shard_map/final/pallas_call | solution.py:809
  179.8 4.4 %final.3 = (bf16[2,512,512]{2,1,0:T(8,128)(2,1)}, bf16[2,512,1536]{2,1,0:T(8,128)(2,1)S(1)}, f32[8,512]{1,0:T(8,128)S(1)}, f32[1,1536]{1,0:T(1,128)S(1)}) custom-call(bf16[2,512,512]{2,1,0:T(8,128)(2,1)S(1)} %copy-done.10, f32[2,512,512]{2,1,0:T(8,128)S(1)} %bitcast.184, ...), custom_call_target="tpu_custom_call", output_to_operand_aliasing={{0}: (12, {}), {1}: (13, {})} | custom-call | tf_op jit(solution)/shard_map/final/pallas_call | solution.py:809
  186.0 7.1 %collective-permute-done.21 = f32[576,128]{1,0:T(8,128)S(1)} collective-permute-done((f32[576,128]{1,0:T(8,128)S(1)}, f32[576,128]{1,0:T(8,128)S(1)}, u32[]{:S(2)}, u32[]{:S(2)}) %collective-permute-start.21) | collective-permute-done | bytes 294944 | tf_op jit(solution)/shard_map/ppermute | solution.py:478
  194.0 4.0 %collective-permute-start.23 = (f32[16,192,128]{2,1,0:T(8,128)S(1)}, f32[16,192,128]{2,1,0:T(8,128)S(1)}, u32[]{:S(2)}, u32[]{:S(2)}) collective-permute-start(f32[16,192,128]{2,1,0:T(8,128)S(1)} %qkv_grads.2), channel_id=1, source_target_pairs={{0,1},{1,0},{2,3},{3,2},{4,5},{5,4},{6,7},{7,6},{8,9},{9,8},{10,11... | collective-permute-start | bytes 4718600 | tf_op jit(solution)/shard_map/ppermute | solution.py:478
  204.9 11.2 %collective-permute-done.26 = f32[52,128]{1,0:T(8,128)S(1)} collective-permute-done((f32[52,128]{1,0:T(8,128)S(1)}, f32[52,128]{1,0:T(8,128)S(1)}, u32[]{:S(2)}, u32[]{:S(2)}) %collective-permute-start.26) | collective-permute-done | bytes 26656 | tf_op jit(solution)/shard_map/ppermute | solution.py:478
  217.4 3.2 %collective-permute-done.29 = f32[52,128]{1,0:T(8,128)S(1)} collective-permute-done((f32[52,128]{1,0:T(8,128)S(1)}, f32[52,128]{1,0:T(8,128)S(1)}, u32[]{:S(2)}, u32[]{:S(2)}) %collective-permute-start.29) | collective-permute-done | bytes 26656 | tf_op jit(solution)/shard_map/ppermute | solution.py:478
  227.0 16.9 %collective-permute-done.33 = f32[52,128]{1,0:T(8,128)S(1)} collective-permute-done((f32[52,128]{1,0:T(8,128)S(1)}, f32[52,128]{1,0:T(8,128)S(1)}, u32[]{:S(2)}, u32[]{:S(2)}) %collective-permute-start.33) | collective-permute-done | bytes 26656 | tf_op jit(solution)/shard_map/ppermute | solution.py:478
  244.1 3.5 %collective-permute-start.35 = (f32[192,128]{1,0:T(8,128)S(1)}, f32[192,128]{1,0:T(8,128)S(1)}, u32[]{:S(2)}, u32[]{:S(2)}) collective-permute-start(f32[192,128]{1,0:T(8,128)S(1)} %fusion.19), channel_id=1, source_target_pairs={{0,8},{1,9},{2,10},{3,11},{4,12},{5,13},{6,14},{7,15},{8,0},{9,1},... | collective-permute-start | bytes 294920 | tf_op jit(solution)/shard_map/ppermute | solution.py:478
  252.9 3.3 %collective-permute-start.39 = (f32[4,96,128]{2,1,0:T(8,128)S(1)}, f32[4,96,128]{2,1,0:T(8,128)S(1)}, u32[]{:S(2)}, u32[]{:S(2)}) collective-permute-start(f32[4,96,128]{2,1,0:T(8,128)S(1)} %get-tuple-element.319), channel_id=1, source_target_pairs={{0,16},{1,17},{2,18},{3,19},{4,20},{5,21},{6,22},{7,23},{8,24},{9,... | collective-permute-start | bytes 589832 | tf_op jit(solution)/shard_map/ppermute | solution.py:478
  256.2 4.7 %collective-permute-done.38 = f32[4,96,128]{2,1,0:T(8,128)S(1)} collective-permute-done((f32[4,96,128]{2,1,0:T(8,128)S(1)}, f32[4,96,128]{2,1,0:T(8,128)S(1)}, u32[]{:S(2)}, u32[]{:S(2)}) %collective-permute-start.38) | collective-permute-done | bytes 196640 | tf_op jit(solution)/shard_map/ppermute | solution.py:478
  267.5 14.0 %collective-permute-done.40.refs_1_ = f32[2,4,96,128]{3,2,1,0:T(8,128)S(1)} collective-permute-done((f32[2,4,96,128]{3,2,1,0:T(8,128)S(1)}, f32[2,4,96,128]{3,2,1,0:T(8,128)S(1)}, u32[]{:S(2)}, u32[]{:S(2)}) %collective-permute-start.40) | collective-permute-done | bytes 393248 | tf_op jit(solution)/shard_map/ppermute | solution.py:478
  281.5 7.3 %collective-permute-start.42 = (f32[2,4,96,128]{3,2,1,0:T(8,128)S(1)}, f32[2,4,96,128]{3,2,1,0:T(8,128)S(1)}, u32[]{:S(2)}, u32[]{:S(2)}) collective-permute-start(f32[2,4,96,128]{3,2,1,0:T(8,128)S(1)} %pad_maximum_fusion.4.refs_0_), channel_id=1, source_target_pairs={{0,1},{1,0},{2,3},{3,2},{4,5},{5,4},{6,7},{7,6},{8,9},{9,8},{10,11... | collective-permute-start | bytes 1179656 | tf_op jit(solution)/shard_map/ppermute | solution.py:478
  297.3 3.7 %copy-done.13 = f32[18432,128]{1,0:T(8,128)S(1)} copy-done((f32[18432,128]{1,0:T(8,128)S(1)}, f32[18432,128]{1,0:T(8,128)}, u32[]{:S(2)}) %copy-start.13) | copy-done | bytes 9437208
  301.0 4.8 %unpack.1 = (f32[2048,512]{1,0:T(8,128)}, f32[512,2048]{1,0:T(8,128)}, f32[512,512]{1,0:T(8,128)}) custom-call(f32[32,576,128]{2,1,0:T(8,128)S(1)} %bitcast.182), custom_call_target="tpu_custom_call" | custom-call | tf_op jit(solution)/shard_map/unpack/pallas_call | solution.py:674
  (200 shorter events, 85.6 us)
Async XLA Ops:
  7.2 290.1 %all-gather.3.cloned.1.call-start = ((), (), s32[]{:S(2)}) async-start(), calls=%async_computation | async-start | bytes 9732096 | tf_op jit(solution)/shard_map/all_gather | solution.py:921
  23.2 7.9 %collective-permute-start.1 = (f32[272,256]{1,0:T(8,128)S(1)}, f32[272,256]{1,0:T(8,128)S(1)}, u32[]{:S(2)}, u32[]{:S(2)}) collective-permute-start(f32[272,256]{1,0:T(8,128)S(1)} %constant_dynamic-slice_fusion.4), channel_id=1, source_target_pairs={{0,2},{1,3},{2,0},{3,1},{4,6},{5,7},{6,4},{7,5},{8,10},{9,11},{10,... | collective-permute-start | bytes 835592 | tf_op jit(solution)/shard_map/ppermute | solution.py:478
  35.2 9.9 %collective-permute-start.3 = (f32[136,256]{1,0:T(8,128)S(1)}, f32[136,256]{1,0:T(8,128)S(1)}, u32[]{:S(2)}, u32[]{:S(2)}) collective-permute-start(f32[136,256]{1,0:T(8,128)S(1)} %dynamic-slice_add_fusion.5), channel_id=1, source_target_pairs={{0,8},{1,9},{2,10},{3,11},{4,12},{5,13},{6,14},{7,15},{8,0},{9,1},... | collective-permute-start | bytes 417800 | tf_op jit(solution)/shard_map/ppermute | solution.py:478
  49.2 5.9 %collective-permute-start.5 = (f32[272,256]{1,0:T(8,128)S(1)}, f32[272,256]{1,0:T(8,128)}, u32[]{:S(2)}, u32[]{:S(2)}) collective-permute-start(f32[272,256]{1,0:T(8,128)S(1)} %select_add_fusion.6), channel_id=1, source_target_pairs={{0,2},{1,3},{2,0},{3,1},{4,6},{5,7},{6,4},{7,5},{8,10},{9,11},{10,... | collective-permute-start | bytes 835592 | tf_op jit(solution)/shard_map/ppermute | solution.py:478
  56.2 6.2 %collective-permute-start.6 = (f32[544,256]{1,0:T(8,128)S(1)}, f32[544,256]{1,0:T(8,128)S(1)}, u32[]{:S(2)}, u32[]{:S(2)}) collective-permute-start(f32[544,256]{1,0:T(8,128)S(1)} %select_add_fusion.2), channel_id=1, source_target_pairs={{0,1},{1,0},{2,3},{3,2},{4,5},{5,4},{6,7},{7,6},{8,9},{9,8},{10,11... | collective-permute-start | bytes 1671176 | tf_op jit(solution)/shard_map/ppermute | solution.py:478
  99.1 9.7 %collective-permute-start.9 = (f32[16,576,128]{2,1,0:T(8,128)}, f32[16,576,128]{2,1,0:T(8,128)}, u32[]{:S(2)}, u32[]{:S(2)}) collective-permute-start(f32[16,576,128]{2,1,0:T(8,128)} %get-tuple-element.209), channel_id=1, source_target_pairs={{0,1},{1,0},{2,3},{3,2},{4,5},{5,4},{6,7},{7,6},{8,9},{9,8},{10,11... | collective-permute-start | bytes 14155784 | tf_op jit(solution)/shard_map/ppermute | solution.py:478
  99.5 9.3 %collective-permute-start.8 = (f32[272,256]{1,0:T(8,128)S(1)}, f32[272,256]{1,0:T(8,128)S(1)}, u32[]{:S(2)}, u32[]{:S(2)}) collective-permute-start(f32[272,256]{1,0:T(8,128)S(1)} %constant_dynamic-slice_fusion.1), channel_id=1, source_target_pairs={{0,2},{1,3},{2,0},{3,1},{4,6},{5,7},{6,4},{7,5},{8,10},{9,11},{10,... | collective-permute-start | bytes 835592 | tf_op jit(solution)/shard_map/ppermute | solution.py:478
  108.9 6.8 %collective-permute-start.12 = (f32[136,256]{1,0:T(8,128)S(1)}, f32[136,256]{1,0:T(8,128)S(1)}, u32[]{:S(2)}, u32[]{:S(2)}) collective-permute-start(f32[136,256]{1,0:T(8,128)S(1)} %constant_dynamic-slice_fusion), channel_id=1, source_target_pairs={{0,4},{1,5},{2,6},{3,7},{4,0},{5,1},{6,2},{7,3},{8,12},{9,13},{10,... | collective-permute-start | bytes 417800 | tf_op jit(solution)/shard_map/ppermute | solution.py:478
  114.0 27.1 %collective-permute-start.10 = (f32[2,4,288,128]{3,2,1,0:T(8,128)}, f32[2,4,288,128]{3,2,1,0:T(8,128)S(1)}, u32[]{:S(2)}, u32[]{:S(2)}) collective-permute-start(f32[2,4,288,128]{3,2,1,0:T(8,128)} %add_bitcast_fusion.1), channel_id=1, source_target_pairs={{0,16},{1,17},{2,18},{3,19},{4,20},{5,21},{6,22},{7,23},{8,24},{9,... | collective-permute-start | bytes 3538952 | tf_op jit(solution)/shard_map/ppermute | solution.py:478
  115.2 26.8 %collective-permute-start.11 = (f32[2,4,288,128]{3,2,1,0:T(8,128)}, f32[2,4,288,128]{3,2,1,0:T(8,128)}, u32[]{:S(2)}, u32[]{:S(2)}) collective-permute-start(f32[2,4,288,128]{3,2,1,0:T(8,128)} %add_bitcast_fusion), channel_id=1, source_target_pairs={{0,2},{1,3},{2,0},{3,1},{4,6},{5,7},{6,4},{7,5},{8,10},{9,11},{10,... | collective-permute-start | bytes 3538952 | tf_op jit(solution)/shard_map/ppermute | solution.py:478
  115.7 8.2 %collective-permute-start.13 = (f32[136,256]{1,0:T(8,128)S(1)}, f32[136,256]{1,0:T(8,128)S(1)}, u32[]{:S(2)}, u32[]{:S(2)}) collective-permute-start(f32[136,256]{1,0:T(8,128)S(1)} %dynamic-slice_add_fusion.4), channel_id=1, source_target_pairs={{0,8},{1,9},{2,10},{3,11},{4,12},{5,13},{6,14},{7,15},{8,0},{9,1},... | collective-permute-start | bytes 417800 | tf_op jit(solution)/shard_map/ppermute | solution.py:478
  129.3 23.2 %collective-permute-start.15 = (f32[272,256]{1,0:T(8,128)S(1)}, f32[272,256]{1,0:T(8,128)S(1)}, u32[]{:S(2)}, u32[]{:S(2)}) collective-permute-start(f32[272,256]{1,0:T(8,128)S(1)} %select_add_fusion.5), channel_id=1, source_target_pairs={{0,2},{1,3},{2,0},{3,1},{4,6},{5,7},{6,4},{7,5},{8,10},{9,11},{10,... | collective-permute-start | bytes 835592 | tf_op jit(solution)/shard_map/ppermute | solution.py:478
  152.6 11.8 %collective-permute-start.17 = (f32[4,288,128]{2,1,0:T(8,128)}, f32[4,288,128]{2,1,0:T(8,128)}, u32[]{:S(2)}, u32[]{:S(2)}) collective-permute-start(f32[4,288,128]{2,1,0:T(8,128)} %get-tuple-element.255), channel_id=1, source_target_pairs={{0,2},{1,3},{2,0},{3,1},{4,6},{5,7},{6,4},{7,5},{8,10},{9,11},{10,... | collective-permute-start | bytes 1769480 | tf_op jit(solution)/shard_map/ppermute | solution.py:478
  153.1 11.4 %collective-permute-start.18 = (f32[4,288,128]{2,1,0:T(8,128)}, f32[4,288,128]{2,1,0:T(8,128)}, u32[]{:S(2)}, u32[]{:S(2)}) collective-permute-start(f32[4,288,128]{2,1,0:T(8,128)} %get-tuple-element.256), channel_id=1, source_target_pairs={{0,16},{1,17},{2,18},{3,19},{4,20},{5,21},{6,22},{7,23},{8,24},{9,... | collective-permute-start | bytes 1769480 | tf_op jit(solution)/shard_map/ppermute | solution.py:478
  154.7 5.4 %collective-permute-start.16 = (f32[544,256]{1,0:T(8,128)}, f32[544,256]{1,0:T(8,128)}, u32[]{:S(2)}, u32[]{:S(2)}) collective-permute-start(f32[544,256]{1,0:T(8,128)} %select_add_fusion.1), channel_id=1, source_target_pairs={{0,1},{1,0},{2,3},{3,2},{4,5},{5,4},{6,7},{7,6},{8,9},{9,8},{10,11... | collective-permute-start | bytes 1671176 | tf_op jit(solution)/shard_map/ppermute | solution.py:478
  167.3 18.6 %collective-permute-start.19 = (f32[576,128]{1,0:T(8,128)S(1)}, f32[576,128]{1,0:T(8,128)S(1)}, u32[]{:S(2)}, u32[]{:S(2)}) collective-permute-start(f32[576,128]{1,0:T(8,128)S(1)} %get-tuple-element.260), channel_id=1, source_target_pairs={{0,4},{1,5},{2,6},{3,7},{4,0},{5,1},{6,2},{7,3},{8,12},{9,13},{10,... | collective-permute-start | bytes 884744 | tf_op jit(solution)/shard_map/ppermute | solution.py:478
  168.7 17.3 %collective-permute-start.20 = (f32[576,128]{1,0:T(8,128)S(1)}, f32[576,128]{1,0:T(8,128)S(1)}, u32[]{:S(2)}, u32[]{:S(2)}) collective-permute-start(f32[576,128]{1,0:T(8,128)S(1)} %get-tuple-element.261), channel_id=1, source_target_pairs={{0,8},{1,9},{2,10},{3,11},{4,12},{5,13},{6,14},{7,15},{8,0},{9,1},... | collective-permute-start | bytes 884744 | tf_op jit(solution)/shard_map/ppermute | solution.py:478
  169.7 23.4 %collective-permute-start.21 = (f32[576,128]{1,0:T(8,128)S(1)}, f32[576,128]{1,0:T(8,128)S(1)}, u32[]{:S(2)}, u32[]{:S(2)}) collective-permute-start(f32[576,128]{1,0:T(8,128)S(1)} %get-tuple-element.262), channel_id=1, source_target_pairs={{0,12},{1,13},{2,14},{3,15},{4,8},{5,9},{6,10},{7,11},{8,4},{9,5},... | collective-permute-start | bytes 884744 | tf_op jit(solution)/shard_map/ppermute | solution.py:478
  194.0 8.0 %collective-permute-start.23 = (f32[16,192,128]{2,1,0:T(8,128)S(1)}, f32[16,192,128]{2,1,0:T(8,128)S(1)}, u32[]{:S(2)}, u32[]{:S(2)}) collective-permute-start(f32[16,192,128]{2,1,0:T(8,128)S(1)} %qkv_grads.2), channel_id=1, source_target_pairs={{0,1},{1,0},{2,3},{3,2},{4,5},{5,4},{6,7},{7,6},{8,9},{9,8},{10,11... | collective-permute-start | bytes 4718600 | tf_op jit(solution)/shard_map/ppermute | solution.py:478
  202.1 14.0 %collective-permute-start.24 = (f32[2,4,96,128]{3,2,1,0:T(8,128)S(1)}, f32[2,4,96,128]{3,2,1,0:T(8,128)S(1)}, u32[]{:S(2)}, u32[]{:S(2)}) collective-permute-start(f32[2,4,96,128]{3,2,1,0:T(8,128)S(1)} %add_bitcast_fusion.3), channel_id=1, source_target_pairs={{0,16},{1,17},{2,18},{3,19},{4,20},{5,21},{6,22},{7,23},{8,24},{9,... | collective-permute-start | bytes 1179656 | tf_op jit(solution)/shard_map/ppermute | solution.py:478
  203.4 12.7 %collective-permute-start.25 = (f32[2,4,96,128]{3,2,1,0:T(8,128)S(1)}, f32[2,4,96,128]{3,2,1,0:T(8,128)S(1)}, u32[]{:S(2)}, u32[]{:S(2)}) collective-permute-start(f32[2,4,96,128]{3,2,1,0:T(8,128)S(1)} %add_bitcast_fusion.2), channel_id=1, source_target_pairs={{0,2},{1,3},{2,0},{3,1},{4,6},{5,7},{6,4},{7,5},{8,10},{9,11},{10,... | collective-permute-start | bytes 1179656 | tf_op jit(solution)/shard_map/ppermute | solution.py:478
  204.4 11.7 %collective-permute-start.26 = (f32[52,128]{1,0:T(8,128)S(1)}, f32[52,128]{1,0:T(8,128)S(1)}, u32[]{:S(2)}, u32[]{:S(2)}) collective-permute-start(f32[52,128]{1,0:T(8,128)S(1)} %fusion.27), channel_id=1, source_target_pairs={{0,2},{1,3},{2,0},{3,1},{4,6},{5,7},{6,4},{7,5},{8,10},{9,11},{10,... | collective-permute-start | bytes 79880 | tf_op jit(solution)/shard_map/ppermute | solution.py:478
  222.2 21.7 %collective-permute-start.30 = (f32[192,128]{1,0:T(8,128)S(1)}, f32[192,128]{1,0:T(8,128)S(1)}, u32[]{:S(2)}, u32[]{:S(2)}) collective-permute-start(f32[192,128]{1,0:T(8,128)S(1)} %get-tuple-element.302), channel_id=1, source_target_pairs={{0,4},{1,5},{2,6},{3,7},{4,0},{5,1},{6,2},{7,3},{8,12},{9,13},{10,... | collective-permute-start | bytes 294920 | tf_op jit(solution)/shard_map/ppermute | solution.py:478
  222.2 21.6 %collective-permute-start.31 = (f32[192,128]{1,0:T(8,128)S(1)}, f32[192,128]{1,0:T(8,128)S(1)}, u32[]{:S(2)}, u32[]{:S(2)}) collective-permute-start(f32[192,128]{1,0:T(8,128)S(1)} %get-tuple-element.303), channel_id=1, source_target_pairs={{0,8},{1,9},{2,10},{3,11},{4,12},{5,13},{6,14},{7,15},{8,0},{9,1},... | collective-permute-start | bytes 294920 | tf_op jit(solution)/shard_map/ppermute | solution.py:478
  224.8 19.1 %collective-permute-start.32 = (f32[192,128]{1,0:T(8,128)S(1)}, f32[192,128]{1,0:T(8,128)S(1)}, u32[]{:S(2)}, u32[]{:S(2)}) collective-permute-start(f32[192,128]{1,0:T(8,128)S(1)} %get-tuple-element.304), channel_id=1, source_target_pairs={{0,12},{1,13},{2,14},{3,15},{4,8},{5,9},{6,10},{7,11},{8,4},{9,5},... | collective-permute-start | bytes 294920 | tf_op jit(solution)/shard_map/ppermute | solution.py:478
  224.9 19.0 %collective-permute-start.33 = (f32[52,128]{1,0:T(8,128)S(1)}, f32[52,128]{1,0:T(8,128)S(1)}, u32[]{:S(2)}, u32[]{:S(2)}) collective-permute-start(f32[52,128]{1,0:T(8,128)S(1)} %add.517), channel_id=1, source_target_pairs={{0,8},{1,9},{2,10},{3,11},{4,12},{5,13},{6,14},{7,15},{8,0},{9,1},... | collective-permute-start | bytes 79880 | tf_op jit(solution)/shard_map/ppermute | solution.py:478
  244.1 6.6 %collective-permute-start.35 = (f32[192,128]{1,0:T(8,128)S(1)}, f32[192,128]{1,0:T(8,128)S(1)}, u32[]{:S(2)}, u32[]{:S(2)}) collective-permute-start(f32[192,128]{1,0:T(8,128)S(1)} %fusion.19), channel_id=1, source_target_pairs={{0,8},{1,9},{2,10},{3,11},{4,12},{5,13},{6,14},{7,15},{8,0},{9,1},... | collective-permute-start | bytes 294920 | tf_op jit(solution)/shard_map/ppermute | solution.py:478
  252.3 8.5 %collective-permute-start.38 = (f32[4,96,128]{2,1,0:T(8,128)S(1)}, f32[4,96,128]{2,1,0:T(8,128)S(1)}, u32[]{:S(2)}, u32[]{:S(2)}) collective-permute-start(f32[4,96,128]{2,1,0:T(8,128)S(1)} %get-tuple-element.318), channel_id=1, source_target_pairs={{0,2},{1,3},{2,0},{3,1},{4,6},{5,7},{6,4},{7,5},{8,10},{9,11},{10,... | collective-permute-start | bytes 589832 | tf_op jit(solution)/shard_map/ppermute | solution.py:478
  252.9 10.7 %collective-permute-start.39 = (f32[4,96,128]{2,1,0:T(8,128)S(1)}, f32[4,96,128]{2,1,0:T(8,128)S(1)}, u32[]{:S(2)}, u32[]{:S(2)}) collective-permute-start(f32[4,96,128]{2,1,0:T(8,128)S(1)} %get-tuple-element.319), channel_id=1, source_target_pairs={{0,16},{1,17},{2,18},{3,19},{4,20},{5,21},{6,22},{7,23},{8,24},{9,... | collective-permute-start | bytes 589832 | tf_op jit(solution)/shard_map/ppermute | solution.py:478
  263.6 17.9 %collective-permute-start.40 = (f32[2,4,96,128]{3,2,1,0:T(8,128)S(1)}, f32[2,4,96,128]{3,2,1,0:T(8,128)S(1)}, u32[]{:S(2)}, u32[]{:S(2)}) collective-permute-start(f32[2,4,96,128]{3,2,1,0:T(8,128)S(1)} %pad_maximum_fusion.4.refs_0_), channel_id=1, source_target_pairs={{0,16},{1,17},{2,18},{3,19},{4,20},{5,21},{6,22},{7,23},{8,24},{9,... | collective-permute-start | bytes 1179656 | tf_op jit(solution)/shard_map/ppermute | solution.py:478
  265.4 16.1 %collective-permute-start.41 = (f32[2,4,96,128]{3,2,1,0:T(8,128)S(1)}, f32[2,4,96,128]{3,2,1,0:T(8,128)S(1)}, u32[]{:S(2)}, u32[]{:S(2)}) collective-permute-start(f32[2,4,96,128]{3,2,1,0:T(8,128)S(1)} %pad_maximum_fusion.5.refs_2_), channel_id=1, source_target_pairs={{0,2},{1,3},{2,0},{3,1},{4,6},{5,7},{6,4},{7,5},{8,10},{9,11},{10,... | collective-permute-start | bytes 1179656 | tf_op jit(solution)/shard_map/ppermute | solution.py:478
  281.5 9.1 %collective-permute-start.42 = (f32[2,4,96,128]{3,2,1,0:T(8,128)S(1)}, f32[2,4,96,128]{3,2,1,0:T(8,128)S(1)}, u32[]{:S(2)}, u32[]{:S(2)}) collective-permute-start(f32[2,4,96,128]{3,2,1,0:T(8,128)S(1)} %pad_maximum_fusion.4.refs_0_), channel_id=1, source_target_pairs={{0,1},{1,0},{2,3},{3,2},{4,5},{5,4},{6,7},{7,6},{8,9},{9,8},{10,11... | collective-permute-start | bytes 1179656 | tf_op jit(solution)/shard_map/ppermute | solution.py:478
  (41 other events, 206.5 us)
Sparse Core Ops, SparseCore 0:
  194.0 103.3 all-gather.2

commit v5 on v4

--- a/solution.py
+++ b/solution.py
@@ -103,7 +103,7 @@
     unit, _ = normalise(x_ref[0].astype(F32))
     low = (unit * gain_ref[...] + shift_ref[...]).astype(BF)
     h_ref[0] = low
-    kv_ref[0] = (dot(low, w_ref[:, width:]) + b_ref[:, width:]).astype(BF)
+    kv_ref[0] = (dot(low, w_ref[:, width:]) + b_ref[...][None, width:]).astype(BF)
     tabs = (tab_ref[0], tab_ref[1])
     norms = []
     for pair in range(PAIRS):
@@ -745,7 +745,7 @@
         grid=(seqs,),
         in_specs=[
             three((span, width)), whole((1, width)), whole((1, width)), whole((width, 3 * width)),
-            whole((1, 3 * width)), whole((2, FEATS, 2 * LANES)),
+            whole((3 * width,)), whole((2, FEATS, 2 * LANES)),
         ],
         out_specs=[
             three((span, width)), three((span, 2 * width)), three((span, HEADS * FEATS)), three((SCAN_ROWS, FEATS)),
@@ -844,7 +844,7 @@
     row = lambda a: a.reshape(1, -1)
     seq_bits = axis_bits("c") + axis_bits("y") + axis_bits("z")
 
-    h1, kv, phi_k, state = run_keys(tokens, row(gain_attn), row(shift_attn), w_qkv, row(b_qkv), tab_in)
+    h1, kv, phi_k, state = run_keys(tokens, row(gain_attn), row(shift_attn), w_qkv, b_qkv, tab_in)
 
     scan = Stream(scan_stream(state.reshape(seqs * SCAN_ROWS, FEATS), seq_bits, len(seq_bits) - 1, False))
     phase([scan], [scan])
@@ -888,9 +888,8 @@
         phase([ffn], [scan])
         old = phase([scan], [scan], back(0, half_pairs, half_pairs), (dnum,) + tuple(old))
         phase([scan], [scan])
-        old = phase([scan], [ffn], back(1, 0, half_pairs), (dnum,) + tuple(old))
-        old = phase([ffn], [scan], back(1, half_pairs, half_pairs), (dnum,) + tuple(old))
-        phase([scan], [scan, ffn])
+        old = phase([scan], [scan, ffn], back(1, 0, half_pairs), (dnum,) + tuple(old))
+        old = phase([scan, ffn], [scan, ffn], back(1, half_pairs, half_pairs), (dnum,) + tuple(old))
         later = scan.value
     else:
         old = phase([scan], [scan], back(0, 0, PAIRS), (dnum,))

time: 319 us -> 317 us (level)
  waiting for transfers between devices: 99.9 us -> 110 us
  starting transfers between devices: 57.8 us -> 48.8 us
    ppermute x46, starting transfers between devices: 57.8 us -> 48.8 us  [send(): return lax.ppermute(values, AXES, [(i, i ^ mask) for i in range(count)])]
    ppermute x46, waiting for transfers between devices: 97.4 us -> 104 us  [send(): return lax.ppermute(values, AXES, [(i, i ^ mask) for i in range(count)])]
    all_gather x1, waiting for transfers between devices: 2.47 us -> 5.74 us  [shards(): packed = lax.all_gather(ffn.value, ('c', 'x', 'y', 'z'))]
    unnamed x55 -> x51, local copies, waits for them, and re-layouts: 10.4 us -> 9.64 us
  transfers between devices with their start and end apart: 47 -> 47, of which waited for: 28 -> 23; matrix products, arithmetic and copies ran while one was open for 4% -> 3% of each run, Pallas kernels for 19% -> 19%
where the time goes in v5:
time: 317 us; the launch traced here: 311 us
  waiting for transfers between devices  110 us (35%)
  Pallas kernels  103 us (32%)
  starting transfers between devices  48.8 us (15%)
  other arithmetic  19.4 us (6%)
  between operations  15.8 us (5%)
  local copies, waits for them, and re-layouts  14.6 us (5%)
    ppermute x46, waiting for transfers between devices, send(): return lax.ppermute(values, AXES, [(i, i ^ mask) for i in range(count)])  104 us
    ppermute x46, starting transfers between devices, send(): return lax.ppermute(values, AXES, [(i, i ^ mask) for i in range(count)])  48.8 us
    pallas_call x1, Pallas kernels, run_middle(): pl.pallas_call(functools.partial(middle_kernel, per, chips), grid_spec=pl...  30.2 us
    pallas_call x4, Pallas kernels, run_scores(): pl.pallas_call(functools.partial(score_back_kernel, first), grid=(count,)...  29.5 us
    pallas_call x2, Pallas kernels, run_local(): pl.pallas_call(local_kernel, grid=(PAIRS,), in_specs=[pl.BlockSpec((1, sp...  15.1 us
    add x10, other arithmetic, add_all(): return functools.reduce(jnp.add, items)  11.3 us
    unnamed x51, local copies, waits for them, and re-layouts  9.64 us
    pallas_call x2, Pallas kernels, run_final(): pl.pallas_call(final_kernel, grid=(1,), in_specs=[three((span, width)), t...  8.81 us
  transfers between devices with their start and end apart: 47, of which 23 were waited for; matrix products, arithmetic and copies ran while one was open for 3% of the time, Pallas kernels for 19%

profile of v5, /device:TPU:13, one launch (start us, length us, event | category | flops | bytes accessed | tf_op | source)
XLA Modules:
  0.0 311.0 jit_solution(11978631098024987343)
XLA Ops:
  9.1 8.4 %keys.1 = (bf16[2,512,512]{2,1,0:T(8,128)(2,1)}, bf16[2,512,1024]{2,1,0:T(8,128)(2,1)}, bf16[2,512,2048]{2,1,0:T(8,128)(2,1)}, f32[2,544,256]{2,1,0:T(8,128)}) custom-call(bf16[2,512,512]{2,1,0:T(8,128)(2,1)} %x_ref.5, f32[1,512]{1,0:T(1,128)} %bitcast.189, f32[1,512]{1,0:T(1,128)} %bitcast.192, bf16[512,1536]{1,0:T(8,128)(2,1)} %w_ref.9, f32[1536]{0:T(1024)} %b_ref.1, ...), custom_call_target="tpu_custom_call" | custom-call | tf_op jit(solution)/shard_map/keys/pallas_call | solution.py:743
  22.9 7.6 %local.2 = (bf16[2,512,512]{2,1,0:T(8,128)(2,1)}, bf16[2,512,2048]{2,1,0:T(8,128)(2,1)}, f32[2,512,1024]{2,1,0:T(8,128)}) custom-call(bf16[2,512,512]{2,1,0:T(8,128)(2,1)} %get-tuple-element.182.h_ref, bf16[512,1536]{1,0:T(8,128)(2,1)} %w_ref.9, f32[1,1536]{1,0:T(1,128)} %reshape.203.b_ref, bf16[2,512,1024]{2,1,0:T(8,128)(2,1)} %get-tuple-element.193.v_ref.kv_ref, ...), custom_call_target="tpu_custom_call" | custom-call | tf_op jit(solution)/shard_map/local/pallas_call | solution.py:696
  30.6 4.5 %collective-permute-done.2 = f32[136,256]{1,0:T(8,128)S(1)} collective-permute-done((f32[136,256]{1,0:T(8,128)S(1)}, f32[136,256]{1,0:T(8,128)S(1)}, u32[]{:S(2)}, u32[]{:S(2)}) %collective-permute-start.2) | collective-permute-done | bytes 139296 | tf_op jit(solution)/shard_map/ppermute | solution.py:478
  37.6 7.5 %local.3 = (bf16[2,512,512]{2,1,0:T(8,128)(2,1)}, bf16[2,512,2048]{2,1,0:T(8,128)(2,1)}, f32[2,512,1024]{2,1,0:T(8,128)}) custom-call(bf16[2,512,512]{2,1,0:T(8,128)(2,1)} %get-tuple-element.182.h_ref, bf16[512,1536]{1,0:T(8,128)(2,1)} %w_ref.9, f32[1,1536]{1,0:T(1,128)} %reshape.203.b_ref, ...), custom_call_target="tpu_custom_call", output_to_operand_aliasing={{0}: (6, {}), {1}: (7, {}), {2}: (8, {})} | custom-call | tf_op jit(solution)/shard_map/local/pallas_call | solution.py:696
  45.3 3.8 %collective-permute-done.4 = f32[136,256]{1,0:T(8,128)S(1)} collective-permute-done((f32[136,256]{1,0:T(8,128)S(1)}, f32[136,256]{1,0:T(8,128)S(1)}, u32[]{:S(2)}, u32[]{:S(2)}) %collective-permute-start.4) | collective-permute-done | bytes 139296 | tf_op jit(solution)/shard_map/ppermute | solution.py:478
  50.5 4.2 %collective-permute-done.5 = f32[272,256]{1,0:T(8,128)S(1)} collective-permute-done((f32[272,256]{1,0:T(8,128)S(1)}, f32[272,256]{1,0:T(8,128)S(1)}, u32[]{:S(2)}, u32[]{:S(2)}) %collective-permute-start.5) | collective-permute-done | bytes 278560 | tf_op jit(solution)/shard_map/ppermute | solution.py:478
  54.8 4.2 %collective-permute-start.6 = (f32[544,256]{1,0:T(8,128)S(1)}, f32[544,256]{1,0:T(8,128)S(1)}, u32[]{:S(2)}, u32[]{:S(2)}) collective-permute-start(f32[544,256]{1,0:T(8,128)S(1)} %select_add_fusion.2), channel_id=1, source_target_pairs={{0,1},{1,0},{2,3},{3,2},{4,5},{5,4},{6,7},{7,6},{8,9},{9,8},{10,11... | collective-permute-start | bytes 1671176 | tf_op jit(solution)/shard_map/ppermute | solution.py:478
  61.8 30.2 %middle.1 = (bf16[1024,512]{1,0:T(8,128)(2,1)}, f32[1024,512]{1,0:T(8,128)}, bf16[1024,1024]{1,0:T(8,128)(2,1)}, f32[2,544,256]{2,1,0:T(8,128)}, f32[8,512]{1,0:...) custom-call(s32[1]{0:T(128)} %bitcast.core_ref.half_ref, ...), custom_call_target="tpu_custom_call" | custom-call | tf_op jit(solution)/shard_map/middle/pallas_call | solution.py:779
  98.7 7.5 %scores.4 = (bf16[2,512,512]{2,1,0:T(8,128)(2,1)}, bf16[2,512,2048]{2,1,0:T(8,128)(2,1)}, f32[2,512,512]{2,1,0:T(8,128)}) custom-call(bf16[2,512,512]{2,1,0:T(8,128)(2,1)} %get-tuple-element.211.q_ref, bf16[2,512,1024]{2,1,0:T(8,128)(2,1)} %get-tuple-element.193.v_ref.kv_ref, bf16[2,512,2048]{2,1,0:T(8,128)(2,1)} %get-tuple-element.202.phiq_ref, ...), custom_call_target="tpu_custom_call" | custom-call | tf_op jit(solution)/shard_map/scores/pallas_call | solution.py:719
  114.3 7.2 %scores.5 = (bf16[2,512,512]{2,1,0:T(8,128)(2,1)}, bf16[2,512,2048]{2,1,0:T(8,128)(2,1)}, f32[2,512,512]{2,1,0:T(8,128)}) custom-call(bf16[2,512,512]{2,1,0:T(8,128)(2,1)} %get-tuple-element.211.q_ref, bf16[2,512,1024]{2,1,0:T(8,128)(2,1)} %get-tuple-element.193.v_ref.kv_ref, ...), custom_call_target="tpu_custom_call", output_to_operand_aliasing={{0}: (8, {}), {1}: (9, {}), {2}: (10, {})} | custom-call | tf_op jit(solution)/shard_map/scores/pallas_call | solution.py:719
  123.4 2.8 collective-permute-done.12
  127.8 7.2 %scores.6 = (bf16[2,512,512]{2,1,0:T(8,128)(2,1)}, bf16[2,512,2048]{2,1,0:T(8,128)(2,1)}, f32[2,512,512]{2,1,0:T(8,128)}) custom-call(bf16[2,512,512]{2,1,0:T(8,128)(2,1)} %get-tuple-element.211.q_ref, bf16[2,512,1024]{2,1,0:T(8,128)(2,1)} %get-tuple-element.193.v_ref.kv_ref, ...), custom_call_target="tpu_custom_call", output_to_operand_aliasing={{0}: (8, {}), {1}: (9, {}), {2}: (10, {})} | custom-call | tf_op jit(solution)/shard_map/scores/pallas_call | solution.py:719
  135.0 10.3 %collective-permute-done.13 = f32[272,256]{1,0:T(8,128)S(1)} collective-permute-done((f32[272,256]{1,0:T(8,128)S(1)}, f32[272,256]{1,0:T(8,128)S(1)}, u32[]{:S(2)}, u32[]{:S(2)}) %collective-permute-start.13) | collective-permute-done | bytes 278560 | tf_op jit(solution)/shard_map/ppermute | solution.py:478
  146.3 2.8 bitcast_add_fusion.1
  149.4 2.6 collective-permute-start.16
  152.1 7.6 %scores.7 = (bf16[2,512,512]{2,1,0:T(8,128)(2,1)}, bf16[2,512,2048]{2,1,0:T(8,128)(2,1)}, f32[2,512,512]{2,1,0:T(8,128)}) custom-call(bf16[2,512,512]{2,1,0:T(8,128)(2,1)} %get-tuple-element.211.q_ref, bf16[2,512,1024]{2,1,0:T(8,128)(2,1)} %get-tuple-element.193.v_ref.kv_ref, ...), custom_call_target="tpu_custom_call", output_to_operand_aliasing={{0}: (8, {}), {1}: (9, {}), {2}: (10, {})} | custom-call | tf_op jit(solution)/shard_map/scores/pallas_call | solution.py:719
  159.7 2.7 collective-permute-done.17
  173.1 4.4 %final.2 = (bf16[2,512,512]{2,1,0:T(8,128)(2,1)}, bf16[2,512,1536]{2,1,0:T(8,128)(2,1)S(1)}, f32[8,512]{1,0:T(8,128)S(1)}, f32[1,1536]{1,0:T(1,128)S(1)}) custom-call(bf16[2,512,512]{2,1,0:T(8,128)(2,1)S(1)} %copy-done.10, f32[2,512,512]{2,1,0:T(8,128)S(1)} %bitcast.183, bf16[2,512,1024]{2,1,0:T(8,128)(2,1)S(1)} %copy-done.3, ...), custom_call_target="tpu_custom_call" | custom-call | tf_op jit(solution)/shard_map/final/pallas_call | solution.py:809
  177.5 4.4 %final.3 = (bf16[2,512,512]{2,1,0:T(8,128)(2,1)}, bf16[2,512,1536]{2,1,0:T(8,128)(2,1)S(1)}, f32[8,512]{1,0:T(8,128)S(1)}, f32[1,1536]{1,0:T(1,128)S(1)}) custom-call(bf16[2,512,512]{2,1,0:T(8,128)(2,1)S(1)} %copy-done.10, f32[2,512,512]{2,1,0:T(8,128)S(1)} %bitcast.184, ...), custom_call_target="tpu_custom_call", output_to_operand_aliasing={{0}: (12, {}), {1}: (13, {})} | custom-call | tf_op jit(solution)/shard_map/final/pallas_call | solution.py:809
  183.6 7.2 %collective-permute-done.21 = f32[576,128]{1,0:T(8,128)S(1)} collective-permute-done((f32[576,128]{1,0:T(8,128)S(1)}, f32[576,128]{1,0:T(8,128)S(1)}, u32[]{:S(2)}, u32[]{:S(2)}) %collective-permute-start.21) | collective-permute-done | bytes 294944 | tf_op jit(solution)/shard_map/ppermute | solution.py:478
  191.7 3.9 %collective-permute-start.23 = (f32[16,192,128]{2,1,0:T(8,128)S(1)}, f32[16,192,128]{2,1,0:T(8,128)S(1)}, u32[]{:S(2)}, u32[]{:S(2)}) collective-permute-start(f32[16,192,128]{2,1,0:T(8,128)S(1)} %qkv_grads.2), channel_id=1, source_target_pairs={{0,1},{1,0},{2,3},{3,2},{4,5},{5,4},{6,7},{7,6},{8,9},{9,8},{10,11... | collective-permute-start | bytes 4718600 | tf_op jit(solution)/shard_map/ppermute | solution.py:478
  201.2 11.3 %collective-permute-done.26 = f32[52,128]{1,0:T(8,128)S(1)} collective-permute-done((f32[52,128]{1,0:T(8,128)S(1)}, f32[52,128]{1,0:T(8,128)S(1)}, u32[]{:S(2)}, u32[]{:S(2)}) %collective-permute-start.26) | collective-permute-done | bytes 26656 | tf_op jit(solution)/shard_map/ppermute | solution.py:478
  214.8 3.0 collective-permute-done.29
  223.3 16.3 %collective-permute-done.33 = f32[52,128]{1,0:T(8,128)S(1)} collective-permute-done((f32[52,128]{1,0:T(8,128)S(1)}, f32[52,128]{1,0:T(8,128)S(1)}, u32[]{:S(2)}, u32[]{:S(2)}) %collective-permute-start.33) | collective-permute-done | bytes 26656 | tf_op jit(solution)/shard_map/ppermute | solution.py:478
  241.0 3.9 %collective-permute-start.35 = (f32[192,128]{1,0:T(8,128)S(1)}, f32[192,128]{1,0:T(8,128)S(1)}, u32[]{:S(2)}, u32[]{:S(2)}) collective-permute-start(f32[192,128]{1,0:T(8,128)S(1)} %fusion.19), channel_id=1, source_target_pairs={{0,8},{1,9},{2,10},{3,11},{4,12},{5,13},{6,14},{7,15},{8,0},{9,1},... | collective-permute-start | bytes 294920 | tf_op jit(solution)/shard_map/ppermute | solution.py:478
  248.1 3.8 %collective-permute-done.36 = f32[192,128]{1,0:T(8,128)S(1)} collective-permute-done((f32[192,128]{1,0:T(8,128)S(1)}, f32[192,128]{1,0:T(8,128)S(1)}, u32[]{:S(2)}, u32[]{:S(2)}) %collective-permute-start.36) | collective-permute-done | bytes 98336 | tf_op jit(solution)/shard_map/ppermute | solution.py:478
  252.1 9.0 %collective-permute-done.38 = f32[4,96,128]{2,1,0:T(8,128)S(1)} collective-permute-done((f32[4,96,128]{2,1,0:T(8,128)S(1)}, f32[4,96,128]{2,1,0:T(8,128)S(1)}, u32[]{:S(2)}, u32[]{:S(2)}) %collective-permute-start.38) | collective-permute-done | bytes 196640 | tf_op jit(solution)/shard_map/ppermute | solution.py:478
  263.5 15.5 %collective-permute-done.40.refs_1_ = f32[2,4,96,128]{3,2,1,0:T(8,128)S(1)} collective-permute-done((f32[2,4,96,128]{3,2,1,0:T(8,128)S(1)}, f32[2,4,96,128]{3,2,1,0:T(8,128)S(1)}, u32[]{:S(2)}, u32[]{:S(2)}) %collective-permute-start.40) | collective-permute-done | bytes 393248 | tf_op jit(solution)/shard_map/ppermute | solution.py:478
  279.0 4.9 %collective-permute-start.42 = (f32[2,4,96,128]{3,2,1,0:T(8,128)S(1)}, f32[2,4,96,128]{3,2,1,0:T(8,128)S(1)}, u32[]{:S(2)}, u32[]{:S(2)}) collective-permute-start(f32[2,4,96,128]{3,2,1,0:T(8,128)S(1)} %pad_maximum_fusion.4.refs_0_), channel_id=1, source_target_pairs={{0,1},{1,0},{2,3},{3,2},{4,5},{5,4},{6,7},{7,6},{8,9},{9,8},{10,11... | collective-permute-start | bytes 1179656 | tf_op jit(solution)/shard_map/ppermute | solution.py:478
  289.4 5.7 %all-gather.3.cloned.1.call-done = f32[18432,128]{1,0:T(8,128)} async-done(((f32[576,128]{1,0:T(8,128)}), f32[18432,128]{1,0:T(8,128)}) %all-gather.3.cloned.1.call-update) | async-done | bytes 9437200 | tf_op jit(solution)/shard_map/all_gather | solution.py:920
  295.2 3.7 %copy-done.12 = f32[18432,128]{1,0:T(8,128)S(1)} copy-done((f32[18432,128]{1,0:T(8,128)S(1)}, f32[18432,128]{1,0:T(8,128)}, u32[]{:S(2)}) %copy-start.12) | copy-done | bytes 9437208
  298.9 4.8 %unpack.1 = (f32[2048,512]{1,0:T(8,128)}, f32[512,2048]{1,0:T(8,128)}, f32[512,512]{1,0:T(8,128)}) custom-call(f32[32,576,128]{2,1,0:T(8,128)S(1)} %bitcast.182), custom_call_target="tpu_custom_call" | custom-call | tf_op jit(solution)/shard_map/unpack/pallas_call | solution.py:674
  (196 shorter events, 72.1 us)
Async XLA Ops:
  7.2 288.0 %all-gather.3.cloned.1.call-start = ((), (), s32[]{:S(2)}) async-start(), calls=%async_computation | async-start | bytes 9732096 | tf_op jit(solution)/shard_map/all_gather | solution.py:920
  22.0 8.5 %collective-permute-start.1 = (f32[272,256]{1,0:T(8,128)S(1)}, f32[272,256]{1,0:T(8,128)S(1)}, u32[]{:S(2)}, u32[]{:S(2)}) collective-permute-start(f32[272,256]{1,0:T(8,128)S(1)} %constant_dynamic-slice_fusion.4), channel_id=1, source_target_pairs={{0,2},{1,3},{2,0},{3,1},{4,6},{5,7},{6,4},{7,5},{8,10},{9,11},{10,... | collective-permute-start | bytes 835592 | tf_op jit(solution)/shard_map/ppermute | solution.py:478
  35.2 9.9 %collective-permute-start.3 = (f32[136,256]{1,0:T(8,128)S(1)}, f32[136,256]{1,0:T(8,128)S(1)}, u32[]{:S(2)}, u32[]{:S(2)}) collective-permute-start(f32[136,256]{1,0:T(8,128)S(1)} %dynamic-slice_add_fusion.5), channel_id=1, source_target_pairs={{0,8},{1,9},{2,10},{3,11},{4,12},{5,13},{6,14},{7,15},{8,0},{9,1},... | collective-permute-start | bytes 417800 | tf_op jit(solution)/shard_map/ppermute | solution.py:478
  54.8 5.8 %collective-permute-start.6 = (f32[544,256]{1,0:T(8,128)S(1)}, f32[544,256]{1,0:T(8,128)S(1)}, u32[]{:S(2)}, u32[]{:S(2)}) collective-permute-start(f32[544,256]{1,0:T(8,128)S(1)} %select_add_fusion.2), channel_id=1, source_target_pairs={{0,1},{1,0},{2,3},{3,2},{4,5},{5,4},{6,7},{7,6},{8,9},{9,8},{10,11... | collective-permute-start | bytes 1671176 | tf_op jit(solution)/shard_map/ppermute | solution.py:478
  96.3 9.9 %collective-permute-start.9 = (f32[16,576,128]{2,1,0:T(8,128)}, f32[16,576,128]{2,1,0:T(8,128)}, u32[]{:S(2)}, u32[]{:S(2)}) collective-permute-start(f32[16,576,128]{2,1,0:T(8,128)} %get-tuple-element.210), channel_id=1, source_target_pairs={{0,1},{1,0},{2,3},{3,2},{4,5},{5,4},{6,7},{7,6},{8,9},{9,8},{10,11... | collective-permute-start | bytes 14155784 | tf_op jit(solution)/shard_map/ppermute | solution.py:478
  96.7 9.5 %collective-permute-start.8 = (f32[272,256]{1,0:T(8,128)S(1)}, f32[272,256]{1,0:T(8,128)S(1)}, u32[]{:S(2)}, u32[]{:S(2)}) collective-permute-start(f32[272,256]{1,0:T(8,128)S(1)} %constant_dynamic-slice_fusion.1), channel_id=1, source_target_pairs={{0,2},{1,3},{2,0},{3,1},{4,6},{5,7},{6,4},{7,5},{8,10},{9,11},{10,... | collective-permute-start | bytes 835592 | tf_op jit(solution)/shard_map/ppermute | solution.py:478
  106.3 6.6 %collective-permute-start.10 = (f32[136,256]{1,0:T(8,128)S(1)}, f32[136,256]{1,0:T(8,128)S(1)}, u32[]{:S(2)}, u32[]{:S(2)}) collective-permute-start(f32[136,256]{1,0:T(8,128)S(1)} %constant_dynamic-slice_fusion), channel_id=1, source_target_pairs={{0,4},{1,5},{2,6},{3,7},{4,0},{5,1},{6,2},{7,3},{8,12},{9,13},{10,... | collective-permute-start | bytes 417800 | tf_op jit(solution)/shard_map/ppermute | solution.py:478
  111.4 33.9 %collective-permute-start.14 = (f32[2,4,288,128]{3,2,1,0:T(8,128)}, f32[2,4,288,128]{3,2,1,0:T(8,128)S(1)}, u32[]{:S(2)}, u32[]{:S(2)}) collective-permute-start(f32[2,4,288,128]{3,2,1,0:T(8,128)} %add_bitcast_fusion.1), channel_id=1, source_target_pairs={{0,16},{1,17},{2,18},{3,19},{4,20},{5,21},{6,22},{7,23},{8,24},{9,... | collective-permute-start | bytes 3538952 | tf_op jit(solution)/shard_map/ppermute | solution.py:478
  112.7 32.6 %collective-permute-start.15 = (f32[2,4,288,128]{3,2,1,0:T(8,128)}, f32[2,4,288,128]{3,2,1,0:T(8,128)}, u32[]{:S(2)}, u32[]{:S(2)}) collective-permute-start(f32[2,4,288,128]{3,2,1,0:T(8,128)} %add_bitcast_fusion), channel_id=1, source_target_pairs={{0,2},{1,3},{2,0},{3,1},{4,6},{5,7},{6,4},{7,5},{8,10},{9,11},{10,... | collective-permute-start | bytes 3538952 | tf_op jit(solution)/shard_map/ppermute | solution.py:478
  112.9 8.6 %collective-permute-start.11 = (f32[136,256]{1,0:T(8,128)S(1)}, f32[136,256]{1,0:T(8,128)S(1)}, u32[]{:S(2)}, u32[]{:S(2)}) collective-permute-start(f32[136,256]{1,0:T(8,128)S(1)} %dynamic-slice_add_fusion.4), channel_id=1, source_target_pairs={{0,8},{1,9},{2,10},{3,11},{4,12},{5,13},{6,14},{7,15},{8,0},{9,1},... | collective-permute-start | bytes 417800 | tf_op jit(solution)/shard_map/ppermute | solution.py:478
  126.3 19.0 %collective-permute-start.13 = (f32[272,256]{1,0:T(8,128)S(1)}, f32[272,256]{1,0:T(8,128)S(1)}, u32[]{:S(2)}, u32[]{:S(2)}) collective-permute-start(f32[272,256]{1,0:T(8,128)S(1)} %select_add_fusion.5), channel_id=1, source_target_pairs={{0,2},{1,3},{2,0},{3,1},{4,6},{5,7},{6,4},{7,5},{8,10},{9,11},{10,... | collective-permute-start | bytes 835592 | tf_op jit(solution)/shard_map/ppermute | solution.py:478
  149.1 13.2 %collective-permute-start.17 = (f32[4,288,128]{2,1,0:T(8,128)}, f32[4,288,128]{2,1,0:T(8,128)}, u32[]{:S(2)}, u32[]{:S(2)}) collective-permute-start(f32[4,288,128]{2,1,0:T(8,128)} %get-tuple-element.250), channel_id=1, source_target_pairs={{0,2},{1,3},{2,0},{3,1},{4,6},{5,7},{6,4},{7,5},{8,10},{9,11},{10,... | collective-permute-start | bytes 1769480 | tf_op jit(solution)/shard_map/ppermute | solution.py:478
  149.2 13.1 %collective-permute-start.18 = (f32[4,288,128]{2,1,0:T(8,128)S(1)}, f32[4,288,128]{2,1,0:T(8,128)}, u32[]{:S(2)}, u32[]{:S(2)}) collective-permute-start(f32[4,288,128]{2,1,0:T(8,128)S(1)} %get-tuple-element.251), channel_id=1, source_target_pairs={{0,16},{1,17},{2,18},{3,19},{4,20},{5,21},{6,22},{7,23},{8,24},{9,... | collective-permute-start | bytes 1769480 | tf_op jit(solution)/shard_map/ppermute | solution.py:478
  149.4 10.2 %collective-permute-start.16 = (f32[544,256]{1,0:T(8,128)}, f32[544,256]{1,0:T(8,128)}, u32[]{:S(2)}, u32[]{:S(2)}) collective-permute-start(f32[544,256]{1,0:T(8,128)} %select_add_fusion.1), channel_id=1, source_target_pairs={{0,1},{1,0},{2,3},{3,2},{4,5},{5,4},{6,7},{7,6},{8,9},{9,8},{10,11... | collective-permute-start | bytes 1671176 | tf_op jit(solution)/shard_map/ppermute | solution.py:478
  165.0 18.6 %collective-permute-start.19 = (f32[576,128]{1,0:T(8,128)S(1)}, f32[576,128]{1,0:T(8,128)S(1)}, u32[]{:S(2)}, u32[]{:S(2)}) collective-permute-start(f32[576,128]{1,0:T(8,128)S(1)} %get-tuple-element.262), channel_id=1, source_target_pairs={{0,4},{1,5},{2,6},{3,7},{4,0},{5,1},{6,2},{7,3},{8,12},{9,13},{10,... | collective-permute-start | bytes 884744 | tf_op jit(solution)/shard_map/ppermute | solution.py:478
  166.3 17.3 %collective-permute-start.20 = (f32[576,128]{1,0:T(8,128)S(1)}, f32[576,128]{1,0:T(8,128)S(1)}, u32[]{:S(2)}, u32[]{:S(2)}) collective-permute-start(f32[576,128]{1,0:T(8,128)S(1)} %get-tuple-element.263), channel_id=1, source_target_pairs={{0,8},{1,9},{2,10},{3,11},{4,12},{5,13},{6,14},{7,15},{8,0},{9,1},... | collective-permute-start | bytes 884744 | tf_op jit(solution)/shard_map/ppermute | solution.py:478
  167.6 23.2 %collective-permute-start.21 = (f32[576,128]{1,0:T(8,128)S(1)}, f32[576,128]{1,0:T(8,128)S(1)}, u32[]{:S(2)}, u32[]{:S(2)}) collective-permute-start(f32[576,128]{1,0:T(8,128)S(1)} %get-tuple-element.264), channel_id=1, source_target_pairs={{0,12},{1,13},{2,14},{3,15},{4,8},{5,9},{6,10},{7,11},{8,4},{9,5},... | collective-permute-start | bytes 884744 | tf_op jit(solution)/shard_map/ppermute | solution.py:478
  191.7 7.6 %collective-permute-start.23 = (f32[16,192,128]{2,1,0:T(8,128)S(1)}, f32[16,192,128]{2,1,0:T(8,128)S(1)}, u32[]{:S(2)}, u32[]{:S(2)}) collective-permute-start(f32[16,192,128]{2,1,0:T(8,128)S(1)} %qkv_grads.2), channel_id=1, source_target_pairs={{0,1},{1,0},{2,3},{3,2},{4,5},{5,4},{6,7},{7,6},{8,9},{9,8},{10,11... | collective-permute-start | bytes 4718600 | tf_op jit(solution)/shard_map/ppermute | solution.py:478
  199.4 13.1 %collective-permute-start.24 = (f32[2,4,96,128]{3,2,1,0:T(8,128)S(1)}, f32[2,4,96,128]{3,2,1,0:T(8,128)S(1)}, u32[]{:S(2)}, u32[]{:S(2)}) collective-permute-start(f32[2,4,96,128]{3,2,1,0:T(8,128)S(1)} %add_bitcast_fusion.3), channel_id=1, source_target_pairs={{0,16},{1,17},{2,18},{3,19},{4,20},{5,21},{6,22},{7,23},{8,24},{9,... | collective-permute-start | bytes 1179656 | tf_op jit(solution)/shard_map/ppermute | solution.py:478
  199.7 12.8 %collective-permute-start.25 = (f32[2,4,96,128]{3,2,1,0:T(8,128)S(1)}, f32[2,4,96,128]{3,2,1,0:T(8,128)S(1)}, u32[]{:S(2)}, u32[]{:S(2)}) collective-permute-start(f32[2,4,96,128]{3,2,1,0:T(8,128)S(1)} %add_bitcast_fusion.2), channel_id=1, source_target_pairs={{0,2},{1,3},{2,0},{3,1},{4,6},{5,7},{6,4},{7,5},{8,10},{9,11},{10,... | collective-permute-start | bytes 1179656 | tf_op jit(solution)/shard_map/ppermute | solution.py:478
  200.7 11.8 %collective-permute-start.26 = (f32[52,128]{1,0:T(8,128)S(1)}, f32[52,128]{1,0:T(8,128)S(1)}, u32[]{:S(2)}, u32[]{:S(2)}) collective-permute-start(f32[52,128]{1,0:T(8,128)S(1)} %fusion.27), channel_id=1, source_target_pairs={{0,2},{1,3},{2,0},{3,1},{4,6},{5,7},{6,4},{7,5},{8,10},{9,11},{10,... | collective-permute-start | bytes 79880 | tf_op jit(solution)/shard_map/ppermute | solution.py:478
  218.6 21.0 %collective-permute-start.30 = (f32[192,128]{1,0:T(8,128)S(1)}, f32[192,128]{1,0:T(8,128)S(1)}, u32[]{:S(2)}, u32[]{:S(2)}) collective-permute-start(f32[192,128]{1,0:T(8,128)S(1)} %get-tuple-element.304), channel_id=1, source_target_pairs={{0,4},{1,5},{2,6},{3,7},{4,0},{5,1},{6,2},{7,3},{8,12},{9,13},{10,... | collective-permute-start | bytes 294920 | tf_op jit(solution)/shard_map/ppermute | solution.py:478
  218.7 20.9 %collective-permute-start.31 = (f32[192,128]{1,0:T(8,128)S(1)}, f32[192,128]{1,0:T(8,128)S(1)}, u32[]{:S(2)}, u32[]{:S(2)}) collective-permute-start(f32[192,128]{1,0:T(8,128)S(1)} %get-tuple-element.305), channel_id=1, source_target_pairs={{0,8},{1,9},{2,10},{3,11},{4,12},{5,13},{6,14},{7,15},{8,0},{9,1},... | collective-permute-start | bytes 294920 | tf_op jit(solution)/shard_map/ppermute | solution.py:478
  221.2 18.4 %collective-permute-start.32 = (f32[192,128]{1,0:T(8,128)S(1)}, f32[192,128]{1,0:T(8,128)S(1)}, u32[]{:S(2)}, u32[]{:S(2)}) collective-permute-start(f32[192,128]{1,0:T(8,128)S(1)} %get-tuple-element.306), channel_id=1, source_target_pairs={{0,12},{1,13},{2,14},{3,15},{4,8},{5,9},{6,10},{7,11},{8,4},{9,5},... | collective-permute-start | bytes 294920 | tf_op jit(solution)/shard_map/ppermute | solution.py:478
  221.3 18.3 %collective-permute-start.33 = (f32[52,128]{1,0:T(8,128)S(1)}, f32[52,128]{1,0:T(8,128)S(1)}, u32[]{:S(2)}, u32[]{:S(2)}) collective-permute-start(f32[52,128]{1,0:T(8,128)S(1)} %add.517), channel_id=1, source_target_pairs={{0,8},{1,9},{2,10},{3,11},{4,12},{5,13},{6,14},{7,15},{8,0},{9,1},... | collective-permute-start | bytes 79880 | tf_op jit(solution)/shard_map/ppermute | solution.py:478
  241.0 7.1 %collective-permute-start.35 = (f32[192,128]{1,0:T(8,128)S(1)}, f32[192,128]{1,0:T(8,128)S(1)}, u32[]{:S(2)}, u32[]{:S(2)}) collective-permute-start(f32[192,128]{1,0:T(8,128)S(1)} %fusion.19), channel_id=1, source_target_pairs={{0,8},{1,9},{2,10},{3,11},{4,12},{5,13},{6,14},{7,15},{8,0},{9,1},... | collective-permute-start | bytes 294920 | tf_op jit(solution)/shard_map/ppermute | solution.py:478
  244.9 7.0 %collective-permute-start.36 = (f32[192,128]{1,0:T(8,128)S(1)}, f32[192,128]{1,0:T(8,128)S(1)}, u32[]{:S(2)}, u32[]{:S(2)}) collective-permute-start(f32[192,128]{1,0:T(8,128)S(1)} %fusion.19), channel_id=1, source_target_pairs={{0,12},{1,13},{2,14},{3,15},{4,8},{5,9},{6,10},{7,11},{8,4},{9,5},... | collective-permute-start | bytes 294920 | tf_op jit(solution)/shard_map/ppermute | solution.py:478
  252.0 9.2 %collective-permute-start.38 = (f32[4,96,128]{2,1,0:T(8,128)S(1)}, f32[4,96,128]{2,1,0:T(8,128)S(1)}, u32[]{:S(2)}, u32[]{:S(2)}) collective-permute-start(f32[4,96,128]{2,1,0:T(8,128)S(1)} %get-tuple-element.320), channel_id=1, source_target_pairs={{0,2},{1,3},{2,0},{3,1},{4,6},{5,7},{6,4},{7,5},{8,10},{9,11},{10,... | collective-permute-start | bytes 589832 | tf_op jit(solution)/shard_map/ppermute | solution.py:478
  252.1 9.1 %collective-permute-start.39 = (f32[4,96,128]{2,1,0:T(8,128)S(1)}, f32[4,96,128]{2,1,0:T(8,128)S(1)}, u32[]{:S(2)}, u32[]{:S(2)}) collective-permute-start(f32[4,96,128]{2,1,0:T(8,128)S(1)} %get-tuple-element.321), channel_id=1, source_target_pairs={{0,16},{1,17},{2,18},{3,19},{4,20},{5,21},{6,22},{7,23},{8,24},{9,... | collective-permute-start | bytes 589832 | tf_op jit(solution)/shard_map/ppermute | solution.py:478
  261.2 17.8 %collective-permute-start.40 = (f32[2,4,96,128]{3,2,1,0:T(8,128)S(1)}, f32[2,4,96,128]{3,2,1,0:T(8,128)S(1)}, u32[]{:S(2)}, u32[]{:S(2)}) collective-permute-start(f32[2,4,96,128]{3,2,1,0:T(8,128)S(1)} %pad_maximum_fusion.4.refs_0_), channel_id=1, source_target_pairs={{0,16},{1,17},{2,18},{3,19},{4,20},{5,21},{6,22},{7,23},{8,24},{9,... | collective-permute-start | bytes 1179656 | tf_op jit(solution)/shard_map/ppermute | solution.py:478
  261.3 17.7 %collective-permute-start.41 = (f32[2,4,96,128]{3,2,1,0:T(8,128)S(1)}, f32[2,4,96,128]{3,2,1,0:T(8,128)S(1)}, u32[]{:S(2)}, u32[]{:S(2)}) collective-permute-start(f32[2,4,96,128]{3,2,1,0:T(8,128)S(1)} %pad_maximum_fusion.5.refs_2_), channel_id=1, source_target_pairs={{0,2},{1,3},{2,0},{3,1},{4,6},{5,7},{6,4},{7,5},{8,10},{9,11},{10,... | collective-permute-start | bytes 1179656 | tf_op jit(solution)/shard_map/ppermute | solution.py:478
  279.0 6.7 %collective-permute-start.42 = (f32[2,4,96,128]{3,2,1,0:T(8,128)S(1)}, f32[2,4,96,128]{3,2,1,0:T(8,128)S(1)}, u32[]{:S(2)}, u32[]{:S(2)}) collective-permute-start(f32[2,4,96,128]{3,2,1,0:T(8,128)S(1)} %pad_maximum_fusion.4.refs_0_), channel_id=1, source_target_pairs={{0,1},{1,0},{2,3},{3,2},{4,5},{5,4},{6,7},{7,6},{8,9},{9,8},{10,11... | collective-permute-start | bytes 1179656 | tf_op jit(solution)/shard_map/ppermute | solution.py:478
  (39 other events, 192.0 us)
Sparse Core Ops, SparseCore 0:
  191.7 103.4 all-gather.2

commit v6 on v5

--- a/solution.py
+++ b/solution.py
@@ -911,16 +911,12 @@
         def both(dphik):
             dx, dqkv, *parts = last(0)(dphik)
             dx, dqkv, *more = last(1)(dphik, dx, dqkv)
-            theirs = some(1 - core, dqkv)
-            return dx, dqkv, theirs, *parts, *more
-
-        dx, dqkv, theirs, *parts = phase([ffn], [ffn], both, (dphik,))
-        more = []
-        qkv_sum = Stream(bucket_stream(theirs, lambda: more[0]))
+            return dx, some(1 - core, dqkv), some(core, dqkv), *parts, *more
+
+        dx, theirs, mine, *parts = phase([ffn], [ffn], both, (dphik,))
+        qkv_sum = Stream(bucket_stream(theirs, mine))
         packed = lax.all_gather(ffn.value, ("c", "x", "y", "z"))
         small = Stream(small_stream(join(*parts), all_bits))
-        more += phase([qkv_sum, small], [small], lambda dqkv: (some(core, dqkv),), (dqkv,))
-        phase((), [qkv_sum])
         while qkv_sum.pending is not None or small.pending is not None:
             both = [item for item in (qkv_sum, small) if item.pending is not None]
             phase(both, both)

time: 317 us -> 315 us (level)
    unnamed x51 -> x47, local copies, waits for them, and re-layouts: 9.64 us -> 7.75 us
  transfers between devices with their start and end apart: 47 -> 47, of which waited for: 23 -> 24; matrix products, arithmetic and copies ran while one was open for 3% -> 3% of each run, Pallas kernels for 19% -> 19%
where the time goes in v6:
time: 315 us; the launch traced here: 309 us
  waiting for transfers between devices  109 us (35%)
  Pallas kernels  103 us (33%)
  starting transfers between devices  50.2 us (16%)
  other arithmetic  19.4 us (6%)
  between operations  15.8 us (5%)
  local copies, waits for them, and re-layouts  12.7 us (4%)
    ppermute x46, waiting for transfers between devices, send(): return lax.ppermute(values, AXES, [(i, i ^ mask) for i in range(count)])  105 us
    ppermute x46, starting transfers between devices, send(): return lax.ppermute(values, AXES, [(i, i ^ mask) for i in range(count)])  50.2 us
    pallas_call x1, Pallas kernels, run_middle(): pl.pallas_call(functools.partial(middle_kernel, per, chips), grid_spec=pl...  30.2 us
    pallas_call x4, Pallas kernels, run_scores(): pl.pallas_call(functools.partial(score_back_kernel, first), grid=(count,)...  29.5 us
    pallas_call x2, Pallas kernels, run_local(): pl.pallas_call(local_kernel, grid=(PAIRS,), in_specs=[pl.BlockSpec((1, sp...  15.1 us
    add x10, other arithmetic, add_all(): return functools.reduce(jnp.add, items)  11.3 us
    pallas_call x2, Pallas kernels, run_final(): pl.pallas_call(final_kernel, grid=(1,), in_specs=[three((span, width)), t...  8.81 us
    pallas_call x1, Pallas kernels, run_keys(): pl.pallas_call(kv_kernel, grid=(seqs,), in_specs=[three((span, width)), w...  8.37 us
  transfers between devices with their start and end apart: 47, of which 24 were waited for; matrix products, arithmetic and copies ran while one was open for 3% of the time, Pallas kernels for 19%

profile of v6, /device:TPU:13, one launch (start us, length us, event | category | flops | bytes accessed | tf_op | source)
XLA Modules:
  0.0 309.4 jit_solution(7447532241991831003)
XLA Ops:
  9.1 8.4 %keys.1 = (bf16[2,512,512]{2,1,0:T(8,128)(2,1)}, bf16[2,512,1024]{2,1,0:T(8,128)(2,1)}, bf16[2,512,2048]{2,1,0:T(8,128)(2,1)}, f32[2,544,256]{2,1,0:T(8,128)}) custom-call(bf16[2,512,512]{2,1,0:T(8,128)(2,1)} %x_ref.5, f32[1,512]{1,0:T(1,128)} %bitcast.188, f32[1,512]{1,0:T(1,128)} %bitcast.191, bf16[512,1536]{1,0:T(8,128)(2,1)} %w_ref.9, f32[1536]{0:T(1024)} %b_ref.1, ...), custom_call_target="tpu_custom_call" | custom-call | tf_op jit(solution)/shard_map/keys/pallas_call | solution.py:743
  22.9 7.6 %local.2 = (bf16[2,512,512]{2,1,0:T(8,128)(2,1)}, bf16[2,512,2048]{2,1,0:T(8,128)(2,1)}, f32[2,512,1024]{2,1,0:T(8,128)}) custom-call(bf16[2,512,512]{2,1,0:T(8,128)(2,1)} %get-tuple-element.181.h_ref, bf16[512,1536]{1,0:T(8,128)(2,1)} %w_ref.9, f32[1,1536]{1,0:T(1,128)} %reshape.201.b_ref, bf16[2,512,1024]{2,1,0:T(8,128)(2,1)} %get-tuple-element.192.v_ref.kv_ref, ...), custom_call_target="tpu_custom_call" | custom-call | tf_op jit(solution)/shard_map/local/pallas_call | solution.py:696
  30.7 4.5 %collective-permute-done.2 = f32[136,256]{1,0:T(8,128)S(1)} collective-permute-done((f32[136,256]{1,0:T(8,128)S(1)}, f32[136,256]{1,0:T(8,128)S(1)}, u32[]{:S(2)}, u32[]{:S(2)}) %collective-permute-start.2) | collective-permute-done | bytes 139296 | tf_op jit(solution)/shard_map/ppermute | solution.py:478
  37.6 7.5 %local.3 = (bf16[2,512,512]{2,1,0:T(8,128)(2,1)}, bf16[2,512,2048]{2,1,0:T(8,128)(2,1)}, f32[2,512,1024]{2,1,0:T(8,128)}) custom-call(bf16[2,512,512]{2,1,0:T(8,128)(2,1)} %get-tuple-element.181.h_ref, bf16[512,1536]{1,0:T(8,128)(2,1)} %w_ref.9, f32[1,1536]{1,0:T(1,128)} %reshape.201.b_ref, ...), custom_call_target="tpu_custom_call", output_to_operand_aliasing={{0}: (6, {}), {1}: (7, {}), {2}: (8, {})} | custom-call | tf_op jit(solution)/shard_map/local/pallas_call | solution.py:696
  45.4 3.8 %collective-permute-done.4 = f32[136,256]{1,0:T(8,128)S(1)} collective-permute-done((f32[136,256]{1,0:T(8,128)S(1)}, f32[136,256]{1,0:T(8,128)S(1)}, u32[]{:S(2)}, u32[]{:S(2)}) %collective-permute-start.4) | collective-permute-done | bytes 139296 | tf_op jit(solution)/shard_map/ppermute | solution.py:478
  50.5 4.2 %collective-permute-done.5 = f32[272,256]{1,0:T(8,128)S(1)} collective-permute-done((f32[272,256]{1,0:T(8,128)S(1)}, f32[272,256]{1,0:T(8,128)S(1)}, u32[]{:S(2)}, u32[]{:S(2)}) %collective-permute-start.5) | collective-permute-done | bytes 278560 | tf_op jit(solution)/shard_map/ppermute | solution.py:478
  54.9 4.2 %collective-permute-start.6 = (f32[544,256]{1,0:T(8,128)S(1)}, f32[544,256]{1,0:T(8,128)S(1)}, u32[]{:S(2)}, u32[]{:S(2)}) collective-permute-start(f32[544,256]{1,0:T(8,128)S(1)} %select_add_fusion.2), channel_id=1, source_target_pairs={{0,1},{1,0},{2,3},{3,2},{4,5},{5,4},{6,7},{7,6},{8,9},{9,8},{10,11... | collective-permute-start | bytes 1671176 | tf_op jit(solution)/shard_map/ppermute | solution.py:478
  61.8 30.2 %middle.1 = (bf16[1024,512]{1,0:T(8,128)(2,1)}, f32[1024,512]{1,0:T(8,128)}, bf16[1024,1024]{1,0:T(8,128)(2,1)}, f32[2,544,256]{2,1,0:T(8,128)}, f32[8,512]{1,0:...) custom-call(s32[1]{0:T(128)} %bitcast.core_ref.half_ref, ...), custom_call_target="tpu_custom_call" | custom-call | tf_op jit(solution)/shard_map/middle/pallas_call | solution.py:779
  98.7 7.5 %scores.4 = (bf16[2,512,512]{2,1,0:T(8,128)(2,1)}, bf16[2,512,2048]{2,1,0:T(8,128)(2,1)}, f32[2,512,512]{2,1,0:T(8,128)}) custom-call(bf16[2,512,512]{2,1,0:T(8,128)(2,1)} %get-tuple-element.210.q_ref, bf16[2,512,1024]{2,1,0:T(8,128)(2,1)} %get-tuple-element.192.v_ref.kv_ref, bf16[2,512,2048]{2,1,0:T(8,128)(2,1)} %get-tuple-element.201.phiq_ref, ...), custom_call_target="tpu_custom_call" | custom-call | tf_op jit(solution)/shard_map/scores/pallas_call | solution.py:719
  114.3 7.2 %scores.5 = (bf16[2,512,512]{2,1,0:T(8,128)(2,1)}, bf16[2,512,2048]{2,1,0:T(8,128)(2,1)}, f32[2,512,512]{2,1,0:T(8,128)}) custom-call(bf16[2,512,512]{2,1,0:T(8,128)(2,1)} %get-tuple-element.210.q_ref, bf16[2,512,1024]{2,1,0:T(8,128)(2,1)} %get-tuple-element.192.v_ref.kv_ref, ...), custom_call_target="tpu_custom_call", output_to_operand_aliasing={{0}: (8, {}), {1}: (9, {}), {2}: (10, {})} | custom-call | tf_op jit(solution)/shard_map/scores/pallas_call | solution.py:719
  123.3 2.8 collective-permute-done.12
  127.8 7.2 %scores.6 = (bf16[2,512,512]{2,1,0:T(8,128)(2,1)}, bf16[2,512,2048]{2,1,0:T(8,128)(2,1)}, f32[2,512,512]{2,1,0:T(8,128)}) custom-call(bf16[2,512,512]{2,1,0:T(8,128)(2,1)} %get-tuple-element.210.q_ref, bf16[2,512,1024]{2,1,0:T(8,128)(2,1)} %get-tuple-element.192.v_ref.kv_ref, ...), custom_call_target="tpu_custom_call", output_to_operand_aliasing={{0}: (8, {}), {1}: (9, {}), {2}: (10, {})} | custom-call | tf_op jit(solution)/shard_map/scores/pallas_call | solution.py:719
  135.0 10.3 %collective-permute-done.13 = f32[272,256]{1,0:T(8,128)S(1)} collective-permute-done((f32[272,256]{1,0:T(8,128)S(1)}, f32[272,256]{1,0:T(8,128)S(1)}, u32[]{:S(2)}, u32[]{:S(2)}) %collective-permute-start.13) | collective-permute-done | bytes 278560 | tf_op jit(solution)/shard_map/ppermute | solution.py:478
  146.3 2.8 bitcast_add_fusion.1
  152.0 7.6 %scores.7 = (bf16[2,512,512]{2,1,0:T(8,128)(2,1)}, bf16[2,512,2048]{2,1,0:T(8,128)(2,1)}, f32[2,512,512]{2,1,0:T(8,128)}) custom-call(bf16[2,512,512]{2,1,0:T(8,128)(2,1)} %get-tuple-element.210.q_ref, bf16[2,512,1024]{2,1,0:T(8,128)(2,1)} %get-tuple-element.192.v_ref.kv_ref, ...), custom_call_target="tpu_custom_call", output_to_operand_aliasing={{0}: (8, {}), {1}: (9, {}), {2}: (10, {})} | custom-call | tf_op jit(solution)/shard_map/scores/pallas_call | solution.py:719
  159.6 2.7 collective-permute-done.17
  173.0 4.4 %final.2 = (bf16[2,512,512]{2,1,0:T(8,128)(2,1)}, bf16[2,512,1536]{2,1,0:T(8,128)(2,1)S(1)}, f32[8,512]{1,0:T(8,128)S(1)}, f32[1,1536]{1,0:T(1,128)S(1)}) custom-call(bf16[2,512,512]{2,1,0:T(8,128)(2,1)S(1)} %copy-done.8, f32[2,512,512]{2,1,0:T(8,128)S(1)} %bitcast.182, bf16[2,512,1024]{2,1,0:T(8,128)(2,1)S(1)} %copy-done.3, ...), custom_call_target="tpu_custom_call" | custom-call | tf_op jit(solution)/shard_map/final/pallas_call | solution.py:809
  177.5 4.4 %final.3 = (bf16[2,512,512]{2,1,0:T(8,128)(2,1)}, bf16[2,512,1536]{2,1,0:T(8,128)(2,1)S(1)}, f32[8,512]{1,0:T(8,128)S(1)}, f32[1,1536]{1,0:T(1,128)S(1)}) custom-call(bf16[2,512,512]{2,1,0:T(8,128)(2,1)S(1)} %copy-done.8, f32[2,512,512]{2,1,0:T(8,128)S(1)} %bitcast.183, ...), custom_call_target="tpu_custom_call", output_to_operand_aliasing={{0}: (12, {}), {1}: (13, {})} | custom-call | tf_op jit(solution)/shard_map/final/pallas_call | solution.py:809
  185.3 5.5 %collective-permute-done.21 = f32[576,128]{1,0:T(8,128)S(1)} collective-permute-done((f32[576,128]{1,0:T(8,128)S(1)}, f32[576,128]{1,0:T(8,128)S(1)}, u32[]{:S(2)}, u32[]{:S(2)}) %collective-permute-start.21) | collective-permute-done | bytes 294944 | tf_op jit(solution)/shard_map/ppermute | solution.py:478
  191.7 3.9 %collective-permute-start.22 = (f32[16,192,128]{2,1,0:T(8,128)S(1)}, f32[16,192,128]{2,1,0:T(8,128)S(1)}, u32[]{:S(2)}, u32[]{:S(2)}) collective-permute-start(f32[16,192,128]{2,1,0:T(8,128)S(1)} %qkv_grads.2), channel_id=1, source_target_pairs={{0,1},{1,0},{2,3},{3,2},{4,5},{5,4},{6,7},{7,6},{8,9},{9,8},{10,11... | collective-permute-start | bytes 4718600 | tf_op jit(solution)/shard_map/ppermute | solution.py:478
  195.7 3.0 collective-permute-done.23
  200.6 11.4 %collective-permute-done.26 = f32[52,128]{1,0:T(8,128)S(1)} collective-permute-done((f32[52,128]{1,0:T(8,128)S(1)}, f32[52,128]{1,0:T(8,128)S(1)}, u32[]{:S(2)}, u32[]{:S(2)}) %collective-permute-start.26) | collective-permute-done | bytes 26656 | tf_op jit(solution)/shard_map/ppermute | solution.py:478
  214.2 3.2 %collective-permute-done.29 = f32[52,128]{1,0:T(8,128)S(1)} collective-permute-done((f32[52,128]{1,0:T(8,128)S(1)}, f32[52,128]{1,0:T(8,128)S(1)}, u32[]{:S(2)}, u32[]{:S(2)}) %collective-permute-start.29) | collective-permute-done | bytes 26656 | tf_op jit(solution)/shard_map/ppermute | solution.py:478
  222.8 16.3 %collective-permute-done.33 = f32[52,128]{1,0:T(8,128)S(1)} collective-permute-done((f32[52,128]{1,0:T(8,128)S(1)}, f32[52,128]{1,0:T(8,128)S(1)}, u32[]{:S(2)}, u32[]{:S(2)}) %collective-permute-start.33) | collective-permute-done | bytes 26656 | tf_op jit(solution)/shard_map/ppermute | solution.py:478
  240.4 4.0 %collective-permute-start.35 = (f32[192,128]{1,0:T(8,128)S(1)}, f32[192,128]{1,0:T(8,128)S(1)}, u32[]{:S(2)}, u32[]{:S(2)}) collective-permute-start(f32[192,128]{1,0:T(8,128)S(1)} %fusion.19), channel_id=1, source_target_pairs={{0,8},{1,9},{2,10},{3,11},{4,12},{5,13},{6,14},{7,15},{8,0},{9,1},... | collective-permute-start | bytes 294920 | tf_op jit(solution)/shard_map/ppermute | solution.py:478
  247.6 3.8 %collective-permute-done.36 = f32[192,128]{1,0:T(8,128)S(1)} collective-permute-done((f32[192,128]{1,0:T(8,128)S(1)}, f32[192,128]{1,0:T(8,128)S(1)}, u32[]{:S(2)}, u32[]{:S(2)}) %collective-permute-start.36) | collective-permute-done | bytes 98336 | tf_op jit(solution)/shard_map/ppermute | solution.py:478
  252.0 8.7 %collective-permute-done.38 = f32[4,96,128]{2,1,0:T(8,128)S(1)} collective-permute-done((f32[4,96,128]{2,1,0:T(8,128)S(1)}, f32[4,96,128]{2,1,0:T(8,128)S(1)}, u32[]{:S(2)}, u32[]{:S(2)}) %collective-permute-start.38) | collective-permute-done | bytes 196640 | tf_op jit(solution)/shard_map/ppermute | solution.py:478
  263.3 14.9 %collective-permute-done.40.refs_1_ = f32[2,4,96,128]{3,2,1,0:T(8,128)S(1)} collective-permute-done((f32[2,4,96,128]{3,2,1,0:T(8,128)S(1)}, f32[2,4,96,128]{3,2,1,0:T(8,128)S(1)}, u32[]{:S(2)}, u32[]{:S(2)}) %collective-permute-start.40) | collective-permute-done | bytes 393248 | tf_op jit(solution)/shard_map/ppermute | solution.py:478
  278.2 5.8 %collective-permute-start.42 = (f32[2,4,96,128]{3,2,1,0:T(8,128)S(1)}, f32[2,4,96,128]{3,2,1,0:T(8,128)S(1)}, u32[]{:S(2)}, u32[]{:S(2)}) collective-permute-start(f32[2,4,96,128]{3,2,1,0:T(8,128)S(1)} %pad_maximum_fusion.4.refs_0_), channel_id=1, source_target_pairs={{0,1},{1,0},{2,3},{3,2},{4,5},{5,4},{6,7},{7,6},{8,9},{9,8},{10,11... | collective-permute-start | bytes 1179656 | tf_op jit(solution)/shard_map/ppermute | solution.py:478
  290.2 3.4 %all-gather.3.cloned.1.call-done = f32[18432,128]{1,0:T(8,128)} async-done(((f32[576,128]{1,0:T(8,128)}), f32[18432,128]{1,0:T(8,128)}) %all-gather.3.cloned.1.call-update) | async-done | bytes 9437200 | tf_op jit(solution)/shard_map/all_gather | solution.py:918
  293.6 3.7 %copy-done.10 = f32[18432,128]{1,0:T(8,128)S(1)} copy-done((f32[18432,128]{1,0:T(8,128)S(1)}, f32[18432,128]{1,0:T(8,128)}, u32[]{:S(2)}) %copy-start.10) | copy-done | bytes 9437208
  297.3 4.8 %unpack.1 = (f32[2048,512]{1,0:T(8,128)}, f32[512,2048]{1,0:T(8,128)}, f32[512,512]{1,0:T(8,128)}) custom-call(f32[32,576,128]{2,1,0:T(8,128)S(1)} %bitcast.181), custom_call_target="tpu_custom_call" | custom-call | tf_op jit(solution)/shard_map/unpack/pallas_call | solution.py:674
  (192 shorter events, 73.9 us)
Async XLA Ops:
  7.2 286.4 %all-gather.3.cloned.1.call-start = ((), (), s32[]{:S(2)}) async-start(), calls=%async_computation | async-start | bytes 9732096 | tf_op jit(solution)/shard_map/all_gather | solution.py:918
  22.0 8.5 %collective-permute-start.1 = (f32[272,256]{1,0:T(8,128)S(1)}, f32[272,256]{1,0:T(8,128)S(1)}, u32[]{:S(2)}, u32[]{:S(2)}) collective-permute-start(f32[272,256]{1,0:T(8,128)S(1)} %constant_dynamic-slice_fusion.4), channel_id=1, source_target_pairs={{0,2},{1,3},{2,0},{3,1},{4,6},{5,7},{6,4},{7,5},{8,10},{9,11},{10,... | collective-permute-start | bytes 835592 | tf_op jit(solution)/shard_map/ppermute | solution.py:478
  35.2 9.9 %collective-permute-start.3 = (f32[136,256]{1,0:T(8,128)S(1)}, f32[136,256]{1,0:T(8,128)S(1)}, u32[]{:S(2)}, u32[]{:S(2)}) collective-permute-start(f32[136,256]{1,0:T(8,128)S(1)} %dynamic-slice_add_fusion.5), channel_id=1, source_target_pairs={{0,8},{1,9},{2,10},{3,11},{4,12},{5,13},{6,14},{7,15},{8,0},{9,1},... | collective-permute-start | bytes 417800 | tf_op jit(solution)/shard_map/ppermute | solution.py:478
  54.9 5.8 %collective-permute-start.6 = (f32[544,256]{1,0:T(8,128)S(1)}, f32[544,256]{1,0:T(8,128)S(1)}, u32[]{:S(2)}, u32[]{:S(2)}) collective-permute-start(f32[544,256]{1,0:T(8,128)S(1)} %select_add_fusion.2), channel_id=1, source_target_pairs={{0,1},{1,0},{2,3},{3,2},{4,5},{5,4},{6,7},{7,6},{8,9},{9,8},{10,11... | collective-permute-start | bytes 1671176 | tf_op jit(solution)/shard_map/ppermute | solution.py:478
  96.3 10.0 %collective-permute-start.9 = (f32[16,576,128]{2,1,0:T(8,128)}, f32[16,576,128]{2,1,0:T(8,128)}, u32[]{:S(2)}, u32[]{:S(2)}) collective-permute-start(f32[16,576,128]{2,1,0:T(8,128)} %get-tuple-element.209), channel_id=1, source_target_pairs={{0,1},{1,0},{2,3},{3,2},{4,5},{5,4},{6,7},{7,6},{8,9},{9,8},{10,11... | collective-permute-start | bytes 14155784 | tf_op jit(solution)/shard_map/ppermute | solution.py:478
  96.7 9.5 %collective-permute-start.8 = (f32[272,256]{1,0:T(8,128)S(1)}, f32[272,256]{1,0:T(8,128)S(1)}, u32[]{:S(2)}, u32[]{:S(2)}) collective-permute-start(f32[272,256]{1,0:T(8,128)S(1)} %constant_dynamic-slice_fusion.1), channel_id=1, source_target_pairs={{0,2},{1,3},{2,0},{3,1},{4,6},{5,7},{6,4},{7,5},{8,10},{9,11},{10,... | collective-permute-start | bytes 835592 | tf_op jit(solution)/shard_map/ppermute | solution.py:478
  106.3 6.6 %collective-permute-start.10 = (f32[136,256]{1,0:T(8,128)S(1)}, f32[136,256]{1,0:T(8,128)S(1)}, u32[]{:S(2)}, u32[]{:S(2)}) collective-permute-start(f32[136,256]{1,0:T(8,128)S(1)} %constant_dynamic-slice_fusion), channel_id=1, source_target_pairs={{0,4},{1,5},{2,6},{3,7},{4,0},{5,1},{6,2},{7,3},{8,12},{9,13},{10,... | collective-permute-start | bytes 417800 | tf_op jit(solution)/shard_map/ppermute | solution.py:478
  111.4 33.9 %collective-permute-start.14 = (f32[2,4,288,128]{3,2,1,0:T(8,128)}, f32[2,4,288,128]{3,2,1,0:T(8,128)S(1)}, u32[]{:S(2)}, u32[]{:S(2)}) collective-permute-start(f32[2,4,288,128]{3,2,1,0:T(8,128)} %add_bitcast_fusion.1), channel_id=1, source_target_pairs={{0,16},{1,17},{2,18},{3,19},{4,20},{5,21},{6,22},{7,23},{8,24},{9,... | collective-permute-start | bytes 3538952 | tf_op jit(solution)/shard_map/ppermute | solution.py:478
  112.7 32.7 %collective-permute-start.15 = (f32[2,4,288,128]{3,2,1,0:T(8,128)}, f32[2,4,288,128]{3,2,1,0:T(8,128)}, u32[]{:S(2)}, u32[]{:S(2)}) collective-permute-start(f32[2,4,288,128]{3,2,1,0:T(8,128)} %add_bitcast_fusion), channel_id=1, source_target_pairs={{0,2},{1,3},{2,0},{3,1},{4,6},{5,7},{6,4},{7,5},{8,10},{9,11},{10,... | collective-permute-start | bytes 3538952 | tf_op jit(solution)/shard_map/ppermute | solution.py:478
  112.9 8.6 %collective-permute-start.11 = (f32[136,256]{1,0:T(8,128)S(1)}, f32[136,256]{1,0:T(8,128)S(1)}, u32[]{:S(2)}, u32[]{:S(2)}) collective-permute-start(f32[136,256]{1,0:T(8,128)S(1)} %dynamic-slice_add_fusion.4), channel_id=1, source_target_pairs={{0,8},{1,9},{2,10},{3,11},{4,12},{5,13},{6,14},{7,15},{8,0},{9,1},... | collective-permute-start | bytes 417800 | tf_op jit(solution)/shard_map/ppermute | solution.py:478
  126.3 19.0 %collective-permute-start.13 = (f32[272,256]{1,0:T(8,128)S(1)}, f32[272,256]{1,0:T(8,128)S(1)}, u32[]{:S(2)}, u32[]{:S(2)}) collective-permute-start(f32[272,256]{1,0:T(8,128)S(1)} %select_add_fusion.5), channel_id=1, source_target_pairs={{0,2},{1,3},{2,0},{3,1},{4,6},{5,7},{6,4},{7,5},{8,10},{9,11},{10,... | collective-permute-start | bytes 835592 | tf_op jit(solution)/shard_map/ppermute | solution.py:478
  149.1 13.2 %collective-permute-start.17 = (f32[4,288,128]{2,1,0:T(8,128)}, f32[4,288,128]{2,1,0:T(8,128)}, u32[]{:S(2)}, u32[]{:S(2)}) collective-permute-start(f32[4,288,128]{2,1,0:T(8,128)} %get-tuple-element.249), channel_id=1, source_target_pairs={{0,2},{1,3},{2,0},{3,1},{4,6},{5,7},{6,4},{7,5},{8,10},{9,11},{10,... | collective-permute-start | bytes 1769480 | tf_op jit(solution)/shard_map/ppermute | solution.py:478
  149.2 13.2 %collective-permute-start.18 = (f32[4,288,128]{2,1,0:T(8,128)S(1)}, f32[4,288,128]{2,1,0:T(8,128)}, u32[]{:S(2)}, u32[]{:S(2)}) collective-permute-start(f32[4,288,128]{2,1,0:T(8,128)S(1)} %get-tuple-element.250), channel_id=1, source_target_pairs={{0,16},{1,17},{2,18},{3,19},{4,20},{5,21},{6,22},{7,23},{8,24},{9,... | collective-permute-start | bytes 1769480 | tf_op jit(solution)/shard_map/ppermute | solution.py:478
  149.4 10.2 %collective-permute-start.16 = (f32[544,256]{1,0:T(8,128)}, f32[544,256]{1,0:T(8,128)}, u32[]{:S(2)}, u32[]{:S(2)}) collective-permute-start(f32[544,256]{1,0:T(8,128)} %select_add_fusion.1), channel_id=1, source_target_pairs={{0,1},{1,0},{2,3},{3,2},{4,5},{5,4},{6,7},{7,6},{8,9},{9,8},{10,11... | collective-permute-start | bytes 1671176 | tf_op jit(solution)/shard_map/ppermute | solution.py:478
  165.0 20.3 %collective-permute-start.19 = (f32[576,128]{1,0:T(8,128)S(1)}, f32[576,128]{1,0:T(8,128)S(1)}, u32[]{:S(2)}, u32[]{:S(2)}) collective-permute-start(f32[576,128]{1,0:T(8,128)S(1)} %get-tuple-element.261), channel_id=1, source_target_pairs={{0,4},{1,5},{2,6},{3,7},{4,0},{5,1},{6,2},{7,3},{8,12},{9,13},{10,... | collective-permute-start | bytes 884744 | tf_op jit(solution)/shard_map/ppermute | solution.py:478
  166.3 19.0 %collective-permute-start.20 = (f32[576,128]{1,0:T(8,128)S(1)}, f32[576,128]{1,0:T(8,128)S(1)}, u32[]{:S(2)}, u32[]{:S(2)}) collective-permute-start(f32[576,128]{1,0:T(8,128)S(1)} %get-tuple-element.262), channel_id=1, source_target_pairs={{0,8},{1,9},{2,10},{3,11},{4,12},{5,13},{6,14},{7,15},{8,0},{9,1},... | collective-permute-start | bytes 884744 | tf_op jit(solution)/shard_map/ppermute | solution.py:478
  167.6 23.2 %collective-permute-start.21 = (f32[576,128]{1,0:T(8,128)S(1)}, f32[576,128]{1,0:T(8,128)S(1)}, u32[]{:S(2)}, u32[]{:S(2)}) collective-permute-start(f32[576,128]{1,0:T(8,128)S(1)} %get-tuple-element.263), channel_id=1, source_target_pairs={{0,12},{1,13},{2,14},{3,15},{4,8},{5,9},{6,10},{7,11},{8,4},{9,5},... | collective-permute-start | bytes 884744 | tf_op jit(solution)/shard_map/ppermute | solution.py:478
  191.7 7.0 %collective-permute-start.22 = (f32[16,192,128]{2,1,0:T(8,128)S(1)}, f32[16,192,128]{2,1,0:T(8,128)S(1)}, u32[]{:S(2)}, u32[]{:S(2)}) collective-permute-start(f32[16,192,128]{2,1,0:T(8,128)S(1)} %qkv_grads.2), channel_id=1, source_target_pairs={{0,1},{1,0},{2,3},{3,2},{4,5},{5,4},{6,7},{7,6},{8,9},{9,8},{10,11... | collective-permute-start | bytes 4718600 | tf_op jit(solution)/shard_map/ppermute | solution.py:478
  198.8 13.1 %collective-permute-start.24 = (f32[2,4,96,128]{3,2,1,0:T(8,128)S(1)}, f32[2,4,96,128]{3,2,1,0:T(8,128)S(1)}, u32[]{:S(2)}, u32[]{:S(2)}) collective-permute-start(f32[2,4,96,128]{3,2,1,0:T(8,128)S(1)} %add_bitcast_fusion.3), channel_id=1, source_target_pairs={{0,16},{1,17},{2,18},{3,19},{4,20},{5,21},{6,22},{7,23},{8,24},{9,... | collective-permute-start | bytes 1179656 | tf_op jit(solution)/shard_map/ppermute | solution.py:478
  199.1 12.8 %collective-permute-start.25 = (f32[2,4,96,128]{3,2,1,0:T(8,128)S(1)}, f32[2,4,96,128]{3,2,1,0:T(8,128)S(1)}, u32[]{:S(2)}, u32[]{:S(2)}) collective-permute-start(f32[2,4,96,128]{3,2,1,0:T(8,128)S(1)} %add_bitcast_fusion.2), channel_id=1, source_target_pairs={{0,2},{1,3},{2,0},{3,1},{4,6},{5,7},{6,4},{7,5},{8,10},{9,11},{10,... | collective-permute-start | bytes 1179656 | tf_op jit(solution)/shard_map/ppermute | solution.py:478
  200.1 11.9 %collective-permute-start.26 = (f32[52,128]{1,0:T(8,128)S(1)}, f32[52,128]{1,0:T(8,128)S(1)}, u32[]{:S(2)}, u32[]{:S(2)}) collective-permute-start(f32[52,128]{1,0:T(8,128)S(1)} %fusion.27), channel_id=1, source_target_pairs={{0,2},{1,3},{2,0},{3,1},{4,6},{5,7},{6,4},{7,5},{8,10},{9,11},{10,... | collective-permute-start | bytes 79880 | tf_op jit(solution)/shard_map/ppermute | solution.py:478
  217.9 21.2 %collective-permute-start.30 = (f32[192,128]{1,0:T(8,128)S(1)}, f32[192,128]{1,0:T(8,128)S(1)}, u32[]{:S(2)}, u32[]{:S(2)}) collective-permute-start(f32[192,128]{1,0:T(8,128)S(1)} %get-tuple-element.302), channel_id=1, source_target_pairs={{0,4},{1,5},{2,6},{3,7},{4,0},{5,1},{6,2},{7,3},{8,12},{9,13},{10,... | collective-permute-start | bytes 294920 | tf_op jit(solution)/shard_map/ppermute | solution.py:478
  218.0 21.1 %collective-permute-start.31 = (f32[192,128]{1,0:T(8,128)S(1)}, f32[192,128]{1,0:T(8,128)S(1)}, u32[]{:S(2)}, u32[]{:S(2)}) collective-permute-start(f32[192,128]{1,0:T(8,128)S(1)} %get-tuple-element.303), channel_id=1, source_target_pairs={{0,8},{1,9},{2,10},{3,11},{4,12},{5,13},{6,14},{7,15},{8,0},{9,1},... | collective-permute-start | bytes 294920 | tf_op jit(solution)/shard_map/ppermute | solution.py:478
  220.6 18.5 %collective-permute-start.32 = (f32[192,128]{1,0:T(8,128)S(1)}, f32[192,128]{1,0:T(8,128)S(1)}, u32[]{:S(2)}, u32[]{:S(2)}) collective-permute-start(f32[192,128]{1,0:T(8,128)S(1)} %get-tuple-element.304), channel_id=1, source_target_pairs={{0,12},{1,13},{2,14},{3,15},{4,8},{5,9},{6,10},{7,11},{8,4},{9,5},... | collective-permute-start | bytes 294920 | tf_op jit(solution)/shard_map/ppermute | solution.py:478
  220.6 18.5 %collective-permute-start.33 = (f32[52,128]{1,0:T(8,128)S(1)}, f32[52,128]{1,0:T(8,128)S(1)}, u32[]{:S(2)}, u32[]{:S(2)}) collective-permute-start(f32[52,128]{1,0:T(8,128)S(1)} %add.517), channel_id=1, source_target_pairs={{0,8},{1,9},{2,10},{3,11},{4,12},{5,13},{6,14},{7,15},{8,0},{9,1},... | collective-permute-start | bytes 79880 | tf_op jit(solution)/shard_map/ppermute | solution.py:478
  240.4 7.1 %collective-permute-start.35 = (f32[192,128]{1,0:T(8,128)S(1)}, f32[192,128]{1,0:T(8,128)S(1)}, u32[]{:S(2)}, u32[]{:S(2)}) collective-permute-start(f32[192,128]{1,0:T(8,128)S(1)} %fusion.19), channel_id=1, source_target_pairs={{0,8},{1,9},{2,10},{3,11},{4,12},{5,13},{6,14},{7,15},{8,0},{9,1},... | collective-permute-start | bytes 294920 | tf_op jit(solution)/shard_map/ppermute | solution.py:478
  244.4 7.0 %collective-permute-start.36 = (f32[192,128]{1,0:T(8,128)S(1)}, f32[192,128]{1,0:T(8,128)S(1)}, u32[]{:S(2)}, u32[]{:S(2)}) collective-permute-start(f32[192,128]{1,0:T(8,128)S(1)} %fusion.19), channel_id=1, source_target_pairs={{0,12},{1,13},{2,14},{3,15},{4,8},{5,9},{6,10},{7,11},{8,4},{9,5},... | collective-permute-start | bytes 294920 | tf_op jit(solution)/shard_map/ppermute | solution.py:478
  251.5 9.2 %collective-permute-start.38 = (f32[4,96,128]{2,1,0:T(8,128)S(1)}, f32[4,96,128]{2,1,0:T(8,128)S(1)}, u32[]{:S(2)}, u32[]{:S(2)}) collective-permute-start(f32[4,96,128]{2,1,0:T(8,128)S(1)} %get-tuple-element.318), channel_id=1, source_target_pairs={{0,2},{1,3},{2,0},{3,1},{4,6},{5,7},{6,4},{7,5},{8,10},{9,11},{10,... | collective-permute-start | bytes 589832 | tf_op jit(solution)/shard_map/ppermute | solution.py:478
  251.6 9.1 %collective-permute-start.39 = (f32[4,96,128]{2,1,0:T(8,128)S(1)}, f32[4,96,128]{2,1,0:T(8,128)S(1)}, u32[]{:S(2)}, u32[]{:S(2)}) collective-permute-start(f32[4,96,128]{2,1,0:T(8,128)S(1)} %get-tuple-element.319), channel_id=1, source_target_pairs={{0,16},{1,17},{2,18},{3,19},{4,20},{5,21},{6,22},{7,23},{8,24},{9,... | collective-permute-start | bytes 589832 | tf_op jit(solution)/shard_map/ppermute | solution.py:478
  260.8 17.4 %collective-permute-start.40 = (f32[2,4,96,128]{3,2,1,0:T(8,128)S(1)}, f32[2,4,96,128]{3,2,1,0:T(8,128)S(1)}, u32[]{:S(2)}, u32[]{:S(2)}) collective-permute-start(f32[2,4,96,128]{3,2,1,0:T(8,128)S(1)} %pad_maximum_fusion.4.refs_0_), channel_id=1, source_target_pairs={{0,16},{1,17},{2,18},{3,19},{4,20},{5,21},{6,22},{7,23},{8,24},{9,... | collective-permute-start | bytes 1179656 | tf_op jit(solution)/shard_map/ppermute | solution.py:478
  261.1 17.1 %collective-permute-start.41 = (f32[2,4,96,128]{3,2,1,0:T(8,128)S(1)}, f32[2,4,96,128]{3,2,1,0:T(8,128)S(1)}, u32[]{:S(2)}, u32[]{:S(2)}) collective-permute-start(f32[2,4,96,128]{3,2,1,0:T(8,128)S(1)} %pad_maximum_fusion.5.refs_2_), channel_id=1, source_target_pairs={{0,2},{1,3},{2,0},{3,1},{4,6},{5,7},{6,4},{7,5},{8,10},{9,11},{10,... | collective-permute-start | bytes 1179656 | tf_op jit(solution)/shard_map/ppermute | solution.py:478
  278.2 7.6 %collective-permute-start.42 = (f32[2,4,96,128]{3,2,1,0:T(8,128)S(1)}, f32[2,4,96,128]{3,2,1,0:T(8,128)S(1)}, u32[]{:S(2)}, u32[]{:S(2)}) collective-permute-start(f32[2,4,96,128]{3,2,1,0:T(8,128)S(1)} %pad_maximum_fusion.4.refs_0_), channel_id=1, source_target_pairs={{0,1},{1,0},{2,3},{3,2},{4,5},{5,4},{6,7},{7,6},{8,9},{9,8},{10,11... | collective-permute-start | bytes 1179656 | tf_op jit(solution)/shard_map/ppermute | solution.py:478
  (37 other events, 186.3 us)
Sparse Core Ops, SparseCore 0:
  191.7 101.8 all-gather.2
